TPU v7x, 32 devices: a whole 2x2x4 slice. The times are simulated.
32 devices in a mesh: groups: 2 (over y), tile: 4 (over z), sect: 2 (over x), half: 2 (over core).
Axes of the slice: x: 2, y: 2, z: 4, core: 2. Of those that a mesh axis runs over, the one named last changes fastest.
Arguments:
- patches: bfloat16 [4, 4, 32, 256, 256], P(('groups', 'sect'), 'tile', 'half'), parts along dimension 0, may hold values from -6 to 6
- pair_lists: int32 [3, 4, 4, 24], P(None, ('groups', 'sect'), 'tile', 'half'), parts along dimension 1, may hold values from 0 to 15, as said below
- move_plan: int32 [2, 4, 4, 24], P(None, ('groups', 'sect'), 'tile', 'half'), parts along dimension 1, may hold values from -1 to 5, as said below
Outputs:
- work_surfaces: float32 [4, 4, 12, 256, 256], P(('groups', 'sect'), 'tile', 'half'), parts along dimension 0
- peak_values: float32 [4, 4, 24], P(('groups', 'sect'), 'tile', 'half'), parts along dimension 0
There are 2 independent parts, one for each index of `groups`. A program takes and returns all parts, laid end to end along the dimension named above; each array names one. Nothing has to cross between parts.
Inputs may be any that keep to these rules, and one draw needn't show every extreme that they name: `pair_lists`: kind 0 names the tile row below (r + 1), kind 1 the next section (s + 1). Every slot of the last tile row has kind 1 and every slot of the last section kind 0; the device of the last tile row in the last section has no live slot. Entries a and b are below 16. `move_plan`: entry 0 is the target tile row of a slot (-1 for unused), entry 1 its work slot there (-1 for unused). A device has at most 12 live slots and at most 3 live slots with the same target; within one section and column half no two live slots share a target and a work slot, work slots are below 6, and live slots are all assigned. Some device has 12 live slots and some target receives 6.
All inputs are finite; a program needn't handle non-finite values.
Results may differ from a plain program's by a relative error of at most 0.0003.
Values may be sent and summed in bfloat16 or wider, within the bound.
No kernel may reach another device: no remote copies, remote signals or barrier semaphores. Data moves between devices by JAX's collectives and lax.ppermute only.
A program may use at most 64 MiB of HBM per device.

v0:
```python
import math

import jax
import jax.numpy as jnp
from jax import lax
from jax.sharding import PartitionSpec as P

FLOOR = 0.05


def passed_along(value, axis, steps):
    count = lax.axis_size(axis)
    leading, last = (max(0, -steps), min(count, count - steps))
    return lax.ppermute(value, axis, [(source, source + steps) for source in range(leading, last)])


def split_table(table):
    upper_part = table.astype(jnp.bfloat16)
    widened = lax.optimization_barrier(upper_part).astype(jnp.float32)
    lower_part = (table - widened).astype(jnp.bfloat16)
    return (upper_part, lower_part)


def transform_tables(length):
    indices = jnp.arange(length, dtype=jnp.int32)
    phase_index = indices[:, None] * indices[None, :] % length
    angles = phase_index.astype(jnp.float32) * (2.0 * math.pi / length)
    cosine_table = jnp.cos(angles)
    sine_table = jnp.sin(angles)
    return (cosine_table, sine_table, split_table(cosine_table), split_table(sine_table))


def matmul(left, right):
    return jnp.dot(left, right, precision=lax.Precision.HIGH, preferred_element_type=jnp.float32)


def narrow_product(picture, pieces):
    return jnp.dot(picture, pieces[0], preferred_element_type=jnp.float32) + jnp.dot(
        picture, pieces[1], preferred_element_type=jnp.float32
    )


def spectrum(picture, tables):
    cosine_table, sine_table, cosine_pieces, sine_pieces = tables
    right_cos = narrow_product(picture, cosine_pieces)
    right_sin = narrow_product(picture, sine_pieces)
    real_part = matmul(cosine_table, right_cos) - matmul(sine_table, right_sin)
    imag_part = -(matmul(sine_table, right_cos) + matmul(cosine_table, right_sin))
    return (real_part, imag_part)


def correlate(couple, tables):
    cosine_table, sine_table = (tables[0], tables[1])
    length = couple.shape[-1]
    first_re, first_im = spectrum(couple[0], tables)
    second_re, second_im = spectrum(couple[1], tables)
    cross_re = first_re * second_re + first_im * second_im
    cross_im = first_im * second_re - first_re * second_im
    divisor = jnp.maximum(
        jnp.sqrt(cross_re * cross_re + cross_im * cross_im), FLOOR * length * length
    )
    norm_re = cross_re / divisor
    norm_im = cross_im / divisor
    upper = matmul(norm_re, cosine_table) - matmul(norm_im, sine_table)
    lower = matmul(norm_re, sine_table) + matmul(norm_im, cosine_table)
    return (matmul(cosine_table, upper) - matmul(sine_table, lower)) / length


def settle(arrived_place, lane_ids, work_ids):
    matches = arrived_place[None, :] == work_ids[:, None]
    present = jnp.any(matches, axis=1)
    picked = jnp.sum(jnp.where(matches, lane_ids[None, :], 0), axis=1)
    return (present, picked)


def body(patches, pair_lists, move_plan):
    own_patches = patches[0, 0]
    from_below = passed_along(own_patches, "tile", -1)
    from_next = passed_along(own_patches, "sect", -1)
    pair_kinds = pair_lists[0, 0, 0]
    first_index = pair_lists[1, 0, 0]
    second_index = pair_lists[2, 0, 0]
    targets = move_plan[0, 0, 0]
    places = move_plan[1, 0, 0]
    slot_count = pair_kinds.shape[0]
    patch_count = own_patches.shape[0]
    work_count = slot_count // 2
    tile_count = lax.axis_size("tile")
    per_peer = (slot_count + tile_count - 1) // tile_count
    lane_total = tile_count * per_peer
    tables = transform_tables(own_patches.shape[-1])
    slot_alive = targets >= 0
    firsts = jnp.take(own_patches, first_index, axis=0)
    partners = jnp.concatenate([from_below, from_next], axis=0)
    seconds = jnp.take(partners, pair_kinds * patch_count + second_index, axis=0)
    pair_stack = jnp.stack([firsts, seconds], axis=1)
    slot_order = jnp.arange(slot_count, dtype=jnp.int32)
    earlier = (
        (targets[:, None] == targets[None, :])
        & (slot_order[None, :] < slot_order[:, None])
        & slot_alive[None, :]
    )
    position = jnp.sum(earlier.astype(jnp.int32), axis=1)
    lane_of_slot = jnp.where(slot_alive, targets * per_peer + position, -1)
    lane_ids = jnp.arange(lane_total, dtype=jnp.int32)
    lane_hits = lane_of_slot[None, :] == lane_ids[:, None]
    lane_used = jnp.any(lane_hits, axis=1)
    lane_source = jnp.sum(jnp.where(lane_hits, slot_order[None, :], 0), axis=1)
    lane_place = jnp.where(lane_used, jnp.take(places, lane_source), -1)
    work_ids = jnp.arange(work_count, dtype=jnp.int32)

    def run_couple(couple):
        return correlate(couple, tables)

    outgoing = jnp.take(pair_stack, lane_source, axis=0)
    outgoing = jnp.where(lane_used[:, None, None, None], outgoing, jnp.zeros_like(outgoing))
    arrived, arrived_place = (
        lax.all_to_all(outgoing, "tile", split_axis=0, concat_axis=0, tiled=True),
        lax.all_to_all(lane_place, "tile", split_axis=0, concat_axis=0, tiled=True),
    )
    present, picked = settle(arrived_place, lane_ids, work_ids)
    chosen = jnp.take(arrived, picked, axis=0)
    work_pairs = jnp.where(present[:, None, None, None], chosen, jnp.zeros_like(chosen))
    surfaces = lax.map(run_couple, work_pairs)
    work_peaks = jnp.max(surfaces, axis=(1, 2))
    work_peaks = jnp.where(present, work_peaks, jnp.zeros_like(work_peaks))
    returned = jnp.take(work_peaks, jnp.maximum(arrived_place, 0))
    returned = jnp.where(arrived_place >= 0, returned, jnp.zeros_like(returned))
    homecoming = lax.all_to_all(returned, "tile", split_axis=0, concat_axis=0, tiled=True)
    slot_peaks = jnp.take(homecoming, jnp.maximum(lane_of_slot, 0))
    peak_values = jnp.where(slot_alive, slot_peaks, jnp.zeros_like(slot_peaks))
    return (surfaces[None, None], peak_values[None, None])


def solution(mesh):
    in_specs = (
        P(("groups", "sect"), "tile", "half", None, None),
        P(None, ("groups", "sect"), "tile", "half"),
        P(None, ("groups", "sect"), "tile", "half"),
    )
    out_specs = (
        P(("groups", "sect"), "tile", "half", None, None),
        P(("groups", "sect"), "tile", "half"),
    )
    return jax.shard_map(body, mesh=mesh, in_specs=in_specs, out_specs=out_specs, check_vma=False)
```

profile of v0, /device:TPU:0, one launch (start us, length us, event | category | flops | bytes accessed | tf_op | source)
XLA Modules:
  0.0 304.8 jit_solution(11675553964444325043)
XLA Ops:
  7.2 8.7 %all-to-all-start = ((s32[4,3,1]{1,2,0:T(1,128)}), s32[4,3,1]{1,2,0:T(1,128)S(1)}, u32[]{:S(2)}, u32[]{:S(2)}) async-start(s32[4,3,1]{1,2,0:T(1,128)} %bitcast.4), calls=%async_computation | async-start | bytes 4096 | tf_op jit(solution)/shard_map/all_to_all | solution.py:119
  16.6 2.2 gather_fusion.1
  20.2 31.3 %collective-permute-done = bf16[16,256,256]{2,1,0:T(8,128)(2,1)} collective-permute-done((bf16[16,256,256]{2,1,0:T(8,128)(2,1)}, bf16[16,256,256]{2,1,0:T(8,128)(2,1)}, u32[]{:S(2)}, u32[]{:S(2)}) %collective-permute-start) | collective-permute-done | bytes 2097184 | tf_op jit(solution)/shard_map/ppermute | solution.py:14
  52.1 4.5 %pad_maximum_fusion = bf16[32,256,256]{2,1,0:T(8,128)(2,1)} fusion(bf16[16,256,256]{2,1,0:T(8,128)(2,1)} %collective-permute-done.1, bf16[16,256,256]{2,1,0:T(8,128)(2,1)} %collective-permute-done), kind=kLoop, calls=%fused_computation.136 | loop fusion | flops 2097152 | bytes 8388608 | tf_op jit(solution)/shard_map/concatenate | solution.py:94
  56.6 2.8 gather_fusion.2
  61.2 2.5 gather_fusion.3
  63.7 4.0 %select_select_fusion = bf16[12,2,256,256]{3,2,1,0:T(8,128)(2,1)} fusion(bf16[12,2,256,256]{3,2,1,0:T(8,128)(2,1)} %gather_fusion.3, pred[12]{0:T(512)(128)(4,1)S(1)} %compare_and_fusion.2, pred[12]{0:T(512)(128)(4,1)S(1)} %fusion.139), kind=kLoop, calls=%fused_computation.138 | loop fusion | flops 3145728 | bytes 6291480 | tf_op jit(solution)/shard_map/jit(_where)/select_n | solution.py:116
  67.7 8.0 %all-to-all-start.1 = ((bf16[12,2,256,256]{3,2,1,0:T(8,128)(2,1)}), bf16[12,2,256,256]{3,2,1,0:T(8,128)(2,1)S(1)}, u32[]{:S(2)}, u32[]{:S(2)}) async-start(bf16[12,2,256,256]{3,2,1,0:T(8,128)(2,1)} %select_select_fusion), calls=%async_computation.1 | async-start | bytes 6291456 | tf_op jit(solution)/shard_map/all_to_all | solution.py:118
  76.6 1.6 fusion.138
  78.3 2.0 subtract_convert_fusion
  81.7 63.4 %all-to-all-done.1 = bf16[12,2,256,256]{3,2,1,0:T(8,128)(2,1)S(1)} async-done(((bf16[12,2,256,256]{3,2,1,0:T(8,128)(2,1)}), bf16[12,2,256,256]{3,2,1,0:T(8,128)(2,1)S(1)}, u32[]{:S(2)}, u32[]{:S(2)}) %all-to-all-start.1) | async-done | bytes 3145760 | tf_op jit(solution)/shard_map/all_to_all | solution.py:118
  145.1 1.9 gather_fusion.4
  147.0 1.8 select_select_fusion.1
  148.8 143.3 %while.12 = (s32[]{:T(128)}, f32[6,256,256]{1,2,0:T(8,128)S(1)}, bf16[6,2,256,256]{3,2,1,0:T(8,128)(2,1)S(1)}, bf16[256,256]{1,0:T(8,128)(2,1)S(1)}, bf16[256,25...) while((s32[]{:T(128)}, f32[6,256,256]{1,2,0:T(8,128)S(1)}, ...), condition=%wide.region_6.7_spmd.clone.clone, body=%wide.region_5.6_spmd.clone.clone.sunk | while | flops 1697120256 | bytes 15990933 | solution.py:124
  164.6 1.4 fusion.248
  166.0 1.4 convolution_add_fusion.20
  167.4 1.4 fusion.246
  168.8 1.4 convolution_subtract_fusion.7
  188.4 1.4 fusion.248
  189.9 1.4 convolution_add_fusion.20
  192.7 1.4 convolution_subtract_fusion.7
  212.3 1.4 fusion.248
  216.5 1.4 convolution_subtract_fusion.7
  236.2 1.4 fusion.248
  240.4 1.4 convolution_subtract_fusion.7
  260.1 1.4 fusion.248
  264.3 1.4 convolution_subtract_fusion.7
  283.9 1.4 fusion.248
  288.2 1.4 convolution_subtract_fusion.7
  293.7 3.2 %all-to-all-start.2 = ((f32[4,3,1]{1,2,0:T(1,128)}), f32[4,3,1]{1,2,0:T(1,128)S(1)}, u32[]{:S(2)}, u32[]{:S(2)}) async-start(f32[4,3,1]{1,2,0:T(1,128)} %bitcast.22), calls=%async_computation.2 | async-start | bytes 4096 | tf_op jit(solution)/shard_map/all_to_all | solution.py:129
  297.0 1.6 copy.13
  298.6 3.7 %all-to-all-done.2 = f32[4,3,1]{1,2,0:T(1,128)S(1)} async-done(((f32[4,3,1]{1,2,0:T(1,128)}), f32[4,3,1]{1,2,0:T(1,128)S(1)}, u32[]{:S(2)}, u32[]{:S(2)}) %all-to-all-start.2) | async-done | bytes 80 | tf_op jit(solution)/shard_map/all_to_all | solution.py:129
  (176 shorter events, 138.6 us)
Async XLA Ops:
  0.6 50.9 %collective-permute-start = (bf16[16,256,256]{2,1,0:T(8,128)(2,1)}, bf16[16,256,256]{2,1,0:T(8,128)(2,1)}, u32[]{:S(2)}, u32[]{:S(2)}) collective-permute-start(bf16[16,256,256]{2,1,0:T(8,128)(2,1)} %bitcast.200), channel_id=1, source_target_pairs={{4,0},{8,4},{12,8},{5,1},{9,5},{13,9},{6,2},{10,6},{14,10},{7,3},{... | collective-permute-start | bytes 6291464 | tf_op jit(solution)/shard_map/ppermute | solution.py:14
  1.9 50.2 %collective-permute-start.1 = (bf16[16,256,256]{2,1,0:T(8,128)(2,1)}, bf16[16,256,256]{2,1,0:T(8,128)(2,1)}, u32[]{:S(2)}, u32[]{:S(2)}) collective-permute-start(bf16[16,256,256]{2,1,0:T(8,128)(2,1)} %bitcast.201), channel_id=1, source_target_pairs={{2,0},{3,1},{6,4},{7,5},{10,8},{11,9},{14,12},{15,13},{18,16},{19,... | collective-permute-start | bytes 6291464 | tf_op jit(solution)/shard_map/ppermute | solution.py:14
  7.2 60.5 %all-to-all-start = ((s32[4,3,1]{1,2,0:T(1,128)}), s32[4,3,1]{1,2,0:T(1,128)S(1)}, u32[]{:S(2)}, u32[]{:S(2)}) async-start(s32[4,3,1]{1,2,0:T(1,128)} %bitcast.4), calls=%async_computation | async-start | bytes 4096 | tf_op jit(solution)/shard_map/all_to_all | solution.py:119
  16.6 2.3 copy-start.3
  59.5 1.4 copy-start.1
  67.7 10.6 %copy-start.2 = (s32[2,1,1,12]{3,2,1,0:T(1,128)S(1)}, s32[2,1,1,12]{3,2,1,0:T(1,128)}, u32[]{:S(2)}) copy-start(s32[2,1,1,12]{3,2,1,0:T(1,128)} %param.7) | copy-start | bytes 292
  67.7 77.4 %all-to-all-start.1 = ((bf16[12,2,256,256]{3,2,1,0:T(8,128)(2,1)}), bf16[12,2,256,256]{3,2,1,0:T(8,128)(2,1)S(1)}, u32[]{:S(2)}, u32[]{:S(2)}) async-start(bf16[12,2,256,256]{3,2,1,0:T(8,128)(2,1)} %select_select_fusion), calls=%async_computation.1 | async-start | bytes 6291456 | tf_op jit(solution)/shard_map/all_to_all | solution.py:118
  147.0 1.9 copy-start
  293.7 8.6 %all-to-all-start.2 = ((f32[4,3,1]{1,2,0:T(1,128)}), f32[4,3,1]{1,2,0:T(1,128)S(1)}, u32[]{:S(2)}, u32[]{:S(2)}) async-start(f32[4,3,1]{1,2,0:T(1,128)} %bitcast.22), calls=%async_computation.2 | async-start | bytes 4096 | tf_op jit(solution)/shard_map/all_to_all | solution.py:129
where the time goes:
time: 305 us
  matrix products  142 us (47%)
  waiting for transfers between devices  99 us (32%)
  other arithmetic  22.6 us (7%)
  starting transfers between devices  22.5 us (7%)
  local copies, waits for them, and re-layouts  16.6 us (5%)
    dot_general x84, matrix products, matmul(): jnp.dot(left, right, precision=lax.Precision.HIGH, preferred_element_type...  111 us
    all_to_all x1, waiting for transfers between devices, body(): lax.all_to_all(outgoing, 'tile', split_axis=0, concat_axis=0, tiled=True)  63.4 us
    ppermute x2, waiting for transfers between devices, passed_along(): lax.ppermute(value, axis, [(source, source + steps) for source in range(l...  31.9 us
    dot_general x24, matrix products, narrow_product(): jnp.dot(picture, pieces[0], preferred_element_type=jnp.float32)  27 us
    all_to_all x1, starting transfers between devices, body(): lax.all_to_all(lane_place, 'tile', split_axis=0, concat_axis=0, tiled=True)  8.72 us
    all_to_all x1, starting transfers between devices, body(): lax.all_to_all(outgoing, 'tile', split_axis=0, concat_axis=0, tiled=True)  7.95 us
  transfers between devices with their start and end apart: 5, of which 4 were waited for; matrix products, arithmetic and copies ran while one was open for 10% of the time, Pallas kernels for 0%

commit v1 on v0

v1 whole, which is shorter than its diff:
```python
import functools

import jax
import jax.numpy as jnp
import ml_dtypes
import numpy as np
from jax import lax
from jax.experimental import pallas as pl
from jax.experimental.pallas import tpu as pltpu
from jax.sharding import PartitionSpec as P

FLOOR = 0.05
TOP = 32767.0
TINY = 1e-28
LIMIT = 48 * 1024 * 1024

SMEM = pl.BlockSpec(memory_space=pltpu.SMEM)
VMEM = pl.BlockSpec(memory_space=pltpu.VMEM)
ANY = pl.BlockSpec(memory_space=pl.ANY)
SDS = jax.ShapeDtypeStruct


def shifted(value, axis, steps):
    count = lax.axis_size(axis)
    pairs = [(i, i + steps) for i in range(count) if 0 <= i + steps < count]
    return lax.ppermute(value, axis, pairs)


def rotated(value, axis, steps):
    count = lax.axis_size(axis)
    return lax.ppermute(value, axis, [(i, (i + steps) % count) for i in range(count)])


def packed_table(length):
    half = length // 2
    n = np.arange(length)[:, None]
    v = np.arange(half + 1)[None, :]
    angle = 2.0 * np.pi * ((n * v) % length) / length
    table = np.concatenate([np.cos(angle), np.sin(angle[:, 1:half])], axis=1)
    high = table.astype(np.float32).astype(ml_dtypes.bfloat16)
    low = (table - high.astype(np.float64)).astype(np.float32).astype(ml_dtypes.bfloat16)
    return high, low


def dot(left, right):
    return jnp.dot(left, right, preferred_element_type=jnp.float32)


def pieces(value):
    high = value.astype(jnp.bfloat16)
    low = (value - high.astype(jnp.float32)).astype(jnp.bfloat16)
    return high, low


def packed_transform(picture, th, tl, sh, sl):
    high, low = pieces(dot(picture, th[...]) + dot(picture, tl[...]))
    return dot(sh[...], high) + dot(sh[...], low) + dot(sl[...], high)


def two_lines(packed, half, row, col, edge):
    cp, cq = packed[:half, :half], packed[:half, half:]
    sp, sq = packed[half:, :half], packed[half:, half:]
    sq_in = jnp.where(edge, 0.0, sq)
    re1 = cp - sq_in
    im1 = -(jnp.where(row, 0.0, sp) + jnp.where(col, 0.0, cq))
    re2 = jnp.where(row, sp, jnp.where(col, cq, cp + sq))
    im2 = jnp.where(edge, -sq, sp - cq)
    return re1, im1, re2, im2


def normalized_packed(one, two, length):
    half = length // 2
    floor = FLOOR * length * length
    rows = lax.broadcasted_iota(jnp.int32, (half, half), 0)
    cols = lax.broadcasted_iota(jnp.int32, (half, half), 1)
    row, col = rows == 0, cols == 0
    edge, corner = row | col, row & col
    a_re1, a_im1, a_re2, a_im2 = two_lines(one, half, row, col, edge)
    b_re1, b_im1, b_re2, b_im2 = two_lines(two, half, row, col, edge)

    def scaled(a_re, a_im, b_re, b_im):
        re = a_re * b_re + a_im * b_im
        im = a_im * b_re - a_re * b_im
        factor = jnp.minimum(lax.rsqrt(re * re + im * im), 1.0 / floor)
        return re * factor, im * factor

    n_re1, n_im1 = scaled(a_re1, a_im1, b_re1, b_im1)
    n_re2, n_im2 = scaled(a_re2, a_im2, b_re2, b_im2)

    def real_corner(value, start_row, start_col):
        a = one[start_row : start_row + half, start_col : start_col + half]
        b = two[start_row : start_row + half, start_col : start_col + half]
        product = a * b
        alone = 0.5 * product / jnp.maximum(jnp.abs(product), floor)
        return jnp.where(corner, alone, value)

    cp = jnp.where(edge, n_re1, n_re1 + n_re2)
    cq = jnp.where(row, -n_im1, jnp.where(col, n_re2, -(n_im1 + n_im2)))
    sp = jnp.where(row, n_re2, jnp.where(col, -n_im1, n_im2 - n_im1))
    sq = jnp.where(edge, -n_im2, n_re2 - n_re1)
    cp = real_corner(cp, 0, 0)
    cq = real_corner(cq, 0, half)
    sp = real_corner(sp, half, 0)
    sq = real_corner(sq, half, half)
    packed = jnp.concatenate(
        [jnp.concatenate([cp, cq], axis=1), jnp.concatenate([sp, sq], axis=1)], axis=0
    )
    return packed * (2.0 / length)


def inverse_packed(packed, th, tl, sh, sl):
    high, low = pieces(packed)
    high, low = pieces(dot(th[...], high) + dot(th[...], low) + dot(tl[...], high))
    return dot(high, sh[...]) + dot(high, sl[...]) + dot(low, sh[...])


def lanes_kernel(tiles, per, info, table):
    slots = info.shape[1]
    me = lax.axis_index("tile")
    for d in range(tiles):
        for j in range(per):
            table[0, d * per + j] = -1
            for field in range(1, 4):
                table[field, d * per + j] = 0
            table[4, d * per + j] = -1
    for k in range(slots):
        target = info[3, k]
        rank = jnp.int32(0)
        for q in range(k):
            rank += (info[3, q] == target).astype(jnp.int32)
        distance = lax.rem(target - me + tiles, tiles)
        lane = distance * per + rank

        @pl.when(target >= 0)
        def _():
            table[0, lane] = info[0, k]
            table[1, lane] = info[1, k]
            table[2, lane] = info[2, k]
            table[3, lane] = info[4, k]
            table[4, lane] = k


def gather_kernel(first_lane, per, below, later, patches, to_below, to_later, sems):
    copies = []
    for j in range(per):
        lane = first_lane + j
        copies.append(
            pltpu.make_async_copy(patches.at[below[2, lane]], to_below.at[j], sems.at[0, j])
        )
        copies.append(
            pltpu.make_async_copy(patches.at[later[2, lane]], to_later.at[j], sems.at[1, j])
        )
    for copy in copies:
        copy.start()
    for copy in copies:
        copy.wait()


def pair_kernel(first_lane, table, own, below, later, th, tl, sh, sl, codes, tags):
    j = pl.program_id(0)
    lane = first_lane + j
    kind = table[0, lane]
    length = own.shape[-1]
    tags[j, 0] = 0.0
    tags[j, 1] = -1.0
    tags[j, 2] = 0.0

    @pl.when(kind >= 0)
    def _():
        second = jnp.where(kind == 0, below[0], later[0])
        one = packed_transform(own[0], th, tl, sh, sl)
        two = packed_transform(second, th, tl, sh, sl)
        surface = inverse_packed(normalized_packed(one, two, length), th, tl, sh, sl)
        peak = jnp.max(surface)
        size = jnp.maximum(jnp.maximum(peak, -jnp.min(surface)), TINY)
        grown = jnp.abs(surface) * (TOP * TOP / size)
        root = grown * lax.rsqrt(jnp.maximum(grown, TINY))
        whole = (root + 0.5).astype(jnp.int32)
        codes[0] = jnp.where(surface < 0, -whole, whole).astype(jnp.int16)
        tags[j, 0] = size
        tags[j, 1] = table[3, lane].astype(jnp.float32)
        tags[j, 2] = peak


def settle_kernel(shifts, per, table, *refs):
    count = len(shifts)
    home_tags = refs[:count]
    tags = refs[count : 2 * count]
    codes = refs[2 * count : 3 * count]
    surfaces, peaks = refs[3 * count :]
    surfaces[...] = jnp.zeros_like(surfaces)
    for k in range(peaks.shape[0]):
        peaks[k] = 0.0
    for i, d in enumerate(shifts):
        for j in range(per):
            slot = table[4, d * per + j]

            @pl.when(slot >= 0)
            def _():
                peaks[slot] = home_tags[i][j, 2]

            place = tags[i][j, 1].astype(jnp.int32)

            @pl.when(place >= 0)
            def _():
                value = codes[i][j].astype(jnp.int32).astype(jnp.float32)
                surfaces[place] = value * jnp.abs(value) * (tags[i][j, 0] / (TOP * TOP))


def params():
    return pltpu.CompilerParams(vmem_limit_bytes=LIMIT)


def body(patches, pair_lists, move_plan):
    own = patches[0, 0]
    count, length, _ = own.shape
    info = jnp.concatenate([pair_lists[:, 0, 0], move_plan[:, 0, 0]], axis=0)
    slots = info.shape[1]
    tiles = lax.axis_size("tile")
    per = (slots + tiles - 1) // tiles
    lanes = tiles * per
    shifts = sorted(range(tiles), key=lambda d: (d == 0, -min(d, tiles - d), d))

    table = pl.pallas_call(
        functools.partial(lanes_kernel, tiles, per),
        out_shape=SDS((5, lanes), jnp.int32),
        in_specs=[SMEM],
        out_specs=SMEM,
        name="lanes",
    )(info)
    table_above = shifted(table, "tile", 1)
    table_before = shifted(table, "sect", 1)

    high, low = packed_table(length)
    tables = [jnp.asarray(t) for t in (high, low, high.T.copy(), low.T.copy())]
    picture = SDS((per, length, length), jnp.bfloat16)

    arrivals = []
    for d in shifts:
        to_below, to_later = pl.pallas_call(
            functools.partial(gather_kernel, d * per, per),
            out_shape=(picture, picture),
            in_specs=[SMEM, SMEM, ANY],
            out_specs=(ANY, ANY),
            scratch_shapes=[pltpu.SemaphoreType.DMA((2, per))],
            name=f"gather_{d}",
        )(table_above, table_before, own)
        arrivals.append((shifted(to_below, "tile", -1), shifted(to_later, "sect", -1)))

    square = (1, length, length)
    whole = pl.BlockSpec((length, length), lambda j, t: (0, 0))
    home_tags, tags, codes = [], [], []
    for d, (below, later) in zip(shifts, arrivals):
        lane_codes, lane_tags = pl.pallas_call(
            functools.partial(pair_kernel, d * per),
            out_shape=(
                SDS((per, length, length), jnp.int16),
                SDS((per, 3), jnp.float32),
            ),
            grid_spec=pltpu.PrefetchScalarGridSpec(
                num_scalar_prefetch=1,
                grid=(per,),
                in_specs=[
                    pl.BlockSpec(square, lambda j, t, d=d: (t[1, d * per + j], 0, 0)),
                    pl.BlockSpec(square, lambda j, t: (j, 0, 0)),
                    pl.BlockSpec(square, lambda j, t: (j, 0, 0)),
                ]
                + [whole] * 4,
                out_specs=(pl.BlockSpec(square, lambda j, t: (j, 0, 0)), SMEM),
            ),
            compiler_params=params(),
            name=f"pairs_{d}",
        )(table, own, below, later, *tables)
        home_tags.append(lane_tags)
        if d == 0:
            tags.append(lane_tags)
            codes.append(lane_codes)
        else:
            tags.append(rotated(lane_tags, "tile", d))
            codes.append(rotated(lane_codes, "tile", d))

    surfaces, peaks = pl.pallas_call(
        functools.partial(settle_kernel, shifts, per),
        out_shape=(
            SDS((slots // 2, length, length), jnp.float32),
            SDS((slots,), jnp.float32),
        ),
        in_specs=[SMEM] + [SMEM] * (2 * tiles) + [VMEM] * tiles,
        out_specs=(VMEM, SMEM),
        compiler_params=params(),
        name="settle",
    )(table, *home_tags, *tags, *codes)
    return surfaces[None, None], peaks[None, None]


def solution(mesh):
    in_specs = (
        P(("groups", "sect"), "tile", "half", None, None),
        P(None, ("groups", "sect"), "tile", "half"),
        P(None, ("groups", "sect"), "tile", "half"),
    )
    out_specs = (
        P(("groups", "sect"), "tile", "half", None, None),
        P(("groups", "sect"), "tile", "half"),
    )
    return jax.shard_map(body, mesh=mesh, in_specs=in_specs, out_specs=out_specs, check_vma=False)
```

time: 305 us -> 185 us (0.61)
  the two profiles are of different devices: /device:TPU:0 before, /device:TPU:14 now
where the time goes in v1:
time: 185 us
  Pallas kernels  138 us (75%)
  starting transfers between devices  25.7 us (14%)
  waiting for transfers between devices  17 us (9%)
    pallas_call x4, Pallas kernels, body(): pl.pallas_call(functools.partial(gather_kernel, d * per, per), out_shape=...  103 us
    pallas_call x4, Pallas kernels, body(): pl.pallas_call(functools.partial(pair_kernel, d * per), out_shape=(SDS((p...  31.2 us
    ppermute x10, starting transfers between devices, shifted(): return lax.ppermute(value, axis, pairs)  23.5 us
    ppermute x6, waiting for transfers between devices, rotated(): lax.ppermute(value, axis, [(i, (i + steps) % count) for i in range(count)])  14.7 us
  transfers between devices with their start and end apart: 16, of which 4 were waited for; matrix products, arithmetic and copies ran while one was open for 0% of the time, Pallas kernels for 59%

profile of v1, /device:TPU:14, one launch (start us, length us, event | category | flops | bytes accessed | tf_op | source)
XLA Modules:
  0.0 184.6 jit_solution(8320912077033546243)
XLA Ops:
  0.6 0.7 copy.11
  1.3 1.3 pad_add_fusion.info
  2.6 1.5 lanes.1.table
  4.1 1.3 collective-permute-start.1
  5.4 3.5 %collective-permute-start = (s32[5,12]{1,0:T(8,128)}, s32[5,12]{1,0:T(8,128)S(1)}, u32[]{:S(2)}, u32[]{:S(2)}) collective-permute-start(s32[5,12]{1,0:T(8,128)} %lanes.1.table), channel_id=1, source_target_pairs={{0,4},{4,8},{8,12},{1,5},{5,9},{9,13},{2,6},{6,10},{10,14},{3,7},{... | collective-permute-start | bytes 728 | tf_op jit(solution)/shard_map/ppermute | solution.py:26
  8.9 0.9 collective-permute-done.1.later
  9.8 1.3 collective-permute-done.below
  11.1 0.6 copy-done.7
  11.7 25.8 %gather_3.1 = (bf16[3,256,256]{2,1,0:T(8,128)(2,1)}, bf16[3,256,256]{2,1,0:T(8,128)(2,1)}) custom-call(s32[5,12]{1,0:T(8,128)} %copy-done.7, s32[5,12]{1,0:T(8,128)} %copy-done.6, bf16[16,256,256]{2,1,0:T(8,128)(2,1)} %bitcast.7), custom_call_target="tpu_custom_call" | custom-call | tf_op jit(solution)/shard_map/gather_3/pallas_call | solution.py:240
  37.5 1.9 %collective-permute-start.6 = (bf16[3,256,256]{2,1,0:T(8,128)(2,1)}, bf16[3,256,256]{2,1,0:T(8,128)(2,1)}, u32[]{:S(2)}, u32[]{:S(2)}) collective-permute-start(bf16[3,256,256]{2,1,0:T(8,128)(2,1)} %get-tuple-element.26), channel_id=1, source_target_pairs={{4,0},{8,4},{12,8},{5,1},{9,5},{13,9},{6,2},{10,6},{14,10},{7,3},{... | collective-permute-start | bytes 1179656 | tf_op jit(solution)/shard_map/ppermute | solution.py:26
  39.4 5.3 %collective-permute-start.7 = (bf16[3,256,256]{2,1,0:T(8,128)(2,1)}, bf16[3,256,256]{2,1,0:T(8,128)(2,1)}, u32[]{:S(2)}, u32[]{:S(2)}) collective-permute-start(bf16[3,256,256]{2,1,0:T(8,128)(2,1)} %get-tuple-element.27), channel_id=1, source_target_pairs={{2,0},{3,1},{6,4},{7,5},{10,8},{11,9},{14,12},{15,13},{18,16},{19,... | collective-permute-start | bytes 1179656 | tf_op jit(solution)/shard_map/ppermute | solution.py:26
  44.7 25.8 %gather_1.1 = (bf16[3,256,256]{2,1,0:T(8,128)(2,1)}, bf16[3,256,256]{2,1,0:T(8,128)(2,1)}) custom-call(s32[5,12]{1,0:T(8,128)} %copy-done.7, s32[5,12]{1,0:T(8,128)} %copy-done.6, bf16[16,256,256]{2,1,0:T(8,128)(2,1)} %bitcast.8), custom_call_target="tpu_custom_call" | custom-call | tf_op jit(solution)/shard_map/gather_1/pallas_call | solution.py:240
  70.5 1.9 %collective-permute-start.4 = (bf16[3,256,256]{2,1,0:T(8,128)(2,1)}, bf16[3,256,256]{2,1,0:T(8,128)(2,1)S(1)}, u32[]{:S(2)}, u32[]{:S(2)}) collective-permute-start(bf16[3,256,256]{2,1,0:T(8,128)(2,1)} %get-tuple-element.23), channel_id=1, source_target_pairs={{4,0},{8,4},{12,8},{5,1},{9,5},{13,9},{6,2},{10,6},{14,10},{7,3},{... | collective-permute-start | bytes 1179656 | tf_op jit(solution)/shard_map/ppermute | solution.py:26
  72.5 2.2 %collective-permute-start.5 = (bf16[3,256,256]{2,1,0:T(8,128)(2,1)}, bf16[3,256,256]{2,1,0:T(8,128)(2,1)}, u32[]{:S(2)}, u32[]{:S(2)}) collective-permute-start(bf16[3,256,256]{2,1,0:T(8,128)(2,1)} %get-tuple-element.24), channel_id=1, source_target_pairs={{2,0},{3,1},{6,4},{7,5},{10,8},{11,9},{14,12},{15,13},{18,16},{19,... | collective-permute-start | bytes 1179656 | tf_op jit(solution)/shard_map/ppermute | solution.py:26
  74.7 25.8 %gather_2.1 = (bf16[3,256,256]{2,1,0:T(8,128)(2,1)}, bf16[3,256,256]{2,1,0:T(8,128)(2,1)}) custom-call(s32[5,12]{1,0:T(8,128)} %copy-done.7, s32[5,12]{1,0:T(8,128)} %copy-done.6, bf16[16,256,256]{2,1,0:T(8,128)(2,1)} %bitcast.9), custom_call_target="tpu_custom_call" | custom-call | tf_op jit(solution)/shard_map/gather_2/pallas_call | solution.py:240
  100.5 1.9 %collective-permute-start.2 = (bf16[3,256,256]{2,1,0:T(8,128)(2,1)}, bf16[3,256,256]{2,1,0:T(8,128)(2,1)S(1)}, u32[]{:S(2)}, u32[]{:S(2)}) collective-permute-start(bf16[3,256,256]{2,1,0:T(8,128)(2,1)} %get-tuple-element.20), channel_id=1, source_target_pairs={{4,0},{8,4},{12,8},{5,1},{9,5},{13,9},{6,2},{10,6},{14,10},{7,3},{... | collective-permute-start | bytes 1179656 | tf_op jit(solution)/shard_map/ppermute | solution.py:26
  102.4 2.0 %collective-permute-start.3 = (bf16[3,256,256]{2,1,0:T(8,128)(2,1)}, bf16[3,256,256]{2,1,0:T(8,128)(2,1)}, u32[]{:S(2)}, u32[]{:S(2)}) collective-permute-start(bf16[3,256,256]{2,1,0:T(8,128)(2,1)} %get-tuple-element.21), channel_id=1, source_target_pairs={{2,0},{3,1},{6,4},{7,5},{10,8},{11,9},{14,12},{15,13},{18,16},{19,... | collective-permute-start | bytes 1179656 | tf_op jit(solution)/shard_map/ppermute | solution.py:26
  104.5 25.8 %gather_0.1 = (bf16[3,256,256]{2,1,0:T(8,128)(2,1)}, bf16[3,256,256]{2,1,0:T(8,128)(2,1)}) custom-call(s32[5,12]{1,0:T(8,128)} %copy-done.7, s32[5,12]{1,0:T(8,128)} %copy-done.6, bf16[16,256,256]{2,1,0:T(8,128)(2,1)} %bitcast.10), custom_call_target="tpu_custom_call" | custom-call | tf_op jit(solution)/shard_map/gather_0/pallas_call | solution.py:240
  130.3 2.1 %collective-permute-start.8 = (bf16[3,256,256]{2,1,0:T(8,128)(2,1)}, bf16[3,256,256]{2,1,0:T(8,128)(2,1)S(1)}, u32[]{:S(2)}, u32[]{:S(2)}) collective-permute-start(bf16[3,256,256]{2,1,0:T(8,128)(2,1)} %get-tuple-element.29), channel_id=1, source_target_pairs={{4,0},{8,4},{12,8},{5,1},{9,5},{13,9},{6,2},{10,6},{14,10},{7,3},{... | collective-permute-start | bytes 1179656 | tf_op jit(solution)/shard_map/ppermute | solution.py:26
  132.4 8.1 %pairs_3.1 = (s16[3,256,256]{2,1,0:T(8,128)(2,1)S(1)}, f32[3,3]{1,0:T(4,128)S(1)}) custom-call(s32[5,12]{1,0:T(8,128)S(1)} %copy-done.5, bf16[16,256,256]{2,1,0:T(8,128)(2,1)S(1)} %bitcast.11, bf16[3,256,256]{2,1,0:T(8,128)(2,1)} %collective-permute-done.6.below, bf16[3,256,256]{2,1,0:T(8,128)(2,1)} %collective-permute-done.7.later, ...), custom_call_target="tpu_custom_call" | custom-call | tf_op jit(solution)/shard_map/pairs_3/pallas_call | solution.py:254
  140.5 1.3 collective-permute-start.9
  141.8 0.1 collective-permute-start.15
  141.9 8.0 %pairs_1.1 = (s16[3,256,256]{2,1,0:T(8,128)(2,1)S(1)}, f32[3,3]{1,0:T(4,128)S(1)}) custom-call(s32[5,12]{1,0:T(8,128)S(1)} %copy-done.5, bf16[16,256,256]{2,1,0:T(8,128)(2,1)S(1)} %bitcast.12, bf16[3,256,256]{2,1,0:T(8,128)(2,1)S(1)} %collective-permute-done.4.below, bf16[3,256,256]{2,1,0:T(8,128)(2,1)} %collective-permute-done.5.later, ...), custom_call_target="tpu_custom_call" | custom-call | tf_op jit(solution)/shard_map/pairs_1/pallas_call | solution.py:254
  149.9 0.1 collective-permute-start.14
  150.0 8.0 %pairs_2.1 = (s16[3,256,256]{2,1,0:T(8,128)(2,1)S(1)}, f32[3,3]{1,0:T(4,128)S(1)}) custom-call(s32[5,12]{1,0:T(8,128)S(1)} %copy-done.5, bf16[16,256,256]{2,1,0:T(8,128)(2,1)S(1)} %bitcast.13, bf16[3,256,256]{2,1,0:T(8,128)(2,1)S(1)} %collective-permute-done.2.below, bf16[3,256,256]{2,1,0:T(8,128)(2,1)} %collective-permute-done.3.later, ...), custom_call_target="tpu_custom_call" | custom-call | tf_op jit(solution)/shard_map/pairs_2/pallas_call | solution.py:254
  158.0 0.1 collective-permute-start.13
  158.1 0.1 collective-permute-start.12
  158.3 2.0 %collective-permute-start.11 = (f32[3,3]{1,0:T(4,128)S(1)}, f32[3,3]{1,0:T(4,128)S(1)}, u32[]{:S(2)}, u32[]{:S(2)}) collective-permute-start(f32[3,3]{1,0:T(4,128)S(1)} %get-tuple-element.25.refs_1_), channel_id=1, source_target_pairs={{0,4},{4,8},{8,12},{12,0},{1,5},{5,9},{9,13},{13,1},{2,6},{6,10},{... | collective-permute-start | bytes 116 | tf_op jit(solution)/shard_map/ppermute | solution.py:31
  160.2 7.1 %pairs_0.1 = (s16[3,256,256]{2,1,0:T(8,128)(2,1)S(1)}, f32[3,3]{1,0:T(4,128)S(1)}) custom-call(s32[5,12]{1,0:T(8,128)S(1)} %copy-done.5, bf16[16,256,256]{2,1,0:T(8,128)(2,1)S(1)} %bitcast.14, bf16[3,256,256]{2,1,0:T(8,128)(2,1)S(1)} %collective-permute-done.8.below, bf16[3,256,256]{2,1,0:T(8,128)(2,1)S(1)} %collective-permute-done.9.later, ...), custom_call_target="tpu_custom_call" | custom-call | tf_op jit(solution)/shard_map/pairs_0/pallas_call | solution.py:254
  167.3 10.3 %collective-permute-done.12.refs_6_ = f32[3,3]{1,0:T(4,128)S(1)} collective-permute-done((f32[3,3]{1,0:T(4,128)S(1)}, f32[3,3]{1,0:T(4,128)S(1)}, u32[]{:S(2)}, u32[]{:S(2)}) %collective-permute-start.12) | collective-permute-done | bytes 68 | tf_op jit(solution)/shard_map/ppermute | solution.py:31
  177.6 4.5 %collective-permute-done.10.refs_4_ = f32[3,3]{1,0:T(4,128)S(1)} collective-permute-done((f32[3,3]{1,0:T(4,128)S(1)}, f32[3,3]{1,0:T(4,128)S(1)}, u32[]{:S(2)}, u32[]{:S(2)}) %collective-permute-start.10) | collective-permute-done | bytes 68 | tf_op jit(solution)/shard_map/ppermute | solution.py:31
  182.1 2.5 %settle.1 = (f32[6,256,256]{2,1,0:T(8,128)}, f32[12]{0:T(128)}) custom-call(s32[5,12]{1,0:T(8,128)S(1)} %copy-done.5, f32[3,3]{1,0:T(4,128)S(1)} %get-tuple-element.22.refs_0_, f32[3,3]{1,0:T(4,128)S(1)} %get-tuple-element.25.refs_1_, f32[3,3]{1,0:T(4,128)S(1)} %get-tuple-element.28.refs_2_, f32[3,3]{1,0:T(4,128)S(1)} %get-tuple-element.31.refs_3_.refs_7_, ...), custom_call_target="tpu_custom_call" | custom-call | tf_op jit(solution)/shard_map/settle/pallas_call | solution.py:282
  (30 shorter events, 0.1 us)
Async XLA Ops:
  4.1 5.7 %collective-permute-start.1 = (s32[5,12]{1,0:T(8,128)}, s32[5,12]{1,0:T(8,128)S(1)}, u32[]{:S(2)}, u32[]{:S(2)}) collective-permute-start(s32[5,12]{1,0:T(8,128)} %lanes.1.table), channel_id=1, source_target_pairs={{0,2},{1,3},{4,6},{5,7},{8,10},{9,11},{12,14},{13,15},{16,18},{17,... | collective-permute-start | bytes 728 | tf_op jit(solution)/shard_map/ppermute | solution.py:26
  5.4 5.7 %collective-permute-start = (s32[5,12]{1,0:T(8,128)}, s32[5,12]{1,0:T(8,128)S(1)}, u32[]{:S(2)}, u32[]{:S(2)}) collective-permute-start(s32[5,12]{1,0:T(8,128)} %lanes.1.table), channel_id=1, source_target_pairs={{0,4},{4,8},{8,12},{1,5},{5,9},{9,13},{2,6},{6,10},{10,14},{3,7},{... | collective-permute-start | bytes 728 | tf_op jit(solution)/shard_map/ppermute | solution.py:26
  9.8 1.3 copy-start.6
  11.1 0.6 copy-start.7
  37.5 64.9 %collective-permute-start.6 = (bf16[3,256,256]{2,1,0:T(8,128)(2,1)}, bf16[3,256,256]{2,1,0:T(8,128)(2,1)}, u32[]{:S(2)}, u32[]{:S(2)}) collective-permute-start(bf16[3,256,256]{2,1,0:T(8,128)(2,1)} %get-tuple-element.26), channel_id=1, source_target_pairs={{4,0},{8,4},{12,8},{5,1},{9,5},{13,9},{6,2},{10,6},{14,10},{7,3},{... | collective-permute-start | bytes 1179656 | tf_op jit(solution)/shard_map/ppermute | solution.py:26
  39.4 90.8 %collective-permute-start.7 = (bf16[3,256,256]{2,1,0:T(8,128)(2,1)}, bf16[3,256,256]{2,1,0:T(8,128)(2,1)}, u32[]{:S(2)}, u32[]{:S(2)}) collective-permute-start(bf16[3,256,256]{2,1,0:T(8,128)(2,1)} %get-tuple-element.27), channel_id=1, source_target_pairs={{2,0},{3,1},{6,4},{7,5},{10,8},{11,9},{14,12},{15,13},{18,16},{19,... | collective-permute-start | bytes 1179656 | tf_op jit(solution)/shard_map/ppermute | solution.py:26
  70.5 70.0 %collective-permute-start.4 = (bf16[3,256,256]{2,1,0:T(8,128)(2,1)}, bf16[3,256,256]{2,1,0:T(8,128)(2,1)S(1)}, u32[]{:S(2)}, u32[]{:S(2)}) collective-permute-start(bf16[3,256,256]{2,1,0:T(8,128)(2,1)} %get-tuple-element.23), channel_id=1, source_target_pairs={{4,0},{8,4},{12,8},{5,1},{9,5},{13,9},{6,2},{10,6},{14,10},{7,3},{... | collective-permute-start | bytes 1179656 | tf_op jit(solution)/shard_map/ppermute | solution.py:26
  72.4 59.9 %copy-start = (bf16[1,1,16,256,256]{4,3,2,1,0:T(8,128)(2,1)S(1)}, bf16[1,1,16,256,256]{4,3,2,1,0:T(8,128)(2,1)}, u32[]{:S(2)}) copy-start(bf16[1,1,16,256,256]{4,3,2,1,0:T(8,128)(2,1)} %param.7) | copy-start | bytes 6291460
  72.5 59.9 %copy-start.1 = (bf16[256,256]{1,0:T(8,128)(2,1)S(1)}, bf16[256,256]{1,0:T(8,128)(2,1)}, u32[]{:S(2)}) copy-start(bf16[256,256]{1,0:T(8,128)(2,1)} %constant.11.clone.sl) | copy-start | bytes 393220
  72.5 59.9 %copy-start.2 = (bf16[256,256]{1,0:T(8,128)(2,1)S(1)}, bf16[256,256]{1,0:T(8,128)(2,1)}, u32[]{:S(2)}) copy-start(bf16[256,256]{1,0:T(8,128)(2,1)} %constant.10.clone.sh) | copy-start | bytes 393220
  72.5 59.9 %copy-start.3 = (bf16[256,256]{1,0:T(8,128)(2,1)S(1)}, bf16[256,256]{1,0:T(8,128)(2,1)}, u32[]{:S(2)}) copy-start(bf16[256,256]{1,0:T(8,128)(2,1)} %constant.9.clone.tl) | copy-start | bytes 393220
  72.5 59.9 %copy-start.4 = (bf16[256,256]{1,0:T(8,128)(2,1)S(1)}, bf16[256,256]{1,0:T(8,128)(2,1)}, u32[]{:S(2)}) copy-start(bf16[256,256]{1,0:T(8,128)(2,1)} %constant.8.clone.th) | copy-start | bytes 393220
  72.5 59.9 %copy-start.5 = (s32[5,12]{1,0:T(8,128)S(1)}, s32[5,12]{1,0:T(8,128)}, u32[]{:S(2)}) copy-start(s32[5,12]{1,0:T(8,128)} %lanes.1.table) | copy-start | bytes 724
  72.5 69.3 %collective-permute-start.5 = (bf16[3,256,256]{2,1,0:T(8,128)(2,1)}, bf16[3,256,256]{2,1,0:T(8,128)(2,1)}, u32[]{:S(2)}, u32[]{:S(2)}) collective-permute-start(bf16[3,256,256]{2,1,0:T(8,128)(2,1)} %get-tuple-element.24), channel_id=1, source_target_pairs={{2,0},{3,1},{6,4},{7,5},{10,8},{11,9},{14,12},{15,13},{18,16},{19,... | collective-permute-start | bytes 1179656 | tf_op jit(solution)/shard_map/ppermute | solution.py:26
  100.5 49.4 %collective-permute-start.2 = (bf16[3,256,256]{2,1,0:T(8,128)(2,1)}, bf16[3,256,256]{2,1,0:T(8,128)(2,1)S(1)}, u32[]{:S(2)}, u32[]{:S(2)}) collective-permute-start(bf16[3,256,256]{2,1,0:T(8,128)(2,1)} %get-tuple-element.20), channel_id=1, source_target_pairs={{4,0},{8,4},{12,8},{5,1},{9,5},{13,9},{6,2},{10,6},{14,10},{7,3},{... | collective-permute-start | bytes 1179656 | tf_op jit(solution)/shard_map/ppermute | solution.py:26
  102.4 47.6 %collective-permute-start.3 = (bf16[3,256,256]{2,1,0:T(8,128)(2,1)}, bf16[3,256,256]{2,1,0:T(8,128)(2,1)}, u32[]{:S(2)}, u32[]{:S(2)}) collective-permute-start(bf16[3,256,256]{2,1,0:T(8,128)(2,1)} %get-tuple-element.21), channel_id=1, source_target_pairs={{2,0},{3,1},{6,4},{7,5},{10,8},{11,9},{14,12},{15,13},{18,16},{19,... | collective-permute-start | bytes 1179656 | tf_op jit(solution)/shard_map/ppermute | solution.py:26
  130.2 10.2 %copy-start.8 = (bf16[3,256,256]{2,1,0:T(8,128)(2,1)S(1)}, bf16[3,256,256]{2,1,0:T(8,128)(2,1)}, u32[]{:S(2)}) copy-start(bf16[3,256,256]{2,1,0:T(8,128)(2,1)} %get-tuple-element.30) | copy-start | bytes 1179652
  130.3 27.9 %collective-permute-start.8 = (bf16[3,256,256]{2,1,0:T(8,128)(2,1)}, bf16[3,256,256]{2,1,0:T(8,128)(2,1)S(1)}, u32[]{:S(2)}, u32[]{:S(2)}) collective-permute-start(bf16[3,256,256]{2,1,0:T(8,128)(2,1)} %get-tuple-element.29), channel_id=1, source_target_pairs={{4,0},{8,4},{12,8},{5,1},{9,5},{13,9},{6,2},{10,6},{14,10},{7,3},{... | collective-permute-start | bytes 1179656 | tf_op jit(solution)/shard_map/ppermute | solution.py:26
  140.5 17.8 %collective-permute-start.9 = (bf16[3,256,256]{2,1,0:T(8,128)(2,1)S(1)}, bf16[3,256,256]{2,1,0:T(8,128)(2,1)S(1)}, u32[]{:S(2)}, u32[]{:S(2)}) collective-permute-start(bf16[3,256,256]{2,1,0:T(8,128)(2,1)S(1)} %copy-done.8), channel_id=1, source_target_pairs={{2,0},{3,1},{6,4},{7,5},{10,8},{11,9},{14,12},{15,13},{18,16},{19,... | collective-permute-start | bytes 1179656 | tf_op jit(solution)/shard_map/ppermute | solution.py:26
  141.8 40.2 %collective-permute-start.15 = (s16[3,256,256]{2,1,0:T(8,128)(2,1)S(1)}, s16[3,256,256]{2,1,0:T(8,128)(2,1)S(1)}, u32[]{:S(2)}, u32[]{:S(2)}) collective-permute-start(s16[3,256,256]{2,1,0:T(8,128)(2,1)S(1)} %get-tuple-element.34), channel_id=1, source_target_pairs={{0,12},{4,0},{8,4},{12,8},{1,13},{5,1},{9,5},{13,9},{2,14},{6,2},{... | collective-permute-start | bytes 1179656 | tf_op jit(solution)/shard_map/ppermute | solution.py:31
  149.9 32.1 %collective-permute-start.14 = (s16[3,256,256]{2,1,0:T(8,128)(2,1)S(1)}, s16[3,256,256]{2,1,0:T(8,128)(2,1)S(1)}, u32[]{:S(2)}, u32[]{:S(2)}) collective-permute-start(s16[3,256,256]{2,1,0:T(8,128)(2,1)S(1)} %get-tuple-element.33), channel_id=1, source_target_pairs={{0,4},{4,8},{8,12},{12,0},{1,5},{5,9},{9,13},{13,1},{2,6},{6,10},{... | collective-permute-start | bytes 1179656 | tf_op jit(solution)/shard_map/ppermute | solution.py:31
  158.0 24.0 %collective-permute-start.13 = (s16[3,256,256]{2,1,0:T(8,128)(2,1)S(1)}, s16[3,256,256]{2,1,0:T(8,128)(2,1)S(1)}, u32[]{:S(2)}, u32[]{:S(2)}) collective-permute-start(s16[3,256,256]{2,1,0:T(8,128)(2,1)S(1)} %get-tuple-element.32), channel_id=1, source_target_pairs={{0,8},{4,12},{8,0},{12,4},{1,9},{5,13},{9,1},{13,5},{2,10},{6,14},... | collective-permute-start | bytes 1179656 | tf_op jit(solution)/shard_map/ppermute | solution.py:31
  158.1 19.4 %collective-permute-start.12 = (f32[3,3]{1,0:T(4,128)S(1)}, f32[3,3]{1,0:T(4,128)S(1)}, u32[]{:S(2)}, u32[]{:S(2)}) collective-permute-start(f32[3,3]{1,0:T(4,128)S(1)} %get-tuple-element.28.refs_2_), channel_id=1, source_target_pairs={{0,12},{4,0},{8,4},{12,8},{1,13},{5,1},{9,5},{13,9},{2,14},{6,2},{... | collective-permute-start | bytes 116 | tf_op jit(solution)/shard_map/ppermute | solution.py:31
  158.3 19.3 %collective-permute-start.11 = (f32[3,3]{1,0:T(4,128)S(1)}, f32[3,3]{1,0:T(4,128)S(1)}, u32[]{:S(2)}, u32[]{:S(2)}) collective-permute-start(f32[3,3]{1,0:T(4,128)S(1)} %get-tuple-element.25.refs_1_), channel_id=1, source_target_pairs={{0,4},{4,8},{8,12},{12,0},{1,5},{5,9},{9,13},{13,1},{2,6},{6,10},{... | collective-permute-start | bytes 116 | tf_op jit(solution)/shard_map/ppermute | solution.py:31
  177.6 4.5 %collective-permute-start.10 = (f32[3,3]{1,0:T(4,128)S(1)}, f32[3,3]{1,0:T(4,128)S(1)}, u32[]{:S(2)}, u32[]{:S(2)}) collective-permute-start(f32[3,3]{1,0:T(4,128)S(1)} %get-tuple-element.22.refs_0_), channel_id=1, source_target_pairs={{0,8},{4,12},{8,0},{12,4},{1,9},{5,13},{9,1},{13,5},{2,10},{6,14},... | collective-permute-start | bytes 116 | tf_op jit(solution)/shard_map/ppermute | solution.py:31

commit v2 on v1

v2 whole, which is shorter than its diff:
```python
import functools

import jax
import jax.numpy as jnp
import ml_dtypes
import numpy as np
from jax import lax
from jax.experimental import pallas as pl
from jax.experimental.pallas import tpu as pltpu
from jax.sharding import PartitionSpec as P

FLOOR = 0.05
TOP = 32700.0
STEPS = 8.0
HEAD = 16
SETTLE = 200_000_000
HALF = 16384.0
TINY = 1e-28
LIMIT = 48 * 1024 * 1024

ANY = pl.BlockSpec(memory_space=pl.ANY)
SMEM = pl.BlockSpec(memory_space=pltpu.SMEM)
VMEM = pl.BlockSpec(memory_space=pltpu.VMEM)
SDS = jax.ShapeDtypeStruct


def shifted(value, axis, steps):
    count = lax.axis_size(axis)
    pairs = [(i, i + steps) for i in range(count) if 0 <= i + steps < count]
    return lax.ppermute(value, axis, pairs)


def rotated(value, axis, steps):
    count = lax.axis_size(axis)
    return lax.ppermute(value, axis, [(i, (i + steps) % count) for i in range(count)])


def packed_table(length):
    half = length // 2
    n = np.arange(length)[:, None]
    v = np.arange(half + 1)[None, :]
    angle = 2.0 * np.pi * ((n * v) % length) / length
    table = np.concatenate([np.cos(angle), np.sin(angle[:, 1:half])], axis=1)
    high = table.astype(np.float32).astype(ml_dtypes.bfloat16)
    low = (table - high.astype(np.float64)).astype(np.float32).astype(ml_dtypes.bfloat16)
    return high, low


def dot(left, right):
    return jnp.dot(left, right, preferred_element_type=jnp.float32)


def pieces(value):
    high = value.astype(jnp.bfloat16)
    low = (value - high.astype(jnp.float32)).astype(jnp.bfloat16)
    return high, low


def two_lines(packed, half, row, col, edge):
    cp, cq = packed[:half, :half], packed[:half, half:]
    sp, sq = packed[half:, :half], packed[half:, half:]
    sq_in = jnp.where(edge, 0.0, sq)
    re1 = cp - sq_in
    im1 = -(jnp.where(row, 0.0, sp) + jnp.where(col, 0.0, cq))
    re2 = jnp.where(row, sp, jnp.where(col, cq, cp + sq))
    im2 = jnp.where(edge, -sq, sp - cq)
    return re1, im1, re2, im2


def normalized_packed(one, two, length):
    half = length // 2
    floor = FLOOR * length * length
    rows = lax.broadcasted_iota(jnp.int32, (half, half), 0)
    cols = lax.broadcasted_iota(jnp.int32, (half, half), 1)
    row, col = rows == 0, cols == 0
    edge, corner = row | col, row & col
    a_re1, a_im1, a_re2, a_im2 = two_lines(one, half, row, col, edge)
    b_re1, b_im1, b_re2, b_im2 = two_lines(two, half, row, col, edge)

    def scaled(a_re, a_im, b_re, b_im):
        re = a_re * b_re + a_im * b_im
        im = a_im * b_re - a_re * b_im
        factor = jnp.minimum(lax.rsqrt(re * re + im * im), 1.0 / floor)
        return re * factor, im * factor

    n_re1, n_im1 = scaled(a_re1, a_im1, b_re1, b_im1)
    n_re2, n_im2 = scaled(a_re2, a_im2, b_re2, b_im2)

    def real_corner(value, start_row, start_col):
        a = one[start_row : start_row + half, start_col : start_col + half]
        b = two[start_row : start_row + half, start_col : start_col + half]
        product = a * b
        alone = 0.5 * product / jnp.maximum(jnp.abs(product), floor)
        return jnp.where(corner, alone, value)

    cp = jnp.where(edge, n_re1, n_re1 + n_re2)
    cq = jnp.where(row, -n_im1, jnp.where(col, n_re2, -(n_im1 + n_im2)))
    sp = jnp.where(row, n_re2, jnp.where(col, -n_im1, n_im2 - n_im1))
    sq = jnp.where(edge, -n_im2, n_re2 - n_re1)
    cp = real_corner(cp, 0, 0)
    cq = real_corner(cq, 0, half)
    sp = real_corner(sp, half, 0)
    sq = real_corner(sq, half, half)
    packed = jnp.concatenate(
        [jnp.concatenate([cp, cq], axis=1), jnp.concatenate([sp, sq], axis=1)], axis=0
    )
    return packed * (2.0 / length)


def lanes_kernel(tiles, per, pairs, plan, table):
    slots = pairs.shape[-1]
    me = lax.axis_index("tile")
    for lane in range(tiles * per):
        table[0, lane] = -1
        for field in range(1, 3):
            table[field, lane] = 0
        for field in range(3, 5):
            table[field, lane] = -1
    targets = [plan[0, 0, 0, k] for k in range(slots)]
    for k, target in enumerate(targets):
        rank = jnp.int32(0)
        for earlier in targets[:k]:
            rank += (earlier == target).astype(jnp.int32)
        distance = lax.rem(target - me + tiles, tiles)
        lane = distance * per + rank

        @pl.when(target >= 0)
        def _():
            for field in range(3):
                table[field, lane] = pairs[field, 0, 0, k]
            table[3, lane] = plan[1, 0, 0, k]
            table[4, lane] = k


def gather_kernel(lanes_of, *refs):
    count = len(lanes_of)
    tables, patches = refs[1 : count + 1], refs[count + 1]
    *sent, token = refs[-count - 1 :]
    token[0] = 0
    for table, wanted, out in zip(tables, lanes_of, sent):
        for i, (field, lane) in enumerate(wanted):
            out[i] = patches[table[field, lane]]


def correlate(firsts, seconds, places, guests, th, tl, sh, sl, codes, peaks):
    length = codes.shape[-1]
    per = len(firsts)
    packed = [dot(p, th[...]) + dot(p, tl[...]) for p in firsts + seconds]
    packed = [pieces(p) for p in packed]
    packed = [dot(sh[...], h) + dot(sh[...], w) + dot(sl[...], h) for h, w in packed]
    both = [normalized_packed(packed[j], packed[per + j], length) for j in range(per)]
    both = [pieces(p) for p in both]
    both = [dot(th[...], h) + dot(th[...], w) + dot(tl[...], h) for h, w in both]
    both = [pieces(p) for p in both]
    both = [dot(h, sh[...]) + dot(h, sl[...]) + dot(w, sh[...]) for h, w in both]
    cols = lax.broadcasted_iota(jnp.int32, (HEAD, length), 1)
    head = guest_head(guests, length)
    for j, surface in enumerate(both):
        peaks[j] = jnp.max(surface)
        size = jnp.max(jnp.max(jnp.abs(surface), axis=0, keepdims=True), axis=1, keepdims=True)
        step = jnp.ceil(STEPS * jnp.log2(jnp.maximum(size, TINY)))
        grown = jnp.abs(surface) * (TOP * TOP * jnp.exp2(step * (-1.0 / STEPS)))
        root = grown * lax.rsqrt(jnp.maximum(grown, TINY))
        whole = (root + 0.5).astype(jnp.int32)
        whole = jnp.where(surface < 0, -whole, whole)
        codes[j * length : (j + 1) * length] = whole.astype(jnp.int16)
        head = jnp.where(cols == j, step.astype(jnp.int32), head)
        head = jnp.where(cols == per + j, places[j], head)
    codes[per * length :] = head.astype(jnp.int16)


def guest_head(guests, length):
    cols = lax.broadcasted_iota(jnp.int32, (HEAD, length), 1)
    head = jnp.zeros((HEAD, length), jnp.int32)
    if guests is None:
        return head
    per = guests.shape[0]
    for j in range(per):
        peak = jnp.full((HEAD, length), guests[j])
        power = jnp.ceil(jnp.log2(jnp.maximum(jnp.abs(peak), TINY)))
        share = peak * jnp.exp2(-power) * HALF
        high = share.astype(jnp.int32)
        low = ((share - high.astype(jnp.float32)) * HALF).astype(jnp.int32)
        for i, part in enumerate((power.astype(jnp.int32), high, low)):
            head = jnp.where(cols == 2 * per + 3 * j + i, part, head)
    return head


def guest_peak(head, per, j):
    cols = lax.broadcasted_iota(jnp.int32, head.shape, 1)

    def part(i):
        one = jnp.where(cols == 2 * per + 3 * j + i, head, 0)[:1]
        return jnp.sum(one.astype(jnp.float32), axis=1, keepdims=True)

    return jnp.max((part(1) + part(2) * (1.0 / HALF)) * (1.0 / HALF) * jnp.exp2(part(0)))


def any_of(flags):
    some = flags[0]
    for flag in flags[1:]:
        some = some | flag
    return some


def pair_kernel(lanes, at_below, at_later, live_kind, with_guests, table, before, own, *refs):
    per = len(lanes)
    at_hand = refs[1:3]
    guests = refs[0] if with_guests else None
    th, tl, sh, sl = refs[3:7]
    codes, peaks = refs[-2:]
    kinds = [table[0, lane] for lane in lanes]
    for j in range(per):
        peaks[j] = 0.0
    codes[per * codes.shape[-1] :] = guest_head(guests, codes.shape[-1]).astype(jnp.int16)
    wanted = [k >= 0 if live_kind is None else k == live_kind for k in kinds]

    @pl.when(any_of(wanted))
    def _():
        places = [jnp.where(w, table[3, lane] + 1, 0) for w, lane in zip(wanted, lanes)]
        firsts = [own[table[1, lane]] for lane in lanes]
        seconds = [at_hand[1][at_later + j] for j in range(per)]
        if live_kind is None:
            seconds = [
                jnp.where(kinds[j] == 0, at_hand[0][at_below + j], seconds[j]) for j in range(per)
            ]
        correlate(firsts, seconds, places, guests, th, tl, sh, sl, codes, peaks)


def near_kernel(
    lanes, table, table_above, token, own, up, later, th, tl, sh, sl, codes, peaks, visit_codes, visit_peaks
):
    pair_kernel(
        lanes, 0, 0, 1, False, table, token, own, None, None, later, th, tl, sh, sl, codes, peaks
    )
    per = len(lanes)
    row = lax.axis_index("tile")
    for j in range(per):
        visit_peaks[j] = 0.0
    length = codes.shape[-1]
    visit_codes[per * length :] = jnp.zeros((HEAD, length), jnp.int32).astype(jnp.int16)
    kinds = [table_above[0, lane] for lane in lanes]

    @pl.when((row > 0) & any_of([kind == 0 for kind in kinds]))
    def _():
        firsts = [up[j] for j in range(per)]
        seconds = [own[table_above[2, lane]] for lane in lanes]
        places = [
            jnp.where(kind == 0, table_above[3, lane] + 1, 0) for kind, lane in zip(kinds, lanes)
        ]
        correlate(
            firsts, seconds, places, None, th, tl, sh, sl, visit_codes, visit_peaks
        )


def settle_kernel(per, count, blank, before, *refs):
    codes = refs[:count]
    surfaces, token, room, sems = refs[-4:]
    length = surfaces.shape[-1]
    total = count * per
    token[0] = 0.0
    if blank:
        room[total] = jnp.zeros((length, length), jnp.float32)
        fills = [
            pltpu.make_async_copy(room.at[total], surfaces.at[k], sems.at[total + k])
            for k in range(surfaces.shape[0])
        ]
        for fill in fills:
            fill.start()
        for fill in fills:
            fill.wait()
    cols = lax.broadcasted_iota(jnp.int32, (HEAD, length), 1)
    wanted, copies = [], []
    for i, coded in enumerate(codes):
        head = coded[per * length :].astype(jnp.int32)
        for j in range(per):
            k = i * per + j
            place = jnp.max(jnp.where(cols == per + j, head, 0))
            wanted.append(place > 0)
            target = jnp.maximum(place - 1, 0)
            copies.append(pltpu.make_async_copy(room.at[k], surfaces.at[target], sems.at[k]))
    for i, coded in enumerate(codes):
        for j in range(per):
            k = i * per + j

            @pl.when(wanted[k])
            def _():
                head = coded[per * length :].astype(jnp.int32)
                step = jnp.where(cols == j, head, -(1 << 15))[:1].astype(jnp.float32)
                scale = jnp.exp2(jnp.max(step, axis=1, keepdims=True) * (1.0 / STEPS))
                value = coded[j * length : (j + 1) * length].astype(jnp.int32).astype(jnp.float32)
                room[k] = value * jnp.abs(value) * (scale * (1.0 / (TOP * TOP)))
                copies[k].start()

    for k in range(total):

        @pl.when(wanted[k])
        def _():
            copies[k].wait()


def settle_peaks_kernel(tiles, per, count, before, *refs):
    codes, table, home_peaks = refs[:count], refs[count], refs[count + 1 : count + 1 + tiles]
    surfaces, peaks, token, room, sems = refs[-5:]
    settle_kernel(per, count, False, before, *codes, surfaces, token, room, sems)
    head = codes[-1][per * surfaces.shape[-1] :].astype(jnp.int32)
    back_peaks = [guest_peak(head, per, j) for j in range(per)]
    for k in range(peaks.shape[0]):
        peaks[k] = 0.0
    for d in range(tiles):
        for j in range(per):
            lane = d * per + j
            slot = table[4, lane]
            peak = home_peaks[d][j]
            if d == 1:
                peak = jnp.where(table[0, lane] == 0, back_peaks[j], peak)

            @pl.when(slot >= 0)
            def _():
                peaks[slot] = peak


def params():
    return pltpu.CompilerParams(vmem_limit_bytes=LIMIT)


def cost(flops=1):
    return pl.CostEstimate(flops=flops, bytes_accessed=1, transcendentals=0)


def body(patches, pair_lists, move_plan):
    own = patches[0, 0]
    length = own.shape[-1]
    slots = pair_lists.shape[-1]
    tiles = lax.axis_size("tile")
    per = (slots + tiles - 1) // tiles
    up_one = tiles - 1
    far = sorted(range(2, up_one), key=lambda d: -min(d, tiles - d))
    groups_below = [far, [up_one, 0]]
    groups_later = [far, [1, up_one], [0]]

    def lanes_at(d):
        return [d * per + j for j in range(per)]

    def call(kernel, name, outs, *operands, last=()):
        return pl.pallas_call(
            kernel,
            out_shape=outs,
            in_specs=[VMEM if o.dtype in (own.dtype, jnp.int16) else SMEM for o in operands]
            + [ANY] * len(last),
            out_specs=jax.tree.map(lambda o: SMEM if len(o.shape) == 1 else VMEM, outs),
            compiler_params=params(),
            cost_estimate=cost(),
            name=name,
        )(*operands, *last)

    def picked(name, token, wanted, *arrived):
        lists = [[(f, lane) for d in ds for lane in lanes_at(d)] for _, f, ds in wanted]
        outs = tuple(SDS((len(w), length, length), own.dtype) for w in lists)
        tables = [t for t, _, _ in wanted]
        *sent, token = call(
            functools.partial(gather_kernel, lists),
            name,
            outs + (SDS((1,), jnp.int32),),
            token,
            *tables,
            own,
            last=arrived,
        )
        return sent, token

    table = pl.pallas_call(
        functools.partial(lanes_kernel, tiles, per),
        out_shape=SDS((5, tiles * per), jnp.int32),
        in_specs=[SMEM, SMEM],
        out_specs=SMEM,
        name="lanes",
    )(pair_lists, move_plan)
    table_above = shifted(table, "tile", 1)
    table_before = shifted(table, "sect", 1)
    (first_up, below_0, later_0), token = picked(
        "gather_first",
        table,
        [(table, 1, [1]), (table_above, 2, groups_below[0]), (table_before, 2, groups_later[0])],
    )
    up = shifted(first_up, "tile", 1)
    below_0, later_0 = shifted(below_0, "tile", -1), shifted(later_0, "sect", -1)
    (below_1, later_1, later_2), token = picked(
        "gather_last",
        token,
        [(table_above, 2, groups_below[1])] + [(table_before, 2, g) for g in groups_later[1:]],
        below_0,
        later_0,
        up,
    )
    below = [below_0, shifted(below_1, "tile", -1)]
    later = [later_0, shifted(later_1, "sect", -1), shifted(later_2, "sect", -1)]

    high, low = packed_table(length)
    tables = [jnp.asarray(t) for t in (high, low, high.T.copy(), low.T.copy())]
    result = (SDS((per * length + HEAD, length), jnp.int16), SDS((per,), jnp.float32))

    works = slots // 2
    surfaces_kind, token_kind = SDS((works, length, length), jnp.float32), SDS((1,), jnp.float32)
    peaks_kind = SDS((slots,), jnp.float32)

    def settled(name, all_codes, before, surfaces=None, table=None, home_peaks=()):
        count = len(all_codes)
        extra = ([] if table is None else [table]) + list(home_peaks)
        blank = surfaces is None
        kernel = functools.partial(settle_kernel, per, count, blank)
        if extra:
            kernel = functools.partial(settle_peaks_kernel, tiles, per, count)
        return pl.pallas_call(
            kernel,
            out_shape=(surfaces_kind,) + ((peaks_kind,) if extra else ()) + (token_kind,),
            in_specs=[SMEM] + [VMEM] * count + [SMEM] * len(extra) + ([] if blank else [ANY]),
            out_specs=(ANY,) + ((SMEM,) if extra else ()) + (SMEM,),
            scratch_shapes=[
                pltpu.VMEM((count * per + 1, length, length), jnp.float32),
                pltpu.SemaphoreType.DMA((count * per + works,)),
            ],
            input_output_aliases={} if blank else {1 + count + len(extra): 0},
            compiler_params=params(),
            cost_estimate=cost(SETTLE),
            name=name,
        )(before, *all_codes, *extra, *([] if blank else [surfaces]))

    home_peaks, moving = [None] * tiles, {}

    def paired(d, before, guests, near, late, last=()):
        lane_codes, home_peaks[d] = call(
            functools.partial(
                pair_kernel,
                lanes_at(d),
                groups_below[near].index(d) * per,
                groups_later[late].index(d) * per,
                None,
                d == up_one,
            ),
            f"pairs_{d}",
            result,
            table,
            before,
            own,
            guests,
            below[near],
            later[late],
            *tables,
            last=last,
        )
        moving[d] = lane_codes if d == 0 else rotated(lane_codes, "tile", d)
        return home_peaks[d]

    for d in far:
        token = paired(d, token, token, 0, 0)
    lane_codes, home_peaks[1], visit_codes, guests = call(
        functools.partial(near_kernel, lanes_at(1)),
        "pairs_1",
        result + result,
        table,
        table_above,
        token,
        own,
        up,
        later[1],
        *tables,
    )
    moving[1] = rotated(lane_codes, "tile", 1)
    surfaces, before = settled("settle_visit", [visit_codes], guests)
    before = paired(up_one, before, guests, 1, 1, last=[later[2]])
    before = paired(0, before, before, 1, 2)
    early = [moving[d] for d in [0] + far]
    surfaces, before = settled("settle_early", early, before, surfaces)
    surfaces, before = settled("settle_1", [moving[1]], before, surfaces)
    surfaces, peaks, _ = settled(
        "settle_last", [moving[up_one]], before, surfaces, table, home_peaks
    )
    return surfaces[None, None], peaks[None, None]


def solution(mesh):
    in_specs = (
        P(("groups", "sect"), "tile", "half", None, None),
        P(None, ("groups", "sect"), "tile", "half"),
        P(None, ("groups", "sect"), "tile", "half"),
    )
    out_specs = (
        P(("groups", "sect"), "tile", "half", None, None),
        P(("groups", "sect"), "tile", "half"),
    )
    return jax.shard_map(body, mesh=mesh, in_specs=in_specs, out_specs=out_specs, check_vma=False)
```

time: 185 us -> 91.4 us (0.49)
  the two profiles are of different devices: /device:TPU:14 before, /device:TPU:0 now
where the time goes in v2:
time: 91.4 us
  Pallas kernels  32.9 us (36%)
  starting transfers between devices  29.5 us (32%)
  waiting for transfers between devices  25.7 us (28%)
  local copies, waits for them, and re-layouts  2.3 us (3%)
  between operations  1.05 us (1%)
    pallas_call x6, Pallas kernels, call(): pl.pallas_call(kernel, out_shape=outs, in_specs=[VMEM if o.dtype in (own....  21.1 us
    ppermute x8, starting transfers between devices, shifted(): return lax.ppermute(value, axis, pairs)  19.6 us
    ppermute x8, waiting for transfers between devices, shifted(): return lax.ppermute(value, axis, pairs)  17 us
    pallas_call x4, Pallas kernels, settled(): pl.pallas_call(kernel, out_shape=(surfaces_kind,) + ((peaks_kind,) if ext...  10.3 us
    ppermute x3, starting transfers between devices, rotated(): lax.ppermute(value, axis, [(i, (i + steps) % count) for i in range(count)])  9.88 us
    ppermute x3, waiting for transfers between devices, rotated(): lax.ppermute(value, axis, [(i, (i + steps) % count) for i in range(count)])  8.72 us
    unnamed x16, local copies, waits for them, and re-layouts  2.3 us
  transfers between devices with their start and end apart: 11, of which 6 were waited for; matrix products, arithmetic and copies ran while one was open for 0% of the time, Pallas kernels for 27%

profile of v2, /device:TPU:0, one launch (start us, length us, event | category | flops | bytes accessed | tf_op | source)
XLA Modules:
  0.0 91.4 jit_solution(989479854278289042)
XLA Ops:
  0.6 1.5 %lanes.1.refs_0_.refs_1_.table = s32[5,12]{1,0:T(8,128)} custom-call(s32[3,1,1,12]{3,2,1,0:T(1,128)} %pairs.1, s32[2,1,1,12]{3,2,1,0:T(1,128)} %plan.1), custom_call_target="tpu_custom_call" | custom-call | tf_op jit(solution)/shard_map/lanes/pallas_call | solution.py:372
  2.1 4.8 %collective-permute-start.1 = (s32[5,12]{1,0:T(8,128)}, s32[5,12]{1,0:T(8,128)S(1)}, u32[]{:S(2)}, u32[]{:S(2)}) collective-permute-start(s32[5,12]{1,0:T(8,128)} %lanes.1.refs_0_.refs_1_.table), channel_id=1, source_target_pairs={{0,2},{1,3},{4,6},{5,7},{8,10},{9,11},{12,14},{13,15},{16,18},{17,... | collective-permute-start | bytes 728 | tf_op jit(solution)/shard_map/ppermute | solution.py:30
  7.0 3.5 %collective-permute-start = (s32[5,12]{1,0:T(8,128)}, s32[5,12]{1,0:T(8,128)S(1)}, u32[]{:S(2)}, u32[]{:S(2)}) collective-permute-start(s32[5,12]{1,0:T(8,128)} %lanes.1.refs_0_.refs_1_.table), channel_id=1, source_target_pairs={{0,4},{4,8},{8,12},{1,5},{5,9},{9,13},{2,6},{6,10},{10,14},{3,7},{... | collective-permute-start | bytes 728 | tf_op jit(solution)/shard_map/ppermute | solution.py:30
  10.5 1.5 %collective-permute-done.refs_2_.refs_1_.table_above = s32[5,12]{1,0:T(8,128)S(1)} collective-permute-done((s32[5,12]{1,0:T(8,128)}, s32[5,12]{1,0:T(8,128)S(1)}, u32[]{:S(2)}, u32[]{:S(2)}) %collective-permute-start) | collective-permute-done | bytes 272 | tf_op jit(solution)/shard_map/ppermute | solution.py:30
  12.0 1.6 %copy-done = bf16[1,1,16,256,256]{4,3,2,1,0:T(8,128)(2,1)S(1)} copy-done((bf16[1,1,16,256,256]{4,3,2,1,0:T(8,128)(2,1)S(1)}, bf16[1,1,16,256,256]{4,3,2,1,0:T(8,128)(2,1)}, u32[]{:S(2)}) %copy-start) | copy-done | bytes 2097176
  13.6 0.7 copy-done.6
  14.3 1.3 %gather_first.1 = (bf16[3,256,256]{2,1,0:T(8,128)(2,1)S(1)}, bf16[3,256,256]{2,1,0:T(8,128)(2,1)S(1)}, bf16[3,256,256]{2,1,0:T(8,128)(2,1)S(1)}, s32[1]{0:T(128)}) custom-call(s32[5,12]{1,0:T(8,128)S(1)} %copy-done.6, s32[5,12]{1,0:T(8,128)S(1)} %copy-done.6, s32[5,12]{1,0:T(8,128)S(1)} %collective-permute-done.refs_2_.refs_1_.table_above, ...), custom_call_target="tpu_custom_call" | custom-call | flops 1 | bytes 1 | tf_op jit(solution)/shard_map/gather_first/pallas_call | solution.py:346
  15.6 1.3 %collective-permute-start.2 = (bf16[3,256,256]{2,1,0:T(8,128)(2,1)S(1)}, bf16[3,256,256]{2,1,0:T(8,128)(2,1)S(1)}, u32[]{:S(2)}, u32[]{:S(2)}) collective-permute-start(bf16[3,256,256]{2,1,0:T(8,128)(2,1)S(1)} %get-tuple-element.29), channel_id=1, source_target_pairs={{4,0},{8,4},{12,8},{5,1},{9,5},{13,9},{6,2},{10,6},{14,10},{7,3},{... | collective-permute-start | bytes 1179656 | tf_op jit(solution)/shard_map/ppermute | solution.py:30
  16.9 1.3 %collective-permute-start.3 = (bf16[3,256,256]{2,1,0:T(8,128)(2,1)S(1)}, bf16[3,256,256]{2,1,0:T(8,128)(2,1)S(1)}, u32[]{:S(2)}, u32[]{:S(2)}) collective-permute-start(bf16[3,256,256]{2,1,0:T(8,128)(2,1)S(1)} %get-tuple-element.30), channel_id=1, source_target_pairs={{2,0},{3,1},{6,4},{7,5},{10,8},{11,9},{14,12},{15,13},{18,16},{19,... | collective-permute-start | bytes 1179656 | tf_op jit(solution)/shard_map/ppermute | solution.py:30
  18.2 4.8 %collective-permute-start.4 = (bf16[3,256,256]{2,1,0:T(8,128)(2,1)S(1)}, bf16[3,256,256]{2,1,0:T(8,128)(2,1)S(1)}, u32[]{:S(2)}, u32[]{:S(2)}) collective-permute-start(bf16[3,256,256]{2,1,0:T(8,128)(2,1)S(1)} %get-tuple-element.31), channel_id=1, source_target_pairs={{0,4},{4,8},{8,12},{1,5},{5,9},{9,13},{2,6},{6,10},{10,14},{3,7},{... | collective-permute-start | bytes 1179656 | tf_op jit(solution)/shard_map/ppermute | solution.py:30
  23.1 4.4 %collective-permute-done.2.refs_5_.refs_1_ = bf16[3,256,256]{2,1,0:T(8,128)(2,1)S(1)} collective-permute-done((bf16[3,256,256]{2,1,0:T(8,128)(2,1)S(1)}, bf16[3,256,256]{2,1,0:T(8,128)(2,1)S(1)}, u32[]{:S(2)}, u32[]{:S(2)}) %collective-permute-start.2) | collective-permute-done | bytes 393248 | tf_op jit(solution)/shard_map/ppermute | solution.py:30
  27.5 1.1 %collective-permute-done.3.refs_6_.refs_2_ = bf16[3,256,256]{2,1,0:T(8,128)(2,1)S(1)} collective-permute-done((bf16[3,256,256]{2,1,0:T(8,128)(2,1)S(1)}, bf16[3,256,256]{2,1,0:T(8,128)(2,1)S(1)}, u32[]{:S(2)}, u32[]{:S(2)}) %collective-permute-start.3) | collective-permute-done | bytes 393248 | tf_op jit(solution)/shard_map/ppermute | solution.py:30
  28.5 1.4 %collective-permute-done.4.refs_7_.up = bf16[3,256,256]{2,1,0:T(8,128)(2,1)S(1)} collective-permute-done((bf16[3,256,256]{2,1,0:T(8,128)(2,1)S(1)}, bf16[3,256,256]{2,1,0:T(8,128)(2,1)S(1)}, u32[]{:S(2)}, u32[]{:S(2)}) %collective-permute-start.4) | collective-permute-done | bytes 393248 | tf_op jit(solution)/shard_map/ppermute | solution.py:30
  30.0 0.0 copy-start.5
  30.0 0.0 copy-start.7
  30.0 2.0 %gather_last.1 = (bf16[6,256,256]{2,1,0:T(8,128)(2,1)S(1)}, bf16[6,256,256]{2,1,0:T(8,128)(2,1)S(1)}, bf16[3,256,256]{2,1,0:T(8,128)(2,1)S(1)}, s32[1]{0:T(128)}) custom-call(s32[1]{0:T(128)} %get-tuple-element.28.refs_0_, s32[5,12]{1,0:T(8,128)S(1)} %collective-permute-done.refs_2_.refs_1_.table_above, s32[5,12]{1,0:T(8,128)S(1)} %collective-permute-done.1.refs_3_.refs_2_, ...), custom_call_target="tpu_custom_call" | custom-call | flops 1 | bytes 1 | tf_op jit(solution)/shard_map/gather_last/pallas_call | solution.py:346
  32.0 1.3 %collective-permute-start.5 = (bf16[6,256,256]{2,1,0:T(8,128)(2,1)S(1)}, bf16[6,256,256]{2,1,0:T(8,128)(2,1)S(1)}, u32[]{:S(2)}, u32[]{:S(2)}) collective-permute-start(bf16[6,256,256]{2,1,0:T(8,128)(2,1)S(1)} %get-tuple-element.34), channel_id=1, source_target_pairs={{2,0},{3,1},{6,4},{7,5},{10,8},{11,9},{14,12},{15,13},{18,16},{19,... | collective-permute-start | bytes 2359304 | tf_op jit(solution)/shard_map/ppermute | solution.py:30
  33.3 1.3 %collective-permute-start.6 = (bf16[6,256,256]{2,1,0:T(8,128)(2,1)S(1)}, bf16[6,256,256]{2,1,0:T(8,128)(2,1)S(1)}, u32[]{:S(2)}, u32[]{:S(2)}) collective-permute-start(bf16[6,256,256]{2,1,0:T(8,128)(2,1)S(1)} %get-tuple-element.38), channel_id=1, source_target_pairs={{4,0},{8,4},{12,8},{5,1},{9,5},{13,9},{6,2},{10,6},{14,10},{7,3},{... | collective-permute-start | bytes 2359304 | tf_op jit(solution)/shard_map/ppermute | solution.py:30
  34.6 1.3 %collective-permute-start.7 = (bf16[3,256,256]{2,1,0:T(8,128)(2,1)S(1)}, bf16[3,256,256]{2,1,0:T(8,128)(2,1)S(1)}, u32[]{:S(2)}, u32[]{:S(2)}) collective-permute-start(bf16[3,256,256]{2,1,0:T(8,128)(2,1)S(1)} %get-tuple-element.39), channel_id=1, source_target_pairs={{2,0},{3,1},{6,4},{7,5},{10,8},{11,9},{14,12},{15,13},{18,16},{19,... | collective-permute-start | bytes 1179656 | tf_op jit(solution)/shard_map/ppermute | solution.py:30
  35.9 5.2 %pairs_2.1 = (s16[784,256]{1,0:T(8,128)(2,1)S(1)}, f32[3]{0:T(128)S(1)}) custom-call(s32[5,12]{1,0:T(8,128)S(1)} %copy-done.7, s32[1]{0:T(128)} %get-tuple-element.32.before.refs_0_, bf16[16,256,256]{2,1,0:T(8,128)(2,1)S(1)} %bitcast.5, s32[1]{0:T(128)} %get-tuple-element.32.before.refs_0_, bf16[3,256,256]{2,1,0:T(8,128)(2,1)S(1)} %collective-permute-done.2.refs_5_.refs_1_, ...), custom_call_target="tpu_custom_call" | custom-call | flops 1 | bytes 1 | tf_op jit(solution)/shard_map/pairs_2/pallas_call | solution.py:346
  41.2 4.6 %collective-permute-start.8 = (s16[784,256]{1,0:T(8,128)(2,1)S(1)}, s16[784,256]{1,0:T(8,128)(2,1)S(1)}, u32[]{:S(2)}, u32[]{:S(2)}) collective-permute-start(s16[784,256]{1,0:T(8,128)(2,1)S(1)} %get-tuple-element.43), channel_id=1, source_target_pairs={{0,8},{4,12},{8,0},{12,4},{1,9},{5,13},{9,1},{13,5},{2,10},{6,14},... | collective-permute-start | bytes 1204232 | tf_op jit(solution)/shard_map/ppermute | solution.py:35
  45.8 8.5 %collective-permute-done.5.later.refs_2_ = bf16[6,256,256]{2,1,0:T(8,128)(2,1)S(1)} collective-permute-done((bf16[6,256,256]{2,1,0:T(8,128)(2,1)S(1)}, bf16[6,256,256]{2,1,0:T(8,128)(2,1)S(1)}, u32[]{:S(2)}, u32[]{:S(2)}) %collective-permute-start.5) | collective-permute-done | bytes 786464 | tf_op jit(solution)/shard_map/ppermute | solution.py:30
  54.4 3.9 %pairs_1.1 = (s16[784,256]{1,0:T(8,128)(2,1)S(1)}, f32[3]{0:T(128)S(1)}, s16[784,256]{1,0:T(8,128)(2,1)S(1)}, f32[3]{0:T(128)S(1)}) custom-call(s32[5,12]{1,0:T(8,128)S(1)} %copy-done.7, s32[5,12]{1,0:T(8,128)S(1)} %collective-permute-done.refs_2_.refs_1_.table_above, f32[3]{0:T(128)S(1)} %get-tuple-element.33.token.refs_4_, ...), custom_call_target="tpu_custom_call" | custom-call | flops 1 | bytes 1 | tf_op jit(solution)/shard_map/pairs_1/pallas_call | solution.py:346
  58.3 5.2 %collective-permute-start.9 = (s16[784,256]{1,0:T(8,128)(2,1)S(1)}, s16[784,256]{1,0:T(8,128)(2,1)S(1)}, u32[]{:S(2)}, u32[]{:S(2)}) collective-permute-start(s16[784,256]{1,0:T(8,128)(2,1)S(1)} %get-tuple-element.46), channel_id=1, source_target_pairs={{0,4},{4,8},{8,12},{12,0},{1,5},{5,9},{9,13},{13,1},{2,6},{6,10},{... | collective-permute-start | bytes 1204232 | tf_op jit(solution)/shard_map/ppermute | solution.py:35
  63.5 2.5 %settle_visit.1 = (f32[6,256,256]{2,1,0:T(8,128)}, f32[1]{0:T(128)}) custom-call(f32[3]{0:T(128)S(1)} %get-tuple-element.35.before.refs_0_, s16[784,256]{1,0:T(8,128)(2,1)S(1)} %get-tuple-element.36.refs_0_), custom_call_target="tpu_custom_call" | custom-call | flops 200000000 | bytes 1 | tf_op jit(solution)/shard_map/settle_visit/pallas_call | solution.py:414
  66.0 4.6 %pairs_3.1 = (s16[784,256]{1,0:T(8,128)(2,1)S(1)}, f32[3]{0:T(128)S(1)}) custom-call(s32[5,12]{1,0:T(8,128)S(1)} %copy-done.7, f32[1]{0:T(128)} %get-tuple-element.37.before, bf16[16,256,256]{2,1,0:T(8,128)(2,1)S(1)} %bitcast.7, f32[3]{0:T(128)S(1)} %get-tuple-element.35.before.refs_0_, bf16[6,256,256]{2,1,0:T(8,128)(2,1)S(1)} %collective-permute-done.6.refs_1_, ...), custom_call_target="tpu_custom_call" | custom-call | flops 1 | bytes 1 | tf_op jit(solution)/shard_map/pairs_3/pallas_call | solution.py:346
  70.6 0.1 collective-permute-start.10
  70.7 4.0 %pairs_0.1 = (s16[784,256]{1,0:T(8,128)(2,1)S(1)}, f32[3]{0:T(128)S(1)}) custom-call(s32[5,12]{1,0:T(8,128)S(1)} %copy-done.7, f32[3]{0:T(128)S(1)} %get-tuple-element.40.before.refs_0_.refs_5_, bf16[16,256,256]{2,1,0:T(8,128)(2,1)S(1)} %bitcast.8, f32[3]{0:T(128)S(1)} %get-tuple-element.40.before.refs_0_.refs_5_, ...), custom_call_target="tpu_custom_call" | custom-call | flops 1 | bytes 1 | tf_op jit(solution)/shard_map/pairs_0/pallas_call | solution.py:346
  74.7 8.7 %collective-permute-done.8.refs_1_ = s16[784,256]{1,0:T(8,128)(2,1)S(1)} collective-permute-done((s16[784,256]{1,0:T(8,128)(2,1)S(1)}, s16[784,256]{1,0:T(8,128)(2,1)S(1)}, u32[]{:S(2)}, u32[]{:S(2)}) %collective-permute-start.8) | collective-permute-done | bytes 401440 | tf_op jit(solution)/shard_map/ppermute | solution.py:35
  83.4 2.5 %settle_early.1 = (f32[6,256,256]{2,1,0:T(8,128)}, f32[1]{0:T(128)}) custom-call(f32[3]{0:T(128)S(1)} %get-tuple-element.41.before.refs_2_, s16[784,256]{1,0:T(8,128)(2,1)S(1)} %get-tuple-element.42.refs_0_, s16[784,256]{1,0:T(8,128)(2,1)S(1)} %collective-permute-done.8.refs_1_, ...), custom_call_target="tpu_custom_call", output_to_operand_aliasing={{0}: (3, {})} | custom-call | flops 200000000 | bytes 1 | tf_op jit(solution)/shard_map/settle_early/pallas_call | solution.py:414
  85.9 2.3 %settle_1.1 = (f32[6,256,256]{2,1,0:T(8,128)}, f32[1]{0:T(128)}) custom-call(f32[1]{0:T(128)} %get-tuple-element.45.before, s16[784,256]{1,0:T(8,128)(2,1)S(1)} %collective-permute-done.9.refs_0_, f32[6,256,256]{2,1,0:T(8,128)} %get-tuple-element.47.refs_1_), custom_call_target="tpu_custom_call", output_to_operand_aliasing={{0}: (2, {})} | custom-call | flops 200000000 | bytes 1 | tf_op jit(solution)/shard_map/settle_1/pallas_call | solution.py:414
  88.2 3.1 %settle_last.1 = (f32[6,256,256]{2,1,0:T(8,128)}, f32[12]{0:T(128)}, f32[1]{0:T(128)}) custom-call(f32[1]{0:T(128)} %get-tuple-element.48.before, s16[784,256]{1,0:T(8,128)(2,1)S(1)} %collective-permute-done.10.refs_0_, s32[5,12]{1,0:T(8,128)S(1)} %copy-done.7, f32[3]{0:T(128)S(1)} %get-tuple-element.41.before.refs_2_, ...), custom_call_target="tpu_custom_call", output_to_operand_aliasing={{0}: (7, {})} | custom-call | flops 200000000 | bytes 1 | tf_op jit(solution)/shard_map/settle_last/pallas_call | solution.py:414
  (17 shorter events, 0.0 us)
Async XLA Ops:
  2.1 8.3 %collective-permute-start.1 = (s32[5,12]{1,0:T(8,128)}, s32[5,12]{1,0:T(8,128)S(1)}, u32[]{:S(2)}, u32[]{:S(2)}) collective-permute-start(s32[5,12]{1,0:T(8,128)} %lanes.1.refs_0_.refs_1_.table), channel_id=1, source_target_pairs={{0,2},{1,3},{4,6},{5,7},{8,10},{9,11},{12,14},{13,15},{16,18},{17,... | collective-permute-start | bytes 728 | tf_op jit(solution)/shard_map/ppermute | solution.py:30
  7.0 5.0 %collective-permute-start = (s32[5,12]{1,0:T(8,128)}, s32[5,12]{1,0:T(8,128)S(1)}, u32[]{:S(2)}, u32[]{:S(2)}) collective-permute-start(s32[5,12]{1,0:T(8,128)} %lanes.1.refs_0_.refs_1_.table), channel_id=1, source_target_pairs={{0,4},{4,8},{8,12},{1,5},{5,9},{9,13},{2,6},{6,10},{10,14},{3,7},{... | collective-permute-start | bytes 728 | tf_op jit(solution)/shard_map/ppermute | solution.py:30
  12.0 1.6 %copy-start = (bf16[1,1,16,256,256]{4,3,2,1,0:T(8,128)(2,1)S(1)}, bf16[1,1,16,256,256]{4,3,2,1,0:T(8,128)(2,1)}, u32[]{:S(2)}) copy-start(bf16[1,1,16,256,256]{4,3,2,1,0:T(8,128)(2,1)} %param.7) | copy-start | bytes 6291460
  13.6 0.7 copy-start.6
  14.3 15.7 %copy-start.1 = (bf16[1,1,16,256,256]{4,3,2,1,0:T(8,128)(2,1)S(1)}, bf16[1,1,16,256,256]{4,3,2,1,0:T(8,128)(2,1)}, u32[]{:S(2)}) copy-start(bf16[1,1,16,256,256]{4,3,2,1,0:T(8,128)(2,1)} %param.7) | copy-start | bytes 6291460
  15.6 11.9 %collective-permute-start.2 = (bf16[3,256,256]{2,1,0:T(8,128)(2,1)S(1)}, bf16[3,256,256]{2,1,0:T(8,128)(2,1)S(1)}, u32[]{:S(2)}, u32[]{:S(2)}) collective-permute-start(bf16[3,256,256]{2,1,0:T(8,128)(2,1)S(1)} %get-tuple-element.29), channel_id=1, source_target_pairs={{4,0},{8,4},{12,8},{5,1},{9,5},{13,9},{6,2},{10,6},{14,10},{7,3},{... | collective-permute-start | bytes 1179656 | tf_op jit(solution)/shard_map/ppermute | solution.py:30
  16.9 11.6 %collective-permute-start.3 = (bf16[3,256,256]{2,1,0:T(8,128)(2,1)S(1)}, bf16[3,256,256]{2,1,0:T(8,128)(2,1)S(1)}, u32[]{:S(2)}, u32[]{:S(2)}) collective-permute-start(bf16[3,256,256]{2,1,0:T(8,128)(2,1)S(1)} %get-tuple-element.30), channel_id=1, source_target_pairs={{2,0},{3,1},{6,4},{7,5},{10,8},{11,9},{14,12},{15,13},{18,16},{19,... | collective-permute-start | bytes 1179656 | tf_op jit(solution)/shard_map/ppermute | solution.py:30
  18.2 11.7 %collective-permute-start.4 = (bf16[3,256,256]{2,1,0:T(8,128)(2,1)S(1)}, bf16[3,256,256]{2,1,0:T(8,128)(2,1)S(1)}, u32[]{:S(2)}, u32[]{:S(2)}) collective-permute-start(bf16[3,256,256]{2,1,0:T(8,128)(2,1)S(1)} %get-tuple-element.31), channel_id=1, source_target_pairs={{0,4},{4,8},{8,12},{1,5},{5,9},{9,13},{2,6},{6,10},{10,14},{3,7},{... | collective-permute-start | bytes 1179656 | tf_op jit(solution)/shard_map/ppermute | solution.py:30
  30.0 5.9 %copy-start.2 = (bf16[256,256]{1,0:T(8,128)(2,1)S(1)}, bf16[256,256]{1,0:T(8,128)(2,1)}, u32[]{:S(2)}) copy-start(bf16[256,256]{1,0:T(8,128)(2,1)} %constant.11.clone.refs_6_.sl) | copy-start | bytes 393220
  30.0 5.9 %copy-start.3 = (bf16[256,256]{1,0:T(8,128)(2,1)S(1)}, bf16[256,256]{1,0:T(8,128)(2,1)}, u32[]{:S(2)}) copy-start(bf16[256,256]{1,0:T(8,128)(2,1)} %constant.10.clone.refs_5_.sh) | copy-start | bytes 393220
  30.0 5.9 %copy-start.4 = (bf16[256,256]{1,0:T(8,128)(2,1)S(1)}, bf16[256,256]{1,0:T(8,128)(2,1)}, u32[]{:S(2)}) copy-start(bf16[256,256]{1,0:T(8,128)(2,1)} %constant.9.clone.refs_4_.tl) | copy-start | bytes 393220
  30.0 5.9 %copy-start.5 = (bf16[256,256]{1,0:T(8,128)(2,1)S(1)}, bf16[256,256]{1,0:T(8,128)(2,1)}, u32[]{:S(2)}) copy-start(bf16[256,256]{1,0:T(8,128)(2,1)} %constant.8.clone.refs_3_.th) | copy-start | bytes 393220
  30.0 5.9 %copy-start.7 = (s32[5,12]{1,0:T(8,128)S(1)}, s32[5,12]{1,0:T(8,128)}, u32[]{:S(2)}) copy-start(s32[5,12]{1,0:T(8,128)} %lanes.1.refs_0_.refs_1_.table) | copy-start | bytes 724
  32.0 22.4 %collective-permute-start.5 = (bf16[6,256,256]{2,1,0:T(8,128)(2,1)S(1)}, bf16[6,256,256]{2,1,0:T(8,128)(2,1)S(1)}, u32[]{:S(2)}, u32[]{:S(2)}) collective-permute-start(bf16[6,256,256]{2,1,0:T(8,128)(2,1)S(1)} %get-tuple-element.34), channel_id=1, source_target_pairs={{2,0},{3,1},{6,4},{7,5},{10,8},{11,9},{14,12},{15,13},{18,16},{19,... | collective-permute-start | bytes 2359304 | tf_op jit(solution)/shard_map/ppermute | solution.py:30
  33.3 32.7 %collective-permute-start.6 = (bf16[6,256,256]{2,1,0:T(8,128)(2,1)S(1)}, bf16[6,256,256]{2,1,0:T(8,128)(2,1)S(1)}, u32[]{:S(2)}, u32[]{:S(2)}) collective-permute-start(bf16[6,256,256]{2,1,0:T(8,128)(2,1)S(1)} %get-tuple-element.38), channel_id=1, source_target_pairs={{4,0},{8,4},{12,8},{5,1},{9,5},{13,9},{6,2},{10,6},{14,10},{7,3},{... | collective-permute-start | bytes 2359304 | tf_op jit(solution)/shard_map/ppermute | solution.py:30
  34.6 31.4 %collective-permute-start.7 = (bf16[3,256,256]{2,1,0:T(8,128)(2,1)S(1)}, bf16[3,256,256]{2,1,0:T(8,128)(2,1)S(1)}, u32[]{:S(2)}, u32[]{:S(2)}) collective-permute-start(bf16[3,256,256]{2,1,0:T(8,128)(2,1)S(1)} %get-tuple-element.39), channel_id=1, source_target_pairs={{2,0},{3,1},{6,4},{7,5},{10,8},{11,9},{14,12},{15,13},{18,16},{19,... | collective-permute-start | bytes 1179656 | tf_op jit(solution)/shard_map/ppermute | solution.py:30
  41.2 42.2 %collective-permute-start.8 = (s16[784,256]{1,0:T(8,128)(2,1)S(1)}, s16[784,256]{1,0:T(8,128)(2,1)S(1)}, u32[]{:S(2)}, u32[]{:S(2)}) collective-permute-start(s16[784,256]{1,0:T(8,128)(2,1)S(1)} %get-tuple-element.43), channel_id=1, source_target_pairs={{0,8},{4,12},{8,0},{12,4},{1,9},{5,13},{9,1},{13,5},{2,10},{6,14},... | collective-permute-start | bytes 1204232 | tf_op jit(solution)/shard_map/ppermute | solution.py:35
  58.3 27.6 %collective-permute-start.9 = (s16[784,256]{1,0:T(8,128)(2,1)S(1)}, s16[784,256]{1,0:T(8,128)(2,1)S(1)}, u32[]{:S(2)}, u32[]{:S(2)}) collective-permute-start(s16[784,256]{1,0:T(8,128)(2,1)S(1)} %get-tuple-element.46), channel_id=1, source_target_pairs={{0,4},{4,8},{8,12},{12,0},{1,5},{5,9},{9,13},{13,1},{2,6},{6,10},{... | collective-permute-start | bytes 1204232 | tf_op jit(solution)/shard_map/ppermute | solution.py:35
  70.6 17.6 %collective-permute-start.10 = (s16[784,256]{1,0:T(8,128)(2,1)S(1)}, s16[784,256]{1,0:T(8,128)(2,1)S(1)}, u32[]{:S(2)}, u32[]{:S(2)}) collective-permute-start(s16[784,256]{1,0:T(8,128)(2,1)S(1)} %get-tuple-element.49), channel_id=1, source_target_pairs={{0,12},{4,0},{8,4},{12,8},{1,13},{5,1},{9,5},{13,9},{2,14},{6,2},{... | collective-permute-start | bytes 1204232 | tf_op jit(solution)/shard_map/ppermute | solution.py:35

commit v3 on v2

--- a/solution.py
+++ b/solution.py
@@ -13,6 +13,8 @@
 TOP = 32700.0
 STEPS = 8.0
 HEAD = 16
+LANES = 4_000_000_000
+FIRST = 35_000_000_000
 SETTLE = 200_000_000
 HALF = 16384.0
 TINY = 1e-28
@@ -136,7 +138,8 @@
     count = len(lanes_of)
     tables, patches = refs[1 : count + 1], refs[count + 1]
     *sent, token = refs[-count - 1 :]
-    token[0] = 0
+    for at in np.ndindex(*token.shape):
+        token[at] = refs[0][at]
     for table, wanted, out in zip(tables, lanes_of, sent):
         for i, (field, lane) in enumerate(wanted):
             out[i] = patches[table[field, lane]]
@@ -166,7 +169,7 @@
         codes[j * length : (j + 1) * length] = whole.astype(jnp.int16)
         head = jnp.where(cols == j, step.astype(jnp.int32), head)
         head = jnp.where(cols == per + j, places[j], head)
-    codes[per * length :] = head.astype(jnp.int16)
+    codes[per * length : per * length + HEAD] = head.astype(jnp.int16)
 
 
 def guest_head(guests, length):
@@ -212,7 +215,7 @@
     kinds = [table[0, lane] for lane in lanes]
     for j in range(per):
         peaks[j] = 0.0
-    codes[per * codes.shape[-1] :] = guest_head(guests, codes.shape[-1]).astype(jnp.int16)
+    codes[per * codes.shape[-1] : per * codes.shape[-1] + HEAD] = guest_head(guests, codes.shape[-1]).astype(jnp.int16)
     wanted = [k >= 0 if live_kind is None else k == live_kind for k in kinds]
 
     @pl.when(any_of(wanted))
@@ -227,18 +230,13 @@
         correlate(firsts, seconds, places, guests, th, tl, sh, sl, codes, peaks)
 
 
-def near_kernel(
-    lanes, table, table_above, token, own, up, later, th, tl, sh, sl, codes, peaks, visit_codes, visit_peaks
-):
-    pair_kernel(
-        lanes, 0, 0, 1, False, table, token, own, None, None, later, th, tl, sh, sl, codes, peaks
-    )
+def visit_kernel(lanes, table_above, token, own, up, th, tl, sh, sl, _, codes, peaks):
     per = len(lanes)
+    length = codes.shape[-1]
     row = lax.axis_index("tile")
     for j in range(per):
-        visit_peaks[j] = 0.0
-    length = codes.shape[-1]
-    visit_codes[per * length :] = jnp.zeros((HEAD, length), jnp.int32).astype(jnp.int16)
+        peaks[j] = 0.0
+    codes[per * length : per * length + HEAD] = jnp.zeros((HEAD, length), jnp.int32).astype(jnp.int16)
     kinds = [table_above[0, lane] for lane in lanes]
 
     @pl.when((row > 0) & any_of([kind == 0 for kind in kinds]))
@@ -248,9 +246,7 @@
         places = [
             jnp.where(kind == 0, table_above[3, lane] + 1, 0) for kind, lane in zip(kinds, lanes)
         ]
-        correlate(
-            firsts, seconds, places, None, th, tl, sh, sl, visit_codes, visit_peaks
-        )
+        correlate(firsts, seconds, places, None, th, tl, sh, sl, codes, peaks)
 
 
 def settle_kernel(per, count, blank, before, *refs):
@@ -272,7 +268,7 @@
     cols = lax.broadcasted_iota(jnp.int32, (HEAD, length), 1)
     wanted, copies = [], []
     for i, coded in enumerate(codes):
-        head = coded[per * length :].astype(jnp.int32)
+        head = coded[per * length : per * length + HEAD].astype(jnp.int32)
         for j in range(per):
             k = i * per + j
             place = jnp.max(jnp.where(cols == per + j, head, 0))
@@ -285,7 +281,7 @@
 
             @pl.when(wanted[k])
             def _():
-                head = coded[per * length :].astype(jnp.int32)
+                head = coded[per * length : per * length + HEAD].astype(jnp.int32)
                 step = jnp.where(cols == j, head, -(1 << 15))[:1].astype(jnp.float32)
                 scale = jnp.exp2(jnp.max(step, axis=1, keepdims=True) * (1.0 / STEPS))
                 value = coded[j * length : (j + 1) * length].astype(jnp.int32).astype(jnp.float32)
@@ -303,7 +299,7 @@
     codes, table, home_peaks = refs[:count], refs[count], refs[count + 1 : count + 1 + tiles]
     surfaces, peaks, token, room, sems = refs[-5:]
     settle_kernel(per, count, False, before, *codes, surfaces, token, room, sems)
-    head = codes[-1][per * surfaces.shape[-1] :].astype(jnp.int32)
+    head = codes[-1][per * surfaces.shape[-1] : per * surfaces.shape[-1] + HEAD].astype(jnp.int32)
     back_peaks = [guest_peak(head, per, j) for j in range(per)]
     for k in range(peaks.shape[0]):
         peaks[k] = 0.0
@@ -336,21 +332,21 @@
     per = (slots + tiles - 1) // tiles
     up_one = tiles - 1
     far = sorted(range(2, up_one), key=lambda d: -min(d, tiles - d))
-    groups_below = [far, [up_one, 0]]
-    groups_later = [far, [1, up_one], [0]]
+    groups_below = [far + [up_one], [0]]
+    groups_later = [far, [1], [up_one], [0]]
 
     def lanes_at(d):
         return [d * per + j for j in range(per)]
 
-    def call(kernel, name, outs, *operands, last=()):
+    def call(kernel, name, outs, *operands, last=(), flops=SETTLE):
         return pl.pallas_call(
             kernel,
             out_shape=outs,
             in_specs=[VMEM if o.dtype in (own.dtype, jnp.int16) else SMEM for o in operands]
             + [ANY] * len(last),
-            out_specs=jax.tree.map(lambda o: SMEM if len(o.shape) == 1 else VMEM, outs),
+            out_specs=jax.tree.map(lambda o: SMEM if len(o.shape) == 1 or o.dtype == jnp.int32 else VMEM, outs),
             compiler_params=params(),
-            cost_estimate=cost(),
+            cost_estimate=cost(flops),
             name=name,
         )(*operands, *last)
 
@@ -361,7 +357,7 @@
         *sent, token = call(
             functools.partial(gather_kernel, lists),
             name,
-            outs + (SDS((1,), jnp.int32),),
+            outs + (SDS(token.shape, token.dtype),),
             token,
             *tables,
             own,
@@ -374,32 +370,30 @@
         out_shape=SDS((5, tiles * per), jnp.int32),
         in_specs=[SMEM, SMEM],
         out_specs=SMEM,
+        cost_estimate=cost(LANES),
         name="lanes",
     )(pair_lists, move_plan)
     table_above = shifted(table, "tile", 1)
-    table_before = shifted(table, "sect", 1)
-    (first_up, below_0, later_0), token = picked(
-        "gather_first",
+    (below_0,), same_table = picked("gather_below", table, [(table_above, 2, groups_below[0])])
+    below_0 = shifted(below_0, "tile", -1)
+    table_before = shifted(same_table, "sect", 1)
+    (first_up, below_1, later_0), token = picked(
+        "gather_later",
         table,
-        [(table, 1, [1]), (table_above, 2, groups_below[0]), (table_before, 2, groups_later[0])],
-    )
-    up = shifted(first_up, "tile", 1)
-    below_0, later_0 = shifted(below_0, "tile", -1), shifted(later_0, "sect", -1)
-    (below_1, later_1, later_2), token = picked(
-        "gather_last",
-        token,
-        [(table_above, 2, groups_below[1])] + [(table_before, 2, g) for g in groups_later[1:]],
-        below_0,
-        later_0,
-        up,
-    )
+        [(table, 1, [1]), (table_above, 2, groups_below[1]), (table_before, 2, groups_later[0])],
+    )
+    up, later_0 = shifted(first_up, "tile", 1), shifted(later_0, "sect", -1)
     below = [below_0, shifted(below_1, "tile", -1)]
+    (later_1, later_2), token = picked(
+        "gather_next", token, [(table_before, 2, g) for g in groups_later[1:3]], later_0, up
+    )
     later = [later_0, shifted(later_1, "sect", -1), shifted(later_2, "sect", -1)]
 
     high, low = packed_table(length)
     tables = [jnp.asarray(t) for t in (high, low, high.T.copy(), low.T.copy())]
     result = (SDS((per * length + HEAD, length), jnp.int16), SDS((per,), jnp.float32))
 
+    longer = (SDS((per * length + 2 * HEAD, length), jnp.int16), result[1])
     works = slots // 2
     surfaces_kind, token_kind = SDS((works, length, length), jnp.float32), SDS((1,), jnp.float32)
     peaks_kind = SDS((slots,), jnp.float32)
@@ -428,18 +422,20 @@
 
     home_peaks, moving = [None] * tiles, {}
 
-    def paired(d, before, guests, near, late, last=()):
+    def paired(d, before, guests, last=(), flops=SETTLE):
+        near = [i for i, g in enumerate(groups_below) if d in g or d == 1][0]
+        late = [i for i, g in enumerate(groups_later) if d in g][0]
         lane_codes, home_peaks[d] = call(
             functools.partial(
                 pair_kernel,
                 lanes_at(d),
-                groups_below[near].index(d) * per,
+                0 if d == 1 else groups_below[near].index(d) * per,
                 groups_later[late].index(d) * per,
-                None,
+                1 if d == 1 else None,
                 d == up_one,
             ),
             f"pairs_{d}",
-            result,
+            longer if d == 1 else result,
             table,
             before,
             own,
@@ -448,34 +444,34 @@
             later[late],
             *tables,
             last=last,
+            flops=flops,
         )
         moving[d] = lane_codes if d == 0 else rotated(lane_codes, "tile", d)
         return home_peaks[d]
 
     for d in far:
-        token = paired(d, token, token, 0, 0)
-    lane_codes, home_peaks[1], visit_codes, guests = call(
-        functools.partial(near_kernel, lanes_at(1)),
-        "pairs_1",
-        result + result,
-        table,
+        token = paired(d, token, token, flops=FIRST)
+    (later_3,), _ = picked("gather_home", token, [(table_before, 2, groups_later[3])])
+    later.append(shifted(later_3, "sect", -1))
+    visit_codes, guests = call(
+        functools.partial(visit_kernel, lanes_at(1)),
+        "visit",
+        result,
         table_above,
         token,
         own,
         up,
-        later[1],
         *tables,
-    )
-    moving[1] = rotated(lane_codes, "tile", 1)
+        last=[below[1]],
+    )
     surfaces, before = settled("settle_visit", [visit_codes], guests)
-    before = paired(up_one, before, guests, 1, 1, last=[later[2]])
-    before = paired(0, before, before, 1, 2)
+    before = paired(1, before, before)
+    before = paired(up_one, before, guests)
+    before = paired(0, before, before)
     early = [moving[d] for d in [0] + far]
     surfaces, before = settled("settle_early", early, before, surfaces)
-    surfaces, before = settled("settle_1", [moving[1]], before, surfaces)
-    surfaces, peaks, _ = settled(
-        "settle_last", [moving[up_one]], before, surfaces, table, home_peaks
-    )
+    last = [moving[1], moving[up_one]]
+    surfaces, peaks, _ = settled("settle_last", last, before, surfaces, table, home_peaks)
     return surfaces[None, None], peaks[None, None]
 
 

time: 91.4 us -> 80.9 us (0.89); the launches traced: 91.4 us -> 80 us
  waiting for transfers between devices: 25.7 us -> 14.7 us
  starting transfers between devices: 29.5 us -> 32.6 us
  Pallas kernels: 32.9 us -> 30.9 us
  local copies, waits for them, and re-layouts: 2.3 us -> 0.71 us
    ppermute x8 -> x9, waiting for transfers between devices: 17 us -> 7.87 us  [shifted(): return lax.ppermute(value, axis, pairs)]
    pallas_call x4 -> x3, Pallas kernels: 10.3 us -> 8.14 us  [settled(): pl.pallas_call(kernel, out_shape=(surfaces_kind,) + ((peaks_kind,) if ext...]
    ppermute x3, waiting for transfers between devices: 8.72 us -> 6.82 us  [rotated(): lax.ppermute(value, axis, [(i, (i + steps) % count) for i in range(count)])]
    ppermute x3, starting transfers between devices: 9.88 us -> 11.6 us  [rotated(): lax.ppermute(value, axis, [(i, (i + steps) % count) for i in range(count)])]
    unnamed x16 -> x14, local copies, waits for them, and re-layouts: 2.3 us -> 0.71 us
    ppermute x8 -> x9, starting transfers between devices: 19.6 us -> 21 us  [shifted(): return lax.ppermute(value, axis, pairs)]
    pallas_call x6 -> x9, Pallas kernels: 21.1 us -> 21.1 us  [call(): pl.pallas_call(kernel, out_shape=outs, in_specs=[VMEM if o.dtype in (own....]
  transfers between devices with their start and end apart: 11 -> 12, of which waited for: 6 -> 6; matrix products, arithmetic and copies ran while one was open for 0% -> 0% of each run, Pallas kernels for 27% -> 31%
where the time goes in v3:
time: 80.9 us; the launch traced here: 80 us
  starting transfers between devices  32.6 us (40%)
  Pallas kernels  30.9 us (38%)
  waiting for transfers between devices  14.7 us (18%)
  between operations  1.07 us (1%)
    pallas_call x9, Pallas kernels, call(): pl.pallas_call(kernel, out_shape=outs, in_specs=[VMEM if o.dtype in (own....  21.1 us
    ppermute x9, starting transfers between devices, shifted(): return lax.ppermute(value, axis, pairs)  21 us
    ppermute x3, starting transfers between devices, rotated(): lax.ppermute(value, axis, [(i, (i + steps) % count) for i in range(count)])  11.6 us
    pallas_call x3, Pallas kernels, settled(): pl.pallas_call(kernel, out_shape=(surfaces_kind,) + ((peaks_kind,) if ext...  8.14 us
    ppermute x9, waiting for transfers between devices, shifted(): return lax.ppermute(value, axis, pairs)  7.87 us
    ppermute x3, waiting for transfers between devices, rotated(): lax.ppermute(value, axis, [(i, (i + steps) % count) for i in range(count)])  6.82 us
    pallas_call x1, Pallas kernels, body(): pl.pallas_call(functools.partial(lanes_kernel, tiles, per), out_shape=SDS...  1.64 us
  transfers between devices with their start and end apart: 12, of which 6 were waited for; matrix products, arithmetic and copies ran while one was open for 0% of the time, Pallas kernels for 31%

profile of v3, /device:TPU:0, one launch (start us, length us, event | category | flops | bytes accessed | tf_op | source)
XLA Modules:
  0.0 80.0 jit_solution(2515679919188134258)
XLA Ops:
  0.6 1.6 %lanes.1.refs_0_.refs_1_.table.refs_2_ = s32[5,12]{1,0:T(8,128)} custom-call(s32[3,1,1,12]{3,2,1,0:T(1,128)} %pairs.1, s32[2,1,1,12]{3,2,1,0:T(1,128)} %plan.1), custom_call_target="tpu_custom_call" | custom-call | flops 4000000000 | bytes 1 | tf_op jit(solution)/shard_map/lanes/pallas_call | solution.py:368
  2.3 4.9 %collective-permute-start = (s32[5,12]{1,0:T(8,128)}, s32[5,12]{1,0:T(8,128)S(1)}, u32[]{:S(2)}, u32[]{:S(2)}) collective-permute-start(s32[5,12]{1,0:T(8,128)} %lanes.1.refs_0_.refs_1_.table.refs_2_), channel_id=1, source_target_pairs={{0,4},{4,8},{8,12},{1,5},{5,9},{9,13},{2,6},{6,10},{10,14},{3,7},{... | collective-permute-start | bytes 728 | tf_op jit(solution)/shard_map/ppermute | solution.py:32
  7.2 1.5 %collective-permute-done.refs_1_.refs_2_.table_above = s32[5,12]{1,0:T(8,128)S(1)} collective-permute-done((s32[5,12]{1,0:T(8,128)}, s32[5,12]{1,0:T(8,128)S(1)}, u32[]{:S(2)}, u32[]{:S(2)}) %collective-permute-start) | collective-permute-done | bytes 272 | tf_op jit(solution)/shard_map/ppermute | solution.py:32
  8.8 0.7 copy-done.5
  9.4 1.4 %gather_below.1 = (bf16[6,256,256]{2,1,0:T(8,128)(2,1)S(1)}, s32[5,12]{1,0:T(8,128)S(1)}) custom-call(s32[5,12]{1,0:T(8,128)S(1)} %copy-done.5, s32[5,12]{1,0:T(8,128)S(1)} %collective-permute-done.refs_1_.refs_2_.table_above, bf16[16,256,256]{2,1,0:T(8,128)(2,1)S(1)} %bitcast.3), custom_call_target="tpu_custom_call" | custom-call | flops 200000000 | bytes 1 | tf_op jit(solution)/shard_map/gather_below/pallas_call | solution.py:342
  10.8 1.3 %collective-permute-start.4 = (bf16[6,256,256]{2,1,0:T(8,128)(2,1)S(1)}, bf16[6,256,256]{2,1,0:T(8,128)(2,1)S(1)}, u32[]{:S(2)}, u32[]{:S(2)}) collective-permute-start(bf16[6,256,256]{2,1,0:T(8,128)(2,1)S(1)} %get-tuple-element.33), channel_id=1, source_target_pairs={{4,0},{8,4},{12,8},{5,1},{9,5},{13,9},{6,2},{10,6},{14,10},{7,3},{... | collective-permute-start | bytes 2359304 | tf_op jit(solution)/shard_map/ppermute | solution.py:32
  12.1 3.4 %collective-permute-start.1 = (s32[5,12]{1,0:T(8,128)S(1)}, s32[5,12]{1,0:T(8,128)S(1)}, u32[]{:S(2)}, u32[]{:S(2)}) collective-permute-start(s32[5,12]{1,0:T(8,128)S(1)} %get-tuple-element.28), channel_id=1, source_target_pairs={{0,2},{1,3},{4,6},{5,7},{8,10},{9,11},{12,14},{13,15},{16,18},{17,... | collective-permute-start | bytes 728 | tf_op jit(solution)/shard_map/ppermute | solution.py:32
  15.5 1.3 %collective-permute-done.1.refs_3_.refs_1_.refs_2_ = s32[5,12]{1,0:T(8,128)S(1)} collective-permute-done((s32[5,12]{1,0:T(8,128)S(1)}, s32[5,12]{1,0:T(8,128)S(1)}, u32[]{:S(2)}, u32[]{:S(2)}) %collective-permute-start.1) | collective-permute-done | bytes 272 | tf_op jit(solution)/shard_map/ppermute | solution.py:32
  16.8 1.5 %gather_later.1 = (bf16[3,256,256]{2,1,0:T(8,128)(2,1)S(1)}, bf16[3,256,256]{2,1,0:T(8,128)(2,1)S(1)}, bf16[3,256,256]{2,1,0:T(8,128)(2,1)S(1)}, s32[5,12]{1,0:T(8,128)S(1)}) custom-call(s32[5,12]{1,0:T(8,128)S(1)} %copy-done.5, s32[5,12]{1,0:T(8,128)S(1)} %copy-done.5, s32[5,12]{1,0:T(8,128)S(1)} %collective-permute-done.refs_1_.refs_2_.table_above, ...), custom_call_target="tpu_custom_call" | custom-call | flops 200000000 | bytes 1 | tf_op jit(solution)/shard_map/gather_later/pallas_call | solution.py:342
  18.4 1.4 %collective-permute-start.2 = (bf16[3,256,256]{2,1,0:T(8,128)(2,1)S(1)}, bf16[3,256,256]{2,1,0:T(8,128)(2,1)S(1)}, u32[]{:S(2)}, u32[]{:S(2)}) collective-permute-start(bf16[3,256,256]{2,1,0:T(8,128)(2,1)S(1)} %get-tuple-element.30), channel_id=1, source_target_pairs={{2,0},{3,1},{6,4},{7,5},{10,8},{11,9},{14,12},{15,13},{18,16},{19,... | collective-permute-start | bytes 1179656 | tf_op jit(solution)/shard_map/ppermute | solution.py:32
  19.8 4.8 %collective-permute-start.3 = (bf16[3,256,256]{2,1,0:T(8,128)(2,1)S(1)}, bf16[3,256,256]{2,1,0:T(8,128)(2,1)S(1)}, u32[]{:S(2)}, u32[]{:S(2)}) collective-permute-start(bf16[3,256,256]{2,1,0:T(8,128)(2,1)S(1)} %get-tuple-element.31), channel_id=1, source_target_pairs={{0,4},{4,8},{8,12},{1,5},{5,9},{9,13},{2,6},{6,10},{10,14},{3,7},{... | collective-permute-start | bytes 1179656 | tf_op jit(solution)/shard_map/ppermute | solution.py:32
  24.6 1.3 %collective-permute-start.5 = (bf16[3,256,256]{2,1,0:T(8,128)(2,1)S(1)}, bf16[3,256,256]{2,1,0:T(8,128)(2,1)S(1)}, u32[]{:S(2)}, u32[]{:S(2)}) collective-permute-start(bf16[3,256,256]{2,1,0:T(8,128)(2,1)S(1)} %get-tuple-element.35), channel_id=1, source_target_pairs={{4,0},{8,4},{12,8},{5,1},{9,5},{13,9},{6,2},{10,6},{14,10},{7,3},{... | collective-permute-start | bytes 1179656 | tf_op jit(solution)/shard_map/ppermute | solution.py:32
  25.9 3.6 %collective-permute-done.2.refs_4_.refs_2_ = bf16[3,256,256]{2,1,0:T(8,128)(2,1)S(1)} collective-permute-done((bf16[3,256,256]{2,1,0:T(8,128)(2,1)S(1)}, bf16[3,256,256]{2,1,0:T(8,128)(2,1)S(1)}, u32[]{:S(2)}, u32[]{:S(2)}) %collective-permute-start.2) | collective-permute-done | bytes 393248 | tf_op jit(solution)/shard_map/ppermute | solution.py:32
  29.5 1.4 %collective-permute-done.3.refs_5_.up = bf16[3,256,256]{2,1,0:T(8,128)(2,1)S(1)} collective-permute-done((bf16[3,256,256]{2,1,0:T(8,128)(2,1)S(1)}, bf16[3,256,256]{2,1,0:T(8,128)(2,1)S(1)}, u32[]{:S(2)}, u32[]{:S(2)}) %collective-permute-start.3) | collective-permute-done | bytes 393248 | tf_op jit(solution)/shard_map/ppermute | solution.py:32
  31.0 1.4 %gather_next.1 = (bf16[3,256,256]{2,1,0:T(8,128)(2,1)S(1)}, bf16[3,256,256]{2,1,0:T(8,128)(2,1)S(1)}, s32[5,12]{1,0:T(8,128)S(1)}) custom-call(s32[5,12]{1,0:T(8,128)S(1)} %get-tuple-element.29.refs_0_, s32[5,12]{1,0:T(8,128)S(1)} %collective-permute-done.1.refs_3_.refs_1_.refs_2_, s32[5,12]{1,0:T(8,128)S(1)} %collective-permute-done.1.refs_3_.refs_1_.refs_2_, ...), custom_call_target="tpu_custom_call" | custom-call | flops 200000000 | bytes 1 | tf_op jit(solution)/shard_map/gather_next/pallas_call | solution.py:342
  32.4 1.3 %collective-permute-start.6 = (bf16[3,256,256]{2,1,0:T(8,128)(2,1)S(1)}, bf16[3,256,256]{2,1,0:T(8,128)(2,1)S(1)}, u32[]{:S(2)}, u32[]{:S(2)}) collective-permute-start(bf16[3,256,256]{2,1,0:T(8,128)(2,1)S(1)} %get-tuple-element.39), channel_id=1, source_target_pairs={{2,0},{3,1},{6,4},{7,5},{10,8},{11,9},{14,12},{15,13},{18,16},{19,... | collective-permute-start | bytes 1179656 | tf_op jit(solution)/shard_map/ppermute | solution.py:32
  33.7 1.3 %collective-permute-start.7 = (bf16[3,256,256]{2,1,0:T(8,128)(2,1)S(1)}, bf16[3,256,256]{2,1,0:T(8,128)(2,1)S(1)}, u32[]{:S(2)}, u32[]{:S(2)}) collective-permute-start(bf16[3,256,256]{2,1,0:T(8,128)(2,1)S(1)} %get-tuple-element.41), channel_id=1, source_target_pairs={{2,0},{3,1},{6,4},{7,5},{10,8},{11,9},{14,12},{15,13},{18,16},{19,... | collective-permute-start | bytes 1179656 | tf_op jit(solution)/shard_map/ppermute | solution.py:32
  35.1 4.0 %pairs_2.1 = (s16[784,256]{1,0:T(8,128)(2,1)S(1)}, f32[3]{0:T(128)S(1)}) custom-call(s32[5,12]{1,0:T(8,128)S(1)} %copy-done.5, s32[5,12]{1,0:T(8,128)S(1)} %get-tuple-element.32.before.refs_0_, bf16[16,256,256]{2,1,0:T(8,128)(2,1)S(1)} %bitcast.6, s32[5,12]{1,0:T(8,128)S(1)} %get-tuple-element.32.before.refs_0_, ...), custom_call_target="tpu_custom_call" | custom-call | flops 35000000512 | bytes 1 | tf_op jit(solution)/shard_map/pairs_2/pallas_call | solution.py:342
  39.1 1.1 %gather_home.1 = (bf16[3,256,256]{2,1,0:T(8,128)(2,1)S(1)}, f32[3]{0:T(128)}) custom-call(f32[3]{0:T(128)S(1)} %get-tuple-element.34.token.refs_0_.refs_5_, s32[5,12]{1,0:T(8,128)S(1)} %collective-permute-done.1.refs_3_.refs_1_.refs_2_, bf16[16,256,256]{2,1,0:T(8,128)(2,1)S(1)} %bitcast.7), custom_call_target="tpu_custom_call" | custom-call | flops 200000000 | bytes 1 | tf_op jit(solution)/shard_map/gather_home/pallas_call | solution.py:342
  40.2 1.3 %collective-permute-start.8 = (bf16[3,256,256]{2,1,0:T(8,128)(2,1)S(1)}, bf16[3,256,256]{2,1,0:T(8,128)(2,1)S(1)}, u32[]{:S(2)}, u32[]{:S(2)}) collective-permute-start(bf16[3,256,256]{2,1,0:T(8,128)(2,1)S(1)} %get-tuple-element.43), channel_id=1, source_target_pairs={{2,0},{3,1},{6,4},{7,5},{10,8},{11,9},{14,12},{15,13},{18,16},{19,... | collective-permute-start | bytes 1179656 | tf_op jit(solution)/shard_map/ppermute | solution.py:32
  41.5 3.7 %collective-permute-start.9 = (s16[784,256]{1,0:T(8,128)(2,1)S(1)}, s16[784,256]{1,0:T(8,128)(2,1)S(1)}, u32[]{:S(2)}, u32[]{:S(2)}) collective-permute-start(s16[784,256]{1,0:T(8,128)(2,1)S(1)} %get-tuple-element.46), channel_id=1, source_target_pairs={{0,8},{4,12},{8,0},{12,4},{1,9},{5,13},{9,1},{13,5},{2,10},{6,14},... | collective-permute-start | bytes 1204232 | tf_op jit(solution)/shard_map/ppermute | solution.py:37
  45.2 1.2 %visit.1 = (s16[784,256]{1,0:T(8,128)(2,1)S(1)}, f32[3]{0:T(128)S(1)}) custom-call(s32[5,12]{1,0:T(8,128)S(1)} %collective-permute-done.refs_1_.refs_2_.table_above, f32[3]{0:T(128)S(1)} %get-tuple-element.34.token.refs_0_.refs_5_, bf16[16,256,256]{2,1,0:T(8,128)(2,1)S(1)} %bitcast.8, bf16[3,256,256]{2,1,0:T(8,128)(2,1)S(1)} %collective-permute-done.3.refs_5_.up, ...), custom_call_target="tpu_custom_call" | custom-call | flops 200000000 | bytes 1 | tf_op jit(solution)/shard_map/visit/pallas_call | solution.py:342
  46.4 2.5 %settle_visit.1 = (f32[6,256,256]{2,1,0:T(8,128)}, f32[1]{0:T(128)}) custom-call(f32[3]{0:T(128)S(1)} %get-tuple-element.36.before.refs_0_, s16[784,256]{1,0:T(8,128)(2,1)S(1)} %get-tuple-element.37.refs_0_), custom_call_target="tpu_custom_call" | custom-call | flops 200000000 | bytes 1 | tf_op jit(solution)/shard_map/settle_visit/pallas_call | solution.py:408
  49.0 2.5 %pairs_1.1 = (s16[800,256]{1,0:T(8,128)(2,1)S(1)}, f32[3]{0:T(128)S(1)}) custom-call(s32[5,12]{1,0:T(8,128)S(1)} %copy-done.6, f32[1]{0:T(128)} %get-tuple-element.38.before.refs_0_, bf16[16,256,256]{2,1,0:T(8,128)(2,1)S(1)} %bitcast.9, f32[1]{0:T(128)} %get-tuple-element.38.before.refs_0_, bf16[6,256,256]{2,1,0:T(8,128)(2,1)S(1)} %collective-permute-done.4.refs_1_, ...), custom_call_target="tpu_custom_call" | custom-call | flops 200000000 | bytes 1 | tf_op jit(solution)/shard_map/pairs_1/pallas_call | solution.py:342
  51.5 7.8 %collective-permute-start.10 = (s16[800,256]{1,0:T(8,128)(2,1)S(1)}, s16[800,256]{1,0:T(8,128)(2,1)S(1)}, u32[]{:S(2)}, u32[]{:S(2)}) collective-permute-start(s16[800,256]{1,0:T(8,128)(2,1)S(1)} %get-tuple-element.49), channel_id=1, source_target_pairs={{0,4},{4,8},{8,12},{12,0},{1,5},{5,9},{9,13},{13,1},{2,6},{6,10},{... | collective-permute-start | bytes 1228808 | tf_op jit(solution)/shard_map/ppermute | solution.py:37
  59.3 3.9 %pairs_3.1 = (s16[784,256]{1,0:T(8,128)(2,1)S(1)}, f32[3]{0:T(128)S(1)}) custom-call(s32[5,12]{1,0:T(8,128)S(1)} %copy-done.6, f32[3]{0:T(128)S(1)} %get-tuple-element.40.before.refs_4_, bf16[16,256,256]{2,1,0:T(8,128)(2,1)S(1)} %bitcast.10, f32[3]{0:T(128)S(1)} %get-tuple-element.36.before.refs_0_, bf16[6,256,256]{2,1,0:T(8,128)(2,1)S(1)} %collective-permute-done.4.refs_1_, ...), custom_call_target="tpu_custom_call" | custom-call | flops 200000000 | bytes 1 | tf_op jit(solution)/shard_map/pairs_3/pallas_call | solution.py:342
  63.2 0.1 collective-permute-start.11
  63.3 4.1 %pairs_0.1 = (s16[784,256]{1,0:T(8,128)(2,1)S(1)}, f32[3]{0:T(128)S(1)}) custom-call(s32[5,12]{1,0:T(8,128)S(1)} %copy-done.6, f32[3]{0:T(128)S(1)} %get-tuple-element.42.before.refs_0_.refs_6_, bf16[16,256,256]{2,1,0:T(8,128)(2,1)S(1)} %bitcast.11, f32[3]{0:T(128)S(1)} %get-tuple-element.42.before.refs_0_.refs_6_, ...), custom_call_target="tpu_custom_call" | custom-call | flops 200000000 | bytes 1 | tf_op jit(solution)/shard_map/pairs_0/pallas_call | solution.py:342
  67.3 2.7 %collective-permute-done.9.refs_1_ = s16[784,256]{1,0:T(8,128)(2,1)S(1)} collective-permute-done((s16[784,256]{1,0:T(8,128)(2,1)S(1)}, s16[784,256]{1,0:T(8,128)(2,1)S(1)}, u32[]{:S(2)}, u32[]{:S(2)}) %collective-permute-start.9) | collective-permute-done | bytes 401440 | tf_op jit(solution)/shard_map/ppermute | solution.py:37
  70.1 2.4 %settle_early.1 = (f32[6,256,256]{2,1,0:T(8,128)}, f32[1]{0:T(128)}) custom-call(f32[3]{0:T(128)S(1)} %get-tuple-element.44.before.refs_3_, s16[784,256]{1,0:T(8,128)(2,1)S(1)} %get-tuple-element.45.refs_0_, s16[784,256]{1,0:T(8,128)(2,1)S(1)} %collective-permute-done.9.refs_1_, ...), custom_call_target="tpu_custom_call", output_to_operand_aliasing={{0}: (3, {})} | custom-call | flops 200000000 | bytes 1 | tf_op jit(solution)/shard_map/settle_early/pallas_call | solution.py:408
  72.5 4.1 %collective-permute-done.11.refs_1_ = s16[784,256]{1,0:T(8,128)(2,1)S(1)} collective-permute-done((s16[784,256]{1,0:T(8,128)(2,1)S(1)}, s16[784,256]{1,0:T(8,128)(2,1)S(1)}, u32[]{:S(2)}, u32[]{:S(2)}) %collective-permute-start.11) | collective-permute-done | bytes 401440 | tf_op jit(solution)/shard_map/ppermute | solution.py:37
  76.6 3.2 %settle_last.1 = (f32[6,256,256]{2,1,0:T(8,128)}, f32[12]{0:T(128)}, f32[1]{0:T(128)}) custom-call(f32[1]{0:T(128)} %get-tuple-element.48.before, s16[800,256]{1,0:T(8,128)(2,1)S(1)} %collective-permute-done.10.refs_0_, s16[784,256]{1,0:T(8,128)(2,1)S(1)} %collective-permute-done.11.refs_1_, s32[5,12]{1,0:T(8,128)S(1)} %copy-done.6, ...), custom_call_target="tpu_custom_call", output_to_operand_aliasing={{0}: (8, {})} | custom-call | flops 200000000 | bytes 1 | tf_op jit(solution)/shard_map/settle_last/pallas_call | solution.py:408
  (19 shorter events, 0.1 us)
Async XLA Ops:
  0.6 8.1 %copy-start = (bf16[1,1,16,256,256]{4,3,2,1,0:T(8,128)(2,1)S(1)}, bf16[1,1,16,256,256]{4,3,2,1,0:T(8,128)(2,1)}, u32[]{:S(2)}) copy-start(bf16[1,1,16,256,256]{4,3,2,1,0:T(8,128)(2,1)} %param.7) | copy-start | bytes 6291460
  2.3 6.5 %collective-permute-start = (s32[5,12]{1,0:T(8,128)}, s32[5,12]{1,0:T(8,128)S(1)}, u32[]{:S(2)}, u32[]{:S(2)}) collective-permute-start(s32[5,12]{1,0:T(8,128)} %lanes.1.refs_0_.refs_1_.table.refs_2_), channel_id=1, source_target_pairs={{0,4},{4,8},{8,12},{1,5},{5,9},{9,13},{2,6},{6,10},{10,14},{3,7},{... | collective-permute-start | bytes 728 | tf_op jit(solution)/shard_map/ppermute | solution.py:32
  8.7 0.7 copy-start.5
  10.8 24.2 %collective-permute-start.4 = (bf16[6,256,256]{2,1,0:T(8,128)(2,1)S(1)}, bf16[6,256,256]{2,1,0:T(8,128)(2,1)S(1)}, u32[]{:S(2)}, u32[]{:S(2)}) collective-permute-start(bf16[6,256,256]{2,1,0:T(8,128)(2,1)S(1)} %get-tuple-element.33), channel_id=1, source_target_pairs={{4,0},{8,4},{12,8},{5,1},{9,5},{13,9},{6,2},{10,6},{14,10},{7,3},{... | collective-permute-start | bytes 2359304 | tf_op jit(solution)/shard_map/ppermute | solution.py:32
  12.1 4.7 %collective-permute-start.1 = (s32[5,12]{1,0:T(8,128)S(1)}, s32[5,12]{1,0:T(8,128)S(1)}, u32[]{:S(2)}, u32[]{:S(2)}) collective-permute-start(s32[5,12]{1,0:T(8,128)S(1)} %get-tuple-element.28), channel_id=1, source_target_pairs={{0,2},{1,3},{4,6},{5,7},{8,10},{9,11},{12,14},{13,15},{16,18},{17,... | collective-permute-start | bytes 728 | tf_op jit(solution)/shard_map/ppermute | solution.py:32
  18.3 16.7 %copy-start.1 = (bf16[256,256]{1,0:T(8,128)(2,1)S(1)}, bf16[256,256]{1,0:T(8,128)(2,1)}, u32[]{:S(2)}) copy-start(bf16[256,256]{1,0:T(8,128)(2,1)} %constant.11.clone.refs_6_.sl) | copy-start | bytes 393220
  18.3 16.7 %copy-start.2 = (bf16[256,256]{1,0:T(8,128)(2,1)S(1)}, bf16[256,256]{1,0:T(8,128)(2,1)}, u32[]{:S(2)}) copy-start(bf16[256,256]{1,0:T(8,128)(2,1)} %constant.10.clone.refs_5_.sh) | copy-start | bytes 393220
  18.3 16.7 %copy-start.3 = (bf16[256,256]{1,0:T(8,128)(2,1)S(1)}, bf16[256,256]{1,0:T(8,128)(2,1)}, u32[]{:S(2)}) copy-start(bf16[256,256]{1,0:T(8,128)(2,1)} %constant.9.clone.refs_4_.tl) | copy-start | bytes 393220
  18.4 16.7 %copy-start.4 = (bf16[256,256]{1,0:T(8,128)(2,1)S(1)}, bf16[256,256]{1,0:T(8,128)(2,1)}, u32[]{:S(2)}) copy-start(bf16[256,256]{1,0:T(8,128)(2,1)} %constant.8.clone.refs_3_.th) | copy-start | bytes 393220
  18.4 11.2 %collective-permute-start.2 = (bf16[3,256,256]{2,1,0:T(8,128)(2,1)S(1)}, bf16[3,256,256]{2,1,0:T(8,128)(2,1)S(1)}, u32[]{:S(2)}, u32[]{:S(2)}) collective-permute-start(bf16[3,256,256]{2,1,0:T(8,128)(2,1)S(1)} %get-tuple-element.30), channel_id=1, source_target_pairs={{2,0},{3,1},{6,4},{7,5},{10,8},{11,9},{14,12},{15,13},{18,16},{19,... | collective-permute-start | bytes 1179656 | tf_op jit(solution)/shard_map/ppermute | solution.py:32
  19.8 11.2 %collective-permute-start.3 = (bf16[3,256,256]{2,1,0:T(8,128)(2,1)S(1)}, bf16[3,256,256]{2,1,0:T(8,128)(2,1)S(1)}, u32[]{:S(2)}, u32[]{:S(2)}) collective-permute-start(bf16[3,256,256]{2,1,0:T(8,128)(2,1)S(1)} %get-tuple-element.31), channel_id=1, source_target_pairs={{0,4},{4,8},{8,12},{1,5},{5,9},{9,13},{2,6},{6,10},{10,14},{3,7},{... | collective-permute-start | bytes 1179656 | tf_op jit(solution)/shard_map/ppermute | solution.py:32
  24.6 20.6 %collective-permute-start.5 = (bf16[3,256,256]{2,1,0:T(8,128)(2,1)S(1)}, bf16[3,256,256]{2,1,0:T(8,128)(2,1)S(1)}, u32[]{:S(2)}, u32[]{:S(2)}) collective-permute-start(bf16[3,256,256]{2,1,0:T(8,128)(2,1)S(1)} %get-tuple-element.35), channel_id=1, source_target_pairs={{4,0},{8,4},{12,8},{5,1},{9,5},{13,9},{6,2},{10,6},{14,10},{7,3},{... | collective-permute-start | bytes 1179656 | tf_op jit(solution)/shard_map/ppermute | solution.py:32
  32.4 16.6 %collective-permute-start.6 = (bf16[3,256,256]{2,1,0:T(8,128)(2,1)S(1)}, bf16[3,256,256]{2,1,0:T(8,128)(2,1)S(1)}, u32[]{:S(2)}, u32[]{:S(2)}) collective-permute-start(bf16[3,256,256]{2,1,0:T(8,128)(2,1)S(1)} %get-tuple-element.39), channel_id=1, source_target_pairs={{2,0},{3,1},{6,4},{7,5},{10,8},{11,9},{14,12},{15,13},{18,16},{19,... | collective-permute-start | bytes 1179656 | tf_op jit(solution)/shard_map/ppermute | solution.py:32
  33.7 25.6 %collective-permute-start.7 = (bf16[3,256,256]{2,1,0:T(8,128)(2,1)S(1)}, bf16[3,256,256]{2,1,0:T(8,128)(2,1)S(1)}, u32[]{:S(2)}, u32[]{:S(2)}) collective-permute-start(bf16[3,256,256]{2,1,0:T(8,128)(2,1)S(1)} %get-tuple-element.41), channel_id=1, source_target_pairs={{2,0},{3,1},{6,4},{7,5},{10,8},{11,9},{14,12},{15,13},{18,16},{19,... | collective-permute-start | bytes 1179656 | tf_op jit(solution)/shard_map/ppermute | solution.py:32
  40.2 23.1 %collective-permute-start.8 = (bf16[3,256,256]{2,1,0:T(8,128)(2,1)S(1)}, bf16[3,256,256]{2,1,0:T(8,128)(2,1)S(1)}, u32[]{:S(2)}, u32[]{:S(2)}) collective-permute-start(bf16[3,256,256]{2,1,0:T(8,128)(2,1)S(1)} %get-tuple-element.43), channel_id=1, source_target_pairs={{2,0},{3,1},{6,4},{7,5},{10,8},{11,9},{14,12},{15,13},{18,16},{19,... | collective-permute-start | bytes 1179656 | tf_op jit(solution)/shard_map/ppermute | solution.py:32
  41.5 7.5 %copy-start.6 = (s32[5,12]{1,0:T(8,128)S(1)}, s32[5,12]{1,0:T(8,128)}, u32[]{:S(2)}) copy-start(s32[5,12]{1,0:T(8,128)} %lanes.1.refs_0_.refs_1_.table.refs_2_) | copy-start | bytes 724
  41.5 28.6 %collective-permute-start.9 = (s16[784,256]{1,0:T(8,128)(2,1)S(1)}, s16[784,256]{1,0:T(8,128)(2,1)S(1)}, u32[]{:S(2)}, u32[]{:S(2)}) collective-permute-start(s16[784,256]{1,0:T(8,128)(2,1)S(1)} %get-tuple-element.46), channel_id=1, source_target_pairs={{0,8},{4,12},{8,0},{12,4},{1,9},{5,13},{9,1},{13,5},{2,10},{6,14},... | collective-permute-start | bytes 1204232 | tf_op jit(solution)/shard_map/ppermute | solution.py:37
  51.5 25.1 %collective-permute-start.10 = (s16[800,256]{1,0:T(8,128)(2,1)S(1)}, s16[800,256]{1,0:T(8,128)(2,1)S(1)}, u32[]{:S(2)}, u32[]{:S(2)}) collective-permute-start(s16[800,256]{1,0:T(8,128)(2,1)S(1)} %get-tuple-element.49), channel_id=1, source_target_pairs={{0,4},{4,8},{8,12},{12,0},{1,5},{5,9},{9,13},{13,1},{2,6},{6,10},{... | collective-permute-start | bytes 1228808 | tf_op jit(solution)/shard_map/ppermute | solution.py:37
  63.2 13.4 %collective-permute-start.11 = (s16[784,256]{1,0:T(8,128)(2,1)S(1)}, s16[784,256]{1,0:T(8,128)(2,1)S(1)}, u32[]{:S(2)}, u32[]{:S(2)}) collective-permute-start(s16[784,256]{1,0:T(8,128)(2,1)S(1)} %get-tuple-element.50), channel_id=1, source_target_pairs={{0,12},{4,0},{8,4},{12,8},{1,13},{5,1},{9,5},{13,9},{2,14},{6,2},{... | collective-permute-start | bytes 1204232 | tf_op jit(solution)/shard_map/ppermute | solution.py:37

commit v4 on v3

--- a/solution.py
+++ b/solution.py
@@ -385,7 +385,7 @@
     up, later_0 = shifted(first_up, "tile", 1), shifted(later_0, "sect", -1)
     below = [below_0, shifted(below_1, "tile", -1)]
     (later_1, later_2), token = picked(
-        "gather_next", token, [(table_before, 2, g) for g in groups_later[1:3]], later_0, up
+        "gather_next", token, [(table_before, 2, g) for g in groups_later[1:3]], later_0
     )
     later = [later_0, shifted(later_1, "sect", -1), shifted(later_2, "sect", -1)]
 

time: 80.9 us -> 79.7 us (0.985)
  Pallas kernels: 30.9 us -> 33.4 us
  starting transfers between devices: 32.6 us -> 30.2 us
    pallas_call x9, Pallas kernels: 21.1 us -> 23.8 us  [call(): pl.pallas_call(kernel, out_shape=outs, in_specs=[VMEM if o.dtype in (own....]
    ppermute x3, starting transfers between devices: 11.6 us -> 9.15 us  [rotated(): lax.ppermute(value, axis, [(i, (i + steps) % count) for i in range(count)])]
    ppermute x9, waiting for transfers between devices: 7.87 us -> 6.44 us  [shifted(): return lax.ppermute(value, axis, pairs)]
  transfers between devices with their start and end apart: 12 -> 12, of which waited for: 6 -> 5; matrix products, arithmetic and copies ran while one was open for 0% -> 0% of each run, Pallas kernels for 31% -> 34%
where the time goes in v4:
time: 79.7 us; the launch traced here: 79.3 us
  Pallas kernels  33.4 us (42%)
  starting transfers between devices  30.2 us (38%)
  waiting for transfers between devices  13.9 us (17%)
  between operations  1.09 us (1%)
    pallas_call x9, Pallas kernels, call(): pl.pallas_call(kernel, out_shape=outs, in_specs=[VMEM if o.dtype in (own....  23.8 us
    ppermute x9, starting transfers between devices, shifted(): return lax.ppermute(value, axis, pairs)  21 us
    ppermute x3, starting transfers between devices, rotated(): lax.ppermute(value, axis, [(i, (i + steps) % count) for i in range(count)])  9.15 us
    pallas_call x3, Pallas kernels, settled(): pl.pallas_call(kernel, out_shape=(surfaces_kind,) + ((peaks_kind,) if ext...  8.02 us
    ppermute x3, waiting for transfers between devices, rotated(): lax.ppermute(value, axis, [(i, (i + steps) % count) for i in range(count)])  7.43 us
    ppermute x9, waiting for transfers between devices, shifted(): return lax.ppermute(value, axis, pairs)  6.44 us
    pallas_call x1, Pallas kernels, body(): pl.pallas_call(functools.partial(lanes_kernel, tiles, per), out_shape=SDS...  1.64 us
  transfers between devices with their start and end apart: 12, of which 5 were waited for; matrix products, arithmetic and copies ran while one was open for 0% of the time, Pallas kernels for 34%

profile of v4, /device:TPU:0, one launch (start us, length us, event | category | flops | bytes accessed | tf_op | source)
XLA Modules:
  0.0 79.3 jit_solution(8298930981961630374)
XLA Ops:
  0.6 1.6 %lanes.1.refs_0_.refs_1_.table.refs_2_ = s32[5,12]{1,0:T(8,128)} custom-call(s32[3,1,1,12]{3,2,1,0:T(1,128)} %pairs.1, s32[2,1,1,12]{3,2,1,0:T(1,128)} %plan.1), custom_call_target="tpu_custom_call" | custom-call | flops 4000000000 | bytes 1 | tf_op jit(solution)/shard_map/lanes/pallas_call | solution.py:368
  2.3 4.9 %collective-permute-start = (s32[5,12]{1,0:T(8,128)}, s32[5,12]{1,0:T(8,128)S(1)}, u32[]{:S(2)}, u32[]{:S(2)}) collective-permute-start(s32[5,12]{1,0:T(8,128)} %lanes.1.refs_0_.refs_1_.table.refs_2_), channel_id=1, source_target_pairs={{0,4},{4,8},{8,12},{1,5},{5,9},{9,13},{2,6},{6,10},{10,14},{3,7},{... | collective-permute-start | bytes 728 | tf_op jit(solution)/shard_map/ppermute | solution.py:32
  7.2 1.5 %collective-permute-done.refs_1_.refs_2_.table_above = s32[5,12]{1,0:T(8,128)S(1)} collective-permute-done((s32[5,12]{1,0:T(8,128)}, s32[5,12]{1,0:T(8,128)S(1)}, u32[]{:S(2)}, u32[]{:S(2)}) %collective-permute-start) | collective-permute-done | bytes 272 | tf_op jit(solution)/shard_map/ppermute | solution.py:32
  8.8 0.7 copy-done.5
  9.4 1.4 %gather_below.1 = (bf16[6,256,256]{2,1,0:T(8,128)(2,1)S(1)}, s32[5,12]{1,0:T(8,128)S(1)}) custom-call(s32[5,12]{1,0:T(8,128)S(1)} %copy-done.5, s32[5,12]{1,0:T(8,128)S(1)} %collective-permute-done.refs_1_.refs_2_.table_above, bf16[16,256,256]{2,1,0:T(8,128)(2,1)S(1)} %bitcast.3), custom_call_target="tpu_custom_call" | custom-call | flops 200000000 | bytes 1 | tf_op jit(solution)/shard_map/gather_below/pallas_call | solution.py:342
  10.8 1.3 %collective-permute-start.3 = (bf16[6,256,256]{2,1,0:T(8,128)(2,1)S(1)}, bf16[6,256,256]{2,1,0:T(8,128)(2,1)S(1)}, u32[]{:S(2)}, u32[]{:S(2)}) collective-permute-start(bf16[6,256,256]{2,1,0:T(8,128)(2,1)S(1)} %get-tuple-element.32), channel_id=1, source_target_pairs={{4,0},{8,4},{12,8},{5,1},{9,5},{13,9},{6,2},{10,6},{14,10},{7,3},{... | collective-permute-start | bytes 2359304 | tf_op jit(solution)/shard_map/ppermute | solution.py:32
  12.1 3.4 %collective-permute-start.1 = (s32[5,12]{1,0:T(8,128)S(1)}, s32[5,12]{1,0:T(8,128)S(1)}, u32[]{:S(2)}, u32[]{:S(2)}) collective-permute-start(s32[5,12]{1,0:T(8,128)S(1)} %get-tuple-element.28), channel_id=1, source_target_pairs={{0,2},{1,3},{4,6},{5,7},{8,10},{9,11},{12,14},{13,15},{16,18},{17,... | collective-permute-start | bytes 728 | tf_op jit(solution)/shard_map/ppermute | solution.py:32
  15.5 1.3 %collective-permute-done.1.refs_3_.refs_1_.refs_2_ = s32[5,12]{1,0:T(8,128)S(1)} collective-permute-done((s32[5,12]{1,0:T(8,128)S(1)}, s32[5,12]{1,0:T(8,128)S(1)}, u32[]{:S(2)}, u32[]{:S(2)}) %collective-permute-start.1) | collective-permute-done | bytes 272 | tf_op jit(solution)/shard_map/ppermute | solution.py:32
  16.8 1.5 %gather_later.1 = (bf16[3,256,256]{2,1,0:T(8,128)(2,1)S(1)}, bf16[3,256,256]{2,1,0:T(8,128)(2,1)S(1)}, bf16[3,256,256]{2,1,0:T(8,128)(2,1)S(1)}, s32[5,12]{1,0:T(8,128)S(1)}) custom-call(s32[5,12]{1,0:T(8,128)S(1)} %copy-done.5, s32[5,12]{1,0:T(8,128)S(1)} %copy-done.5, s32[5,12]{1,0:T(8,128)S(1)} %collective-permute-done.refs_1_.refs_2_.table_above, ...), custom_call_target="tpu_custom_call" | custom-call | flops 200000000 | bytes 1 | tf_op jit(solution)/shard_map/gather_later/pallas_call | solution.py:342
  18.3 0.0 copy-start.2
  18.4 1.4 %collective-permute-start.2 = (bf16[3,256,256]{2,1,0:T(8,128)(2,1)S(1)}, bf16[3,256,256]{2,1,0:T(8,128)(2,1)S(1)}, u32[]{:S(2)}, u32[]{:S(2)}) collective-permute-start(bf16[3,256,256]{2,1,0:T(8,128)(2,1)S(1)} %get-tuple-element.30), channel_id=1, source_target_pairs={{2,0},{3,1},{6,4},{7,5},{10,8},{11,9},{14,12},{15,13},{18,16},{19,... | collective-permute-start | bytes 1179656 | tf_op jit(solution)/shard_map/ppermute | solution.py:32
  19.8 4.8 %collective-permute-start.4 = (bf16[3,256,256]{2,1,0:T(8,128)(2,1)S(1)}, bf16[3,256,256]{2,1,0:T(8,128)(2,1)S(1)}, u32[]{:S(2)}, u32[]{:S(2)}) collective-permute-start(bf16[3,256,256]{2,1,0:T(8,128)(2,1)S(1)} %get-tuple-element.34), channel_id=1, source_target_pairs={{0,4},{4,8},{8,12},{1,5},{5,9},{9,13},{2,6},{6,10},{10,14},{3,7},{... | collective-permute-start | bytes 1179656 | tf_op jit(solution)/shard_map/ppermute | solution.py:32
  24.6 1.3 %collective-permute-start.5 = (bf16[3,256,256]{2,1,0:T(8,128)(2,1)S(1)}, bf16[3,256,256]{2,1,0:T(8,128)(2,1)S(1)}, u32[]{:S(2)}, u32[]{:S(2)}) collective-permute-start(bf16[3,256,256]{2,1,0:T(8,128)(2,1)S(1)} %get-tuple-element.35), channel_id=1, source_target_pairs={{4,0},{8,4},{12,8},{5,1},{9,5},{13,9},{6,2},{10,6},{14,10},{7,3},{... | collective-permute-start | bytes 1179656 | tf_op jit(solution)/shard_map/ppermute | solution.py:32
  25.9 3.6 %collective-permute-done.2.refs_4_.refs_2_ = bf16[3,256,256]{2,1,0:T(8,128)(2,1)S(1)} collective-permute-done((bf16[3,256,256]{2,1,0:T(8,128)(2,1)S(1)}, bf16[3,256,256]{2,1,0:T(8,128)(2,1)S(1)}, u32[]{:S(2)}, u32[]{:S(2)}) %collective-permute-start.2) | collective-permute-done | bytes 393248 | tf_op jit(solution)/shard_map/ppermute | solution.py:32
  29.5 1.4 %gather_next.1 = (bf16[3,256,256]{2,1,0:T(8,128)(2,1)S(1)}, bf16[3,256,256]{2,1,0:T(8,128)(2,1)S(1)}, s32[5,12]{1,0:T(8,128)S(1)}) custom-call(s32[5,12]{1,0:T(8,128)S(1)} %get-tuple-element.29.refs_0_, s32[5,12]{1,0:T(8,128)S(1)} %collective-permute-done.1.refs_3_.refs_1_.refs_2_, s32[5,12]{1,0:T(8,128)S(1)} %collective-permute-done.1.refs_3_.refs_1_.refs_2_, ...), custom_call_target="tpu_custom_call" | custom-call | flops 200000000 | bytes 1 | tf_op jit(solution)/shard_map/gather_next/pallas_call | solution.py:342
  31.0 1.3 %collective-permute-start.6 = (bf16[3,256,256]{2,1,0:T(8,128)(2,1)S(1)}, bf16[3,256,256]{2,1,0:T(8,128)(2,1)S(1)}, u32[]{:S(2)}, u32[]{:S(2)}) collective-permute-start(bf16[3,256,256]{2,1,0:T(8,128)(2,1)S(1)} %get-tuple-element.39), channel_id=1, source_target_pairs={{2,0},{3,1},{6,4},{7,5},{10,8},{11,9},{14,12},{15,13},{18,16},{19,... | collective-permute-start | bytes 1179656 | tf_op jit(solution)/shard_map/ppermute | solution.py:32
  32.3 1.3 %collective-permute-start.7 = (bf16[3,256,256]{2,1,0:T(8,128)(2,1)S(1)}, bf16[3,256,256]{2,1,0:T(8,128)(2,1)S(1)}, u32[]{:S(2)}, u32[]{:S(2)}) collective-permute-start(bf16[3,256,256]{2,1,0:T(8,128)(2,1)S(1)} %get-tuple-element.41), channel_id=1, source_target_pairs={{2,0},{3,1},{6,4},{7,5},{10,8},{11,9},{14,12},{15,13},{18,16},{19,... | collective-permute-start | bytes 1179656 | tf_op jit(solution)/shard_map/ppermute | solution.py:32
  33.6 4.0 %pairs_2.1 = (s16[784,256]{1,0:T(8,128)(2,1)S(1)}, f32[3]{0:T(128)S(1)}) custom-call(s32[5,12]{1,0:T(8,128)S(1)} %copy-done.5, s32[5,12]{1,0:T(8,128)S(1)} %get-tuple-element.31.before.refs_0_, bf16[16,256,256]{2,1,0:T(8,128)(2,1)S(1)} %bitcast.6, s32[5,12]{1,0:T(8,128)S(1)} %get-tuple-element.31.before.refs_0_, ...), custom_call_target="tpu_custom_call" | custom-call | flops 35000000512 | bytes 1 | tf_op jit(solution)/shard_map/pairs_2/pallas_call | solution.py:342
  37.6 1.1 %gather_home.1 = (bf16[3,256,256]{2,1,0:T(8,128)(2,1)S(1)}, f32[3]{0:T(128)}) custom-call(f32[3]{0:T(128)S(1)} %get-tuple-element.33.token.refs_0_.refs_5_, s32[5,12]{1,0:T(8,128)S(1)} %collective-permute-done.1.refs_3_.refs_1_.refs_2_, bf16[16,256,256]{2,1,0:T(8,128)(2,1)S(1)} %bitcast.7), custom_call_target="tpu_custom_call" | custom-call | flops 200000000 | bytes 1 | tf_op jit(solution)/shard_map/gather_home/pallas_call | solution.py:342
  38.8 1.3 %collective-permute-start.8 = (bf16[3,256,256]{2,1,0:T(8,128)(2,1)S(1)}, bf16[3,256,256]{2,1,0:T(8,128)(2,1)S(1)}, u32[]{:S(2)}, u32[]{:S(2)}) collective-permute-start(bf16[3,256,256]{2,1,0:T(8,128)(2,1)S(1)} %get-tuple-element.43), channel_id=1, source_target_pairs={{2,0},{3,1},{6,4},{7,5},{10,8},{11,9},{14,12},{15,13},{18,16},{19,... | collective-permute-start | bytes 1179656 | tf_op jit(solution)/shard_map/ppermute | solution.py:32
  40.1 1.2 %collective-permute-start.9 = (s16[784,256]{1,0:T(8,128)(2,1)S(1)}, s16[784,256]{1,0:T(8,128)(2,1)S(1)}, u32[]{:S(2)}, u32[]{:S(2)}) collective-permute-start(s16[784,256]{1,0:T(8,128)(2,1)S(1)} %get-tuple-element.46), channel_id=1, source_target_pairs={{0,8},{4,12},{8,0},{12,4},{1,9},{5,13},{9,1},{13,5},{2,10},{6,14},... | collective-permute-start | bytes 1204232 | tf_op jit(solution)/shard_map/ppermute | solution.py:37
  41.3 1.2 %visit.1 = (s16[784,256]{1,0:T(8,128)(2,1)S(1)}, f32[3]{0:T(128)S(1)}) custom-call(s32[5,12]{1,0:T(8,128)S(1)} %collective-permute-done.refs_1_.refs_2_.table_above, f32[3]{0:T(128)S(1)} %get-tuple-element.33.token.refs_0_.refs_5_, bf16[16,256,256]{2,1,0:T(8,128)(2,1)S(1)} %bitcast.8, bf16[3,256,256]{2,1,0:T(8,128)(2,1)S(1)} %collective-permute-done.4.up, ...), custom_call_target="tpu_custom_call" | custom-call | flops 200000000 | bytes 1 | tf_op jit(solution)/shard_map/visit/pallas_call | solution.py:342
  42.5 2.5 %settle_visit.1 = (f32[6,256,256]{2,1,0:T(8,128)}, f32[1]{0:T(128)}) custom-call(f32[3]{0:T(128)S(1)} %get-tuple-element.36.before.refs_0_, s16[784,256]{1,0:T(8,128)(2,1)S(1)} %get-tuple-element.37.refs_0_), custom_call_target="tpu_custom_call" | custom-call | flops 200000000 | bytes 1 | tf_op jit(solution)/shard_map/settle_visit/pallas_call | solution.py:408
  45.0 5.1 %pairs_1.1 = (s16[800,256]{1,0:T(8,128)(2,1)S(1)}, f32[3]{0:T(128)S(1)}) custom-call(s32[5,12]{1,0:T(8,128)S(1)} %copy-done.6, f32[1]{0:T(128)} %get-tuple-element.38.before.refs_0_, bf16[16,256,256]{2,1,0:T(8,128)(2,1)S(1)} %bitcast.9, f32[1]{0:T(128)} %get-tuple-element.38.before.refs_0_, bf16[6,256,256]{2,1,0:T(8,128)(2,1)S(1)} %collective-permute-done.3.refs_1_, ...), custom_call_target="tpu_custom_call" | custom-call | flops 200000000 | bytes 1 | tf_op jit(solution)/shard_map/pairs_1/pallas_call | solution.py:342
  50.2 7.9 %collective-permute-start.10 = (s16[800,256]{1,0:T(8,128)(2,1)S(1)}, s16[800,256]{1,0:T(8,128)(2,1)S(1)}, u32[]{:S(2)}, u32[]{:S(2)}) collective-permute-start(s16[800,256]{1,0:T(8,128)(2,1)S(1)} %get-tuple-element.49), channel_id=1, source_target_pairs={{0,4},{4,8},{8,12},{12,0},{1,5},{5,9},{9,13},{13,1},{2,6},{6,10},{... | collective-permute-start | bytes 1228808 | tf_op jit(solution)/shard_map/ppermute | solution.py:37
  58.1 3.9 %pairs_3.1 = (s16[784,256]{1,0:T(8,128)(2,1)S(1)}, f32[3]{0:T(128)S(1)}) custom-call(s32[5,12]{1,0:T(8,128)S(1)} %copy-done.6, f32[3]{0:T(128)S(1)} %get-tuple-element.40.before.refs_4_, bf16[16,256,256]{2,1,0:T(8,128)(2,1)S(1)} %bitcast.10, f32[3]{0:T(128)S(1)} %get-tuple-element.36.before.refs_0_, bf16[6,256,256]{2,1,0:T(8,128)(2,1)S(1)} %collective-permute-done.3.refs_1_, ...), custom_call_target="tpu_custom_call" | custom-call | flops 200000000 | bytes 1 | tf_op jit(solution)/shard_map/pairs_3/pallas_call | solution.py:342
  62.0 0.1 collective-permute-start.11
  62.1 4.1 %pairs_0.1 = (s16[784,256]{1,0:T(8,128)(2,1)S(1)}, f32[3]{0:T(128)S(1)}) custom-call(s32[5,12]{1,0:T(8,128)S(1)} %copy-done.6, f32[3]{0:T(128)S(1)} %get-tuple-element.42.before.refs_0_.refs_6_, bf16[16,256,256]{2,1,0:T(8,128)(2,1)S(1)} %bitcast.11, f32[3]{0:T(128)S(1)} %get-tuple-element.42.before.refs_0_.refs_6_, ...), custom_call_target="tpu_custom_call" | custom-call | flops 200000000 | bytes 1 | tf_op jit(solution)/shard_map/pairs_0/pallas_call | solution.py:342
  66.2 2.6 %collective-permute-done.9.refs_1_ = s16[784,256]{1,0:T(8,128)(2,1)S(1)} collective-permute-done((s16[784,256]{1,0:T(8,128)(2,1)S(1)}, s16[784,256]{1,0:T(8,128)(2,1)S(1)}, u32[]{:S(2)}, u32[]{:S(2)}) %collective-permute-start.9) | collective-permute-done | bytes 401440 | tf_op jit(solution)/shard_map/ppermute | solution.py:37
  68.8 2.4 %settle_early.1 = (f32[6,256,256]{2,1,0:T(8,128)}, f32[1]{0:T(128)}) custom-call(f32[3]{0:T(128)S(1)} %get-tuple-element.44.before.refs_3_, s16[784,256]{1,0:T(8,128)(2,1)S(1)} %get-tuple-element.45.refs_0_, s16[784,256]{1,0:T(8,128)(2,1)S(1)} %collective-permute-done.9.refs_1_, ...), custom_call_target="tpu_custom_call", output_to_operand_aliasing={{0}: (3, {})} | custom-call | flops 200000000 | bytes 1 | tf_op jit(solution)/shard_map/settle_early/pallas_call | solution.py:408
  71.2 4.8 %collective-permute-done.11.refs_1_ = s16[784,256]{1,0:T(8,128)(2,1)S(1)} collective-permute-done((s16[784,256]{1,0:T(8,128)(2,1)S(1)}, s16[784,256]{1,0:T(8,128)(2,1)S(1)}, u32[]{:S(2)}, u32[]{:S(2)}) %collective-permute-start.11) | collective-permute-done | bytes 401440 | tf_op jit(solution)/shard_map/ppermute | solution.py:37
  76.0 3.1 %settle_last.1 = (f32[6,256,256]{2,1,0:T(8,128)}, f32[12]{0:T(128)}, f32[1]{0:T(128)}) custom-call(f32[1]{0:T(128)} %get-tuple-element.48.before, s16[800,256]{1,0:T(8,128)(2,1)S(1)} %collective-permute-done.10.refs_0_, s16[784,256]{1,0:T(8,128)(2,1)S(1)} %collective-permute-done.11.refs_1_, s32[5,12]{1,0:T(8,128)S(1)} %copy-done.6, ...), custom_call_target="tpu_custom_call", output_to_operand_aliasing={{0}: (8, {})} | custom-call | flops 200000000 | bytes 1 | tf_op jit(solution)/shard_map/settle_last/pallas_call | solution.py:408
  (19 shorter events, 0.1 us)
Async XLA Ops:
  0.6 8.1 %copy-start = (bf16[1,1,16,256,256]{4,3,2,1,0:T(8,128)(2,1)S(1)}, bf16[1,1,16,256,256]{4,3,2,1,0:T(8,128)(2,1)}, u32[]{:S(2)}) copy-start(bf16[1,1,16,256,256]{4,3,2,1,0:T(8,128)(2,1)} %param.7) | copy-start | bytes 6291460
  2.3 6.5 %collective-permute-start = (s32[5,12]{1,0:T(8,128)}, s32[5,12]{1,0:T(8,128)S(1)}, u32[]{:S(2)}, u32[]{:S(2)}) collective-permute-start(s32[5,12]{1,0:T(8,128)} %lanes.1.refs_0_.refs_1_.table.refs_2_), channel_id=1, source_target_pairs={{0,4},{4,8},{8,12},{1,5},{5,9},{9,13},{2,6},{6,10},{10,14},{3,7},{... | collective-permute-start | bytes 728 | tf_op jit(solution)/shard_map/ppermute | solution.py:32
  8.7 0.7 copy-start.5
  10.8 22.8 %collective-permute-start.3 = (bf16[6,256,256]{2,1,0:T(8,128)(2,1)S(1)}, bf16[6,256,256]{2,1,0:T(8,128)(2,1)S(1)}, u32[]{:S(2)}, u32[]{:S(2)}) collective-permute-start(bf16[6,256,256]{2,1,0:T(8,128)(2,1)S(1)} %get-tuple-element.32), channel_id=1, source_target_pairs={{4,0},{8,4},{12,8},{5,1},{9,5},{13,9},{6,2},{10,6},{14,10},{7,3},{... | collective-permute-start | bytes 2359304 | tf_op jit(solution)/shard_map/ppermute | solution.py:32
  12.1 4.7 %collective-permute-start.1 = (s32[5,12]{1,0:T(8,128)S(1)}, s32[5,12]{1,0:T(8,128)S(1)}, u32[]{:S(2)}, u32[]{:S(2)}) collective-permute-start(s32[5,12]{1,0:T(8,128)S(1)} %get-tuple-element.28), channel_id=1, source_target_pairs={{0,2},{1,3},{4,6},{5,7},{8,10},{9,11},{12,14},{13,15},{16,18},{17,... | collective-permute-start | bytes 728 | tf_op jit(solution)/shard_map/ppermute | solution.py:32
  18.3 15.3 %copy-start.1 = (bf16[256,256]{1,0:T(8,128)(2,1)S(1)}, bf16[256,256]{1,0:T(8,128)(2,1)}, u32[]{:S(2)}) copy-start(bf16[256,256]{1,0:T(8,128)(2,1)} %constant.11.clone.refs_6_.sl) | copy-start | bytes 393220
  18.3 15.3 %copy-start.2 = (bf16[256,256]{1,0:T(8,128)(2,1)S(1)}, bf16[256,256]{1,0:T(8,128)(2,1)}, u32[]{:S(2)}) copy-start(bf16[256,256]{1,0:T(8,128)(2,1)} %constant.10.clone.refs_5_.sh) | copy-start | bytes 393220
  18.3 15.3 %copy-start.3 = (bf16[256,256]{1,0:T(8,128)(2,1)S(1)}, bf16[256,256]{1,0:T(8,128)(2,1)}, u32[]{:S(2)}) copy-start(bf16[256,256]{1,0:T(8,128)(2,1)} %constant.9.clone.refs_4_.tl) | copy-start | bytes 393220
  18.4 15.3 %copy-start.4 = (bf16[256,256]{1,0:T(8,128)(2,1)S(1)}, bf16[256,256]{1,0:T(8,128)(2,1)}, u32[]{:S(2)}) copy-start(bf16[256,256]{1,0:T(8,128)(2,1)} %constant.8.clone.refs_3_.th) | copy-start | bytes 393220
  18.4 11.2 %collective-permute-start.2 = (bf16[3,256,256]{2,1,0:T(8,128)(2,1)S(1)}, bf16[3,256,256]{2,1,0:T(8,128)(2,1)S(1)}, u32[]{:S(2)}, u32[]{:S(2)}) collective-permute-start(bf16[3,256,256]{2,1,0:T(8,128)(2,1)S(1)} %get-tuple-element.30), channel_id=1, source_target_pairs={{2,0},{3,1},{6,4},{7,5},{10,8},{11,9},{14,12},{15,13},{18,16},{19,... | collective-permute-start | bytes 1179656 | tf_op jit(solution)/shard_map/ppermute | solution.py:32
  19.8 20.3 %collective-permute-start.4 = (bf16[3,256,256]{2,1,0:T(8,128)(2,1)S(1)}, bf16[3,256,256]{2,1,0:T(8,128)(2,1)S(1)}, u32[]{:S(2)}, u32[]{:S(2)}) collective-permute-start(bf16[3,256,256]{2,1,0:T(8,128)(2,1)S(1)} %get-tuple-element.34), channel_id=1, source_target_pairs={{0,4},{4,8},{8,12},{1,5},{5,9},{9,13},{2,6},{6,10},{10,14},{3,7},{... | collective-permute-start | bytes 1179656 | tf_op jit(solution)/shard_map/ppermute | solution.py:32
  24.6 16.6 %collective-permute-start.5 = (bf16[3,256,256]{2,1,0:T(8,128)(2,1)S(1)}, bf16[3,256,256]{2,1,0:T(8,128)(2,1)S(1)}, u32[]{:S(2)}, u32[]{:S(2)}) collective-permute-start(bf16[3,256,256]{2,1,0:T(8,128)(2,1)S(1)} %get-tuple-element.35), channel_id=1, source_target_pairs={{4,0},{8,4},{12,8},{5,1},{9,5},{13,9},{6,2},{10,6},{14,10},{7,3},{... | collective-permute-start | bytes 1179656 | tf_op jit(solution)/shard_map/ppermute | solution.py:32
  31.0 14.0 %collective-permute-start.6 = (bf16[3,256,256]{2,1,0:T(8,128)(2,1)S(1)}, bf16[3,256,256]{2,1,0:T(8,128)(2,1)S(1)}, u32[]{:S(2)}, u32[]{:S(2)}) collective-permute-start(bf16[3,256,256]{2,1,0:T(8,128)(2,1)S(1)} %get-tuple-element.39), channel_id=1, source_target_pairs={{2,0},{3,1},{6,4},{7,5},{10,8},{11,9},{14,12},{15,13},{18,16},{19,... | collective-permute-start | bytes 1179656 | tf_op jit(solution)/shard_map/ppermute | solution.py:32
  32.3 25.8 %collective-permute-start.7 = (bf16[3,256,256]{2,1,0:T(8,128)(2,1)S(1)}, bf16[3,256,256]{2,1,0:T(8,128)(2,1)S(1)}, u32[]{:S(2)}, u32[]{:S(2)}) collective-permute-start(bf16[3,256,256]{2,1,0:T(8,128)(2,1)S(1)} %get-tuple-element.41), channel_id=1, source_target_pairs={{2,0},{3,1},{6,4},{7,5},{10,8},{11,9},{14,12},{15,13},{18,16},{19,... | collective-permute-start | bytes 1179656 | tf_op jit(solution)/shard_map/ppermute | solution.py:32
  38.8 23.3 %collective-permute-start.8 = (bf16[3,256,256]{2,1,0:T(8,128)(2,1)S(1)}, bf16[3,256,256]{2,1,0:T(8,128)(2,1)S(1)}, u32[]{:S(2)}, u32[]{:S(2)}) collective-permute-start(bf16[3,256,256]{2,1,0:T(8,128)(2,1)S(1)} %get-tuple-element.43), channel_id=1, source_target_pairs={{2,0},{3,1},{6,4},{7,5},{10,8},{11,9},{14,12},{15,13},{18,16},{19,... | collective-permute-start | bytes 1179656 | tf_op jit(solution)/shard_map/ppermute | solution.py:32
  40.1 4.9 %copy-start.6 = (s32[5,12]{1,0:T(8,128)S(1)}, s32[5,12]{1,0:T(8,128)}, u32[]{:S(2)}) copy-start(s32[5,12]{1,0:T(8,128)} %lanes.1.refs_0_.refs_1_.table.refs_2_) | copy-start | bytes 724
  40.1 28.7 %collective-permute-start.9 = (s16[784,256]{1,0:T(8,128)(2,1)S(1)}, s16[784,256]{1,0:T(8,128)(2,1)S(1)}, u32[]{:S(2)}, u32[]{:S(2)}) collective-permute-start(s16[784,256]{1,0:T(8,128)(2,1)S(1)} %get-tuple-element.46), channel_id=1, source_target_pairs={{0,8},{4,12},{8,0},{12,4},{1,9},{5,13},{9,1},{13,5},{2,10},{6,14},... | collective-permute-start | bytes 1204232 | tf_op jit(solution)/shard_map/ppermute | solution.py:37
  50.2 25.8 %collective-permute-start.10 = (s16[800,256]{1,0:T(8,128)(2,1)S(1)}, s16[800,256]{1,0:T(8,128)(2,1)S(1)}, u32[]{:S(2)}, u32[]{:S(2)}) collective-permute-start(s16[800,256]{1,0:T(8,128)(2,1)S(1)} %get-tuple-element.49), channel_id=1, source_target_pairs={{0,4},{4,8},{8,12},{12,0},{1,5},{5,9},{9,13},{13,1},{2,6},{6,10},{... | collective-permute-start | bytes 1228808 | tf_op jit(solution)/shard_map/ppermute | solution.py:37
  62.0 14.0 %collective-permute-start.11 = (s16[784,256]{1,0:T(8,128)(2,1)S(1)}, s16[784,256]{1,0:T(8,128)(2,1)S(1)}, u32[]{:S(2)}, u32[]{:S(2)}) collective-permute-start(s16[784,256]{1,0:T(8,128)(2,1)S(1)} %get-tuple-element.50), channel_id=1, source_target_pairs={{0,12},{4,0},{8,4},{12,8},{1,13},{5,1},{9,5},{13,9},{2,14},{6,2},{... | collective-permute-start | bytes 1204232 | tf_op jit(solution)/shard_map/ppermute | solution.py:37

commit v5 on v4

--- a/solution.py
+++ b/solution.py
@@ -228,6 +228,13 @@
                 jnp.where(kinds[j] == 0, at_hand[0][at_below + j], seconds[j]) for j in range(per)
             ]
         correlate(firsts, seconds, places, guests, th, tl, sh, sl, codes, peaks)
+
+
+def pair_send_kernel(pair, wanted, table, before, own, guests, below, later, th, tl, sh, sl, other, *refs):
+    *_, codes, peaks, sent = refs
+    for i, (field, lane) in enumerate(wanted):
+        sent[i] = own[other[field, lane]]
+    pair(table, before, own, guests, below, later, th, tl, sh, sl, codes, peaks)
 
 
 def visit_kernel(lanes, table_above, token, own, up, th, tl, sh, sl, _, codes, peaks):
@@ -422,20 +429,26 @@
 
     home_peaks, moving = [None] * tiles, {}
 
-    def paired(d, before, guests, last=(), flops=SETTLE):
+    def paired(d, before, guests, last=(), flops=SETTLE, send=()):
         near = [i for i, g in enumerate(groups_below) if d in g or d == 1][0]
         late = [i for i, g in enumerate(groups_later) if d in g][0]
-        lane_codes, home_peaks[d] = call(
-            functools.partial(
-                pair_kernel,
-                lanes_at(d),
-                0 if d == 1 else groups_below[near].index(d) * per,
-                groups_later[late].index(d) * per,
-                1 if d == 1 else None,
-                d == up_one,
-            ),
+        kernel = functools.partial(
+            pair_kernel,
+            lanes_at(d),
+            0 if d == 1 else groups_below[near].index(d) * per,
+            groups_later[late].index(d) * per,
+            1 if d == 1 else None,
+            d == up_one,
+        )
+        outs = longer if d == 1 else result
+        if send:
+            wanted = [(2, lane) for e in send for lane in lanes_at(e)]
+            kernel = functools.partial(pair_send_kernel, kernel, wanted)
+            outs += (SDS((len(wanted), length, length), own.dtype),)
+        lane_codes, home_peaks[d], *sent = call(
+            kernel,
             f"pairs_{d}",
-            longer if d == 1 else result,
+            outs,
             table,
             before,
             own,
@@ -443,16 +456,17 @@
             below[near],
             later[late],
             *tables,
+            *([table_before] if send else []),
             last=last,
             flops=flops,
         )
         moving[d] = lane_codes if d == 0 else rotated(lane_codes, "tile", d)
-        return home_peaks[d]
+        return home_peaks[d], sent
 
     for d in far:
-        token = paired(d, token, token, flops=FIRST)
-    (later_3,), _ = picked("gather_home", token, [(table_before, 2, groups_later[3])])
-    later.append(shifted(later_3, "sect", -1))
+        send = groups_later[3] if d == far[-1] else ()
+        token, sent = paired(d, token, token, flops=FIRST, send=send)
+    later.append(shifted(sent[0], "sect", -1))
     visit_codes, guests = call(
         functools.partial(visit_kernel, lanes_at(1)),
         "visit",
@@ -465,9 +479,9 @@
         last=[below[1]],
     )
     surfaces, before = settled("settle_visit", [visit_codes], guests)
-    before = paired(1, before, before)
-    before = paired(up_one, before, guests)
-    before = paired(0, before, before)
+    before, _ = paired(1, before, before)
+    before, _ = paired(up_one, before, guests)
+    before, _ = paired(0, before, before)
     early = [moving[d] for d in [0] + far]
     surfaces, before = settled("settle_early", early, before, surfaces)
     last = [moving[1], moving[up_one]]

time: 79.7 us -> 79.3 us (level)
  Pallas kernels: 33.4 us -> 32.4 us
    pallas_call x9 -> x8, Pallas kernels: 23.8 us -> 22.7 us  [call(): pl.pallas_call(kernel, out_shape=outs, in_specs=[VMEM if o.dtype in (own....]
    ppermute x9, waiting for transfers between devices: 6.44 us -> 7.42 us  [shifted(): return lax.ppermute(value, axis, pairs)]
  transfers between devices with their start and end apart: 12 -> 12, of which waited for: 5 -> 6; matrix products, arithmetic and copies ran while one was open for 0% -> 0% of each run, Pallas kernels for 34% -> 33%
where the time goes in v5:
time: 79.3 us; the launch traced here: 78.9 us
  Pallas kernels  32.4 us (41%)
  starting transfers between devices  30.2 us (38%)
  waiting for transfers between devices  14.5 us (18%)
  between operations  1.04 us (1%)
    pallas_call x8, Pallas kernels, call(): pl.pallas_call(kernel, out_shape=outs, in_specs=[VMEM if o.dtype in (own....  22.7 us
    ppermute x9, starting transfers between devices, shifted(): return lax.ppermute(value, axis, pairs)  21 us
    ppermute x3, starting transfers between devices, rotated(): lax.ppermute(value, axis, [(i, (i + steps) % count) for i in range(count)])  9.14 us
    pallas_call x3, Pallas kernels, settled(): pl.pallas_call(kernel, out_shape=(surfaces_kind,) + ((peaks_kind,) if ext...  8.04 us
    ppermute x9, waiting for transfers between devices, shifted(): return lax.ppermute(value, axis, pairs)  7.42 us
    ppermute x3, waiting for transfers between devices, rotated(): lax.ppermute(value, axis, [(i, (i + steps) % count) for i in range(count)])  7.11 us
    pallas_call x1, Pallas kernels, body(): pl.pallas_call(functools.partial(lanes_kernel, tiles, per), out_shape=SDS...  1.64 us
  transfers between devices with their start and end apart: 12, of which 6 were waited for; matrix products, arithmetic and copies ran while one was open for 0% of the time, Pallas kernels for 33%

profile of v5, /device:TPU:0, one launch (start us, length us, event | category | flops | bytes accessed | tf_op | source)
XLA Modules:
  0.0 78.9 jit_solution(3971435787636866443)
XLA Ops:
  0.6 1.6 %lanes.1.refs_0_.refs_1_.table.refs_2_ = s32[5,12]{1,0:T(8,128)} custom-call(s32[3,1,1,12]{3,2,1,0:T(1,128)} %pairs.1, s32[2,1,1,12]{3,2,1,0:T(1,128)} %plan.1), custom_call_target="tpu_custom_call" | custom-call | flops 4000000000 | bytes 1 | tf_op jit(solution)/shard_map/lanes/pallas_call | solution.py:375
  2.3 4.9 %collective-permute-start = (s32[5,12]{1,0:T(8,128)}, s32[5,12]{1,0:T(8,128)S(1)}, u32[]{:S(2)}, u32[]{:S(2)}) collective-permute-start(s32[5,12]{1,0:T(8,128)} %lanes.1.refs_0_.refs_1_.table.refs_2_), channel_id=1, source_target_pairs={{0,4},{4,8},{8,12},{1,5},{5,9},{9,13},{2,6},{6,10},{10,14},{3,7},{... | collective-permute-start | bytes 728 | tf_op jit(solution)/shard_map/ppermute | solution.py:32
  7.2 1.5 %collective-permute-done.refs_1_.refs_2_.table_above = s32[5,12]{1,0:T(8,128)S(1)} collective-permute-done((s32[5,12]{1,0:T(8,128)}, s32[5,12]{1,0:T(8,128)S(1)}, u32[]{:S(2)}, u32[]{:S(2)}) %collective-permute-start) | collective-permute-done | bytes 272 | tf_op jit(solution)/shard_map/ppermute | solution.py:32
  8.8 0.7 copy-done.5
  9.4 1.4 %gather_below.1 = (bf16[6,256,256]{2,1,0:T(8,128)(2,1)S(1)}, s32[5,12]{1,0:T(8,128)S(1)}) custom-call(s32[5,12]{1,0:T(8,128)S(1)} %copy-done.5, s32[5,12]{1,0:T(8,128)S(1)} %collective-permute-done.refs_1_.refs_2_.table_above, bf16[16,256,256]{2,1,0:T(8,128)(2,1)S(1)} %bitcast.3), custom_call_target="tpu_custom_call" | custom-call | flops 200000000 | bytes 1 | tf_op jit(solution)/shard_map/gather_below/pallas_call | solution.py:349
  10.8 1.3 %collective-permute-start.3 = (bf16[6,256,256]{2,1,0:T(8,128)(2,1)S(1)}, bf16[6,256,256]{2,1,0:T(8,128)(2,1)S(1)}, u32[]{:S(2)}, u32[]{:S(2)}) collective-permute-start(bf16[6,256,256]{2,1,0:T(8,128)(2,1)S(1)} %get-tuple-element.32), channel_id=1, source_target_pairs={{4,0},{8,4},{12,8},{5,1},{9,5},{13,9},{6,2},{10,6},{14,10},{7,3},{... | collective-permute-start | bytes 2359304 | tf_op jit(solution)/shard_map/ppermute | solution.py:32
  12.1 3.4 %collective-permute-start.1 = (s32[5,12]{1,0:T(8,128)S(1)}, s32[5,12]{1,0:T(8,128)S(1)}, u32[]{:S(2)}, u32[]{:S(2)}) collective-permute-start(s32[5,12]{1,0:T(8,128)S(1)} %get-tuple-element.28), channel_id=1, source_target_pairs={{0,2},{1,3},{4,6},{5,7},{8,10},{9,11},{12,14},{13,15},{16,18},{17,... | collective-permute-start | bytes 728 | tf_op jit(solution)/shard_map/ppermute | solution.py:32
  15.5 1.3 %collective-permute-done.1.refs_3_.refs_1_.refs_2_.other = s32[5,12]{1,0:T(8,128)S(1)} collective-permute-done((s32[5,12]{1,0:T(8,128)S(1)}, s32[5,12]{1,0:T(8,128)S(1)}, u32[]{:S(2)}, u32[]{:S(2)}) %collective-permute-start.1) | collective-permute-done | bytes 272 | tf_op jit(solution)/shard_map/ppermute | solution.py:32
  16.8 1.5 %gather_later.1 = (bf16[3,256,256]{2,1,0:T(8,128)(2,1)S(1)}, bf16[3,256,256]{2,1,0:T(8,128)(2,1)S(1)}, bf16[3,256,256]{2,1,0:T(8,128)(2,1)S(1)}, s32[5,12]{1,0:T(8,128)S(1)}) custom-call(s32[5,12]{1,0:T(8,128)S(1)} %copy-done.5, s32[5,12]{1,0:T(8,128)S(1)} %copy-done.5, s32[5,12]{1,0:T(8,128)S(1)} %collective-permute-done.refs_1_.refs_2_.table_above, ...), custom_call_target="tpu_custom_call" | custom-call | flops 200000000 | bytes 1 | tf_op jit(solution)/shard_map/gather_later/pallas_call | solution.py:349
  18.3 0.0 copy-start.1
  18.4 1.4 %collective-permute-start.2 = (bf16[3,256,256]{2,1,0:T(8,128)(2,1)S(1)}, bf16[3,256,256]{2,1,0:T(8,128)(2,1)S(1)}, u32[]{:S(2)}, u32[]{:S(2)}) collective-permute-start(bf16[3,256,256]{2,1,0:T(8,128)(2,1)S(1)} %get-tuple-element.30), channel_id=1, source_target_pairs={{2,0},{3,1},{6,4},{7,5},{10,8},{11,9},{14,12},{15,13},{18,16},{19,... | collective-permute-start | bytes 1179656 | tf_op jit(solution)/shard_map/ppermute | solution.py:32
  19.8 4.8 %collective-permute-start.4 = (bf16[3,256,256]{2,1,0:T(8,128)(2,1)S(1)}, bf16[3,256,256]{2,1,0:T(8,128)(2,1)S(1)}, u32[]{:S(2)}, u32[]{:S(2)}) collective-permute-start(bf16[3,256,256]{2,1,0:T(8,128)(2,1)S(1)} %get-tuple-element.34), channel_id=1, source_target_pairs={{0,4},{4,8},{8,12},{1,5},{5,9},{9,13},{2,6},{6,10},{10,14},{3,7},{... | collective-permute-start | bytes 1179656 | tf_op jit(solution)/shard_map/ppermute | solution.py:32
  24.7 1.3 %collective-permute-start.5 = (bf16[3,256,256]{2,1,0:T(8,128)(2,1)S(1)}, bf16[3,256,256]{2,1,0:T(8,128)(2,1)S(1)}, u32[]{:S(2)}, u32[]{:S(2)}) collective-permute-start(bf16[3,256,256]{2,1,0:T(8,128)(2,1)S(1)} %get-tuple-element.35), channel_id=1, source_target_pairs={{4,0},{8,4},{12,8},{5,1},{9,5},{13,9},{6,2},{10,6},{14,10},{7,3},{... | collective-permute-start | bytes 1179656 | tf_op jit(solution)/shard_map/ppermute | solution.py:32
  26.0 3.6 %collective-permute-done.2.refs_4_.later = bf16[3,256,256]{2,1,0:T(8,128)(2,1)S(1)} collective-permute-done((bf16[3,256,256]{2,1,0:T(8,128)(2,1)S(1)}, bf16[3,256,256]{2,1,0:T(8,128)(2,1)S(1)}, u32[]{:S(2)}, u32[]{:S(2)}) %collective-permute-start.2) | collective-permute-done | bytes 393248 | tf_op jit(solution)/shard_map/ppermute | solution.py:32
  29.5 1.4 %gather_next.1 = (bf16[3,256,256]{2,1,0:T(8,128)(2,1)S(1)}, bf16[3,256,256]{2,1,0:T(8,128)(2,1)S(1)}, s32[5,12]{1,0:T(8,128)S(1)}) custom-call(s32[5,12]{1,0:T(8,128)S(1)} %get-tuple-element.29.refs_0_, s32[5,12]{1,0:T(8,128)S(1)} %collective-permute-done.1.refs_3_.refs_1_.refs_2_.other, s32[5,12]{1,0:T(8,128)S(1)} %collective-permute-done.1.refs_3_.refs_1_.refs_2_.other, ...), custom_call_target="tpu_custom_call" | custom-call | flops 200000000 | bytes 1 | tf_op jit(solution)/shard_map/gather_next/pallas_call | solution.py:349
  31.0 1.3 %collective-permute-start.6 = (bf16[3,256,256]{2,1,0:T(8,128)(2,1)S(1)}, bf16[3,256,256]{2,1,0:T(8,128)(2,1)S(1)}, u32[]{:S(2)}, u32[]{:S(2)}) collective-permute-start(bf16[3,256,256]{2,1,0:T(8,128)(2,1)S(1)} %get-tuple-element.39), channel_id=1, source_target_pairs={{2,0},{3,1},{6,4},{7,5},{10,8},{11,9},{14,12},{15,13},{18,16},{19,... | collective-permute-start | bytes 1179656 | tf_op jit(solution)/shard_map/ppermute | solution.py:32
  32.3 1.3 %collective-permute-start.7 = (bf16[3,256,256]{2,1,0:T(8,128)(2,1)S(1)}, bf16[3,256,256]{2,1,0:T(8,128)(2,1)S(1)}, u32[]{:S(2)}, u32[]{:S(2)}) collective-permute-start(bf16[3,256,256]{2,1,0:T(8,128)(2,1)S(1)} %get-tuple-element.41), channel_id=1, source_target_pairs={{2,0},{3,1},{6,4},{7,5},{10,8},{11,9},{14,12},{15,13},{18,16},{19,... | collective-permute-start | bytes 1179656 | tf_op jit(solution)/shard_map/ppermute | solution.py:32
  33.6 4.1 %pairs_2.1 = (s16[784,256]{1,0:T(8,128)(2,1)S(1)}, f32[3]{0:T(128)S(1)}, bf16[3,256,256]{2,1,0:T(8,128)(2,1)S(1)}) custom-call(s32[5,12]{1,0:T(8,128)S(1)} %copy-done.5, s32[5,12]{1,0:T(8,128)S(1)} %get-tuple-element.31.before.guests, bf16[16,256,256]{2,1,0:T(8,128)(2,1)S(1)} %bitcast.6, s32[5,12]{1,0:T(8,128)S(1)} %get-tuple-element.31.before.guests, ...), custom_call_target="tpu_custom_call" | custom-call | flops 35000000512 | bytes 1 | tf_op jit(solution)/shard_map/pairs_2/pallas_call | solution.py:349
  37.7 1.3 %collective-permute-start.8 = (bf16[3,256,256]{2,1,0:T(8,128)(2,1)S(1)}, bf16[3,256,256]{2,1,0:T(8,128)(2,1)S(1)}, u32[]{:S(2)}, u32[]{:S(2)}) collective-permute-start(bf16[3,256,256]{2,1,0:T(8,128)(2,1)S(1)} %get-tuple-element.43), channel_id=1, source_target_pairs={{2,0},{3,1},{6,4},{7,5},{10,8},{11,9},{14,12},{15,13},{18,16},{19,... | collective-permute-start | bytes 1179656 | tf_op jit(solution)/shard_map/ppermute | solution.py:32
  39.0 1.2 %collective-permute-start.9 = (s16[784,256]{1,0:T(8,128)(2,1)S(1)}, s16[784,256]{1,0:T(8,128)(2,1)S(1)}, u32[]{:S(2)}, u32[]{:S(2)}) collective-permute-start(s16[784,256]{1,0:T(8,128)(2,1)S(1)} %get-tuple-element.46), channel_id=1, source_target_pairs={{0,8},{4,12},{8,0},{12,4},{1,9},{5,13},{9,1},{13,5},{2,10},{6,14},... | collective-permute-start | bytes 1204232 | tf_op jit(solution)/shard_map/ppermute | solution.py:37
  40.2 1.2 %visit.1 = (s16[784,256]{1,0:T(8,128)(2,1)S(1)}, f32[3]{0:T(128)S(1)}) custom-call(s32[5,12]{1,0:T(8,128)S(1)} %collective-permute-done.refs_1_.refs_2_.table_above, f32[3]{0:T(128)S(1)} %get-tuple-element.33.token.refs_5_, bf16[16,256,256]{2,1,0:T(8,128)(2,1)S(1)} %bitcast.7, bf16[3,256,256]{2,1,0:T(8,128)(2,1)S(1)} %collective-permute-done.4.up, ...), custom_call_target="tpu_custom_call" | custom-call | flops 200000000 | bytes 1 | tf_op jit(solution)/shard_map/visit/pallas_call | solution.py:349
  41.4 2.5 %settle_visit.1 = (f32[6,256,256]{2,1,0:T(8,128)}, f32[1]{0:T(128)}) custom-call(f32[3]{0:T(128)S(1)} %get-tuple-element.36.before.refs_0_, s16[784,256]{1,0:T(8,128)(2,1)S(1)} %get-tuple-element.37.refs_0_), custom_call_target="tpu_custom_call" | custom-call | flops 200000000 | bytes 1 | tf_op jit(solution)/shard_map/settle_visit/pallas_call | solution.py:415
  44.0 1.0 %collective-permute-done.6.refs_2_ = bf16[3,256,256]{2,1,0:T(8,128)(2,1)S(1)} collective-permute-done((bf16[3,256,256]{2,1,0:T(8,128)(2,1)S(1)}, bf16[3,256,256]{2,1,0:T(8,128)(2,1)S(1)}, u32[]{:S(2)}, u32[]{:S(2)}) %collective-permute-start.6) | collective-permute-done | bytes 393248 | tf_op jit(solution)/shard_map/ppermute | solution.py:32
  44.9 5.1 %pairs_1.1 = (s16[800,256]{1,0:T(8,128)(2,1)S(1)}, f32[3]{0:T(128)S(1)}) custom-call(s32[5,12]{1,0:T(8,128)S(1)} %copy-done.6, f32[1]{0:T(128)} %get-tuple-element.38.before.refs_0_, bf16[16,256,256]{2,1,0:T(8,128)(2,1)S(1)} %bitcast.8, f32[1]{0:T(128)} %get-tuple-element.38.before.refs_0_, bf16[6,256,256]{2,1,0:T(8,128)(2,1)S(1)} %collective-permute-done.3.below.refs_1_, ...), custom_call_target="tpu_custom_call" | custom-call | flops 200000000 | bytes 1 | tf_op jit(solution)/shard_map/pairs_1/pallas_call | solution.py:349
  50.1 4.2 %collective-permute-start.10 = (s16[800,256]{1,0:T(8,128)(2,1)S(1)}, s16[800,256]{1,0:T(8,128)(2,1)S(1)}, u32[]{:S(2)}, u32[]{:S(2)}) collective-permute-start(s16[800,256]{1,0:T(8,128)(2,1)S(1)} %get-tuple-element.49), channel_id=1, source_target_pairs={{0,4},{4,8},{8,12},{12,0},{1,5},{5,9},{9,13},{13,1},{2,6},{6,10},{... | collective-permute-start | bytes 1228808 | tf_op jit(solution)/shard_map/ppermute | solution.py:37
  54.3 3.9 %pairs_3.1 = (s16[784,256]{1,0:T(8,128)(2,1)S(1)}, f32[3]{0:T(128)S(1)}) custom-call(s32[5,12]{1,0:T(8,128)S(1)} %copy-done.6, f32[3]{0:T(128)S(1)} %get-tuple-element.40.before.refs_4_, bf16[16,256,256]{2,1,0:T(8,128)(2,1)S(1)} %bitcast.9, f32[3]{0:T(128)S(1)} %get-tuple-element.36.before.refs_0_, ...), custom_call_target="tpu_custom_call" | custom-call | flops 200000000 | bytes 1 | tf_op jit(solution)/shard_map/pairs_3/pallas_call | solution.py:349
  58.2 3.8 %collective-permute-start.11 = (s16[784,256]{1,0:T(8,128)(2,1)S(1)}, s16[784,256]{1,0:T(8,128)(2,1)S(1)}, u32[]{:S(2)}, u32[]{:S(2)}) collective-permute-start(s16[784,256]{1,0:T(8,128)(2,1)S(1)} %get-tuple-element.50), channel_id=1, source_target_pairs={{0,12},{4,0},{8,4},{12,8},{1,13},{5,1},{9,5},{13,9},{2,14},{6,2},{... | collective-permute-start | bytes 1204232 | tf_op jit(solution)/shard_map/ppermute | solution.py:37
  62.0 4.1 %pairs_0.1 = (s16[784,256]{1,0:T(8,128)(2,1)S(1)}, f32[3]{0:T(128)S(1)}) custom-call(s32[5,12]{1,0:T(8,128)S(1)} %copy-done.6, f32[3]{0:T(128)S(1)} %get-tuple-element.42.before.refs_0_.refs_6_, bf16[16,256,256]{2,1,0:T(8,128)(2,1)S(1)} %bitcast.10, f32[3]{0:T(128)S(1)} %get-tuple-element.42.before.refs_0_.refs_6_, ...), custom_call_target="tpu_custom_call" | custom-call | flops 200000000 | bytes 1 | tf_op jit(solution)/shard_map/pairs_0/pallas_call | solution.py:349
  66.0 2.1 %collective-permute-done.9.refs_1_ = s16[784,256]{1,0:T(8,128)(2,1)S(1)} collective-permute-done((s16[784,256]{1,0:T(8,128)(2,1)S(1)}, s16[784,256]{1,0:T(8,128)(2,1)S(1)}, u32[]{:S(2)}, u32[]{:S(2)}) %collective-permute-start.9) | collective-permute-done | bytes 401440 | tf_op jit(solution)/shard_map/ppermute | solution.py:37
  68.2 2.4 %settle_early.1 = (f32[6,256,256]{2,1,0:T(8,128)}, f32[1]{0:T(128)}) custom-call(f32[3]{0:T(128)S(1)} %get-tuple-element.44.before.refs_3_, s16[784,256]{1,0:T(8,128)(2,1)S(1)} %get-tuple-element.45.refs_0_, s16[784,256]{1,0:T(8,128)(2,1)S(1)} %collective-permute-done.9.refs_1_, ...), custom_call_target="tpu_custom_call", output_to_operand_aliasing={{0}: (3, {})} | custom-call | flops 200000000 | bytes 1 | tf_op jit(solution)/shard_map/settle_early/pallas_call | solution.py:415
  70.6 5.0 %collective-permute-done.11.refs_1_ = s16[784,256]{1,0:T(8,128)(2,1)S(1)} collective-permute-done((s16[784,256]{1,0:T(8,128)(2,1)S(1)}, s16[784,256]{1,0:T(8,128)(2,1)S(1)}, u32[]{:S(2)}, u32[]{:S(2)}) %collective-permute-start.11) | collective-permute-done | bytes 401440 | tf_op jit(solution)/shard_map/ppermute | solution.py:37
  75.6 3.1 %settle_last.1 = (f32[6,256,256]{2,1,0:T(8,128)}, f32[12]{0:T(128)}, f32[1]{0:T(128)}) custom-call(f32[1]{0:T(128)} %get-tuple-element.48.before, s16[800,256]{1,0:T(8,128)(2,1)S(1)} %collective-permute-done.10.refs_0_, s16[784,256]{1,0:T(8,128)(2,1)S(1)} %collective-permute-done.11.refs_1_, s32[5,12]{1,0:T(8,128)S(1)} %copy-done.6, ...), custom_call_target="tpu_custom_call", output_to_operand_aliasing={{0}: (8, {})} | custom-call | flops 200000000 | bytes 1 | tf_op jit(solution)/shard_map/settle_last/pallas_call | solution.py:415
  (18 shorter events, 0.0 us)
Async XLA Ops:
  0.6 8.1 %copy-start = (bf16[1,1,16,256,256]{4,3,2,1,0:T(8,128)(2,1)S(1)}, bf16[1,1,16,256,256]{4,3,2,1,0:T(8,128)(2,1)}, u32[]{:S(2)}) copy-start(bf16[1,1,16,256,256]{4,3,2,1,0:T(8,128)(2,1)} %param.7) | copy-start | bytes 6291460
  2.3 6.5 %collective-permute-start = (s32[5,12]{1,0:T(8,128)}, s32[5,12]{1,0:T(8,128)S(1)}, u32[]{:S(2)}, u32[]{:S(2)}) collective-permute-start(s32[5,12]{1,0:T(8,128)} %lanes.1.refs_0_.refs_1_.table.refs_2_), channel_id=1, source_target_pairs={{0,4},{4,8},{8,12},{1,5},{5,9},{9,13},{2,6},{6,10},{10,14},{3,7},{... | collective-permute-start | bytes 728 | tf_op jit(solution)/shard_map/ppermute | solution.py:32
  8.7 0.7 copy-start.5
  10.8 22.8 %collective-permute-start.3 = (bf16[6,256,256]{2,1,0:T(8,128)(2,1)S(1)}, bf16[6,256,256]{2,1,0:T(8,128)(2,1)S(1)}, u32[]{:S(2)}, u32[]{:S(2)}) collective-permute-start(bf16[6,256,256]{2,1,0:T(8,128)(2,1)S(1)} %get-tuple-element.32), channel_id=1, source_target_pairs={{4,0},{8,4},{12,8},{5,1},{9,5},{13,9},{6,2},{10,6},{14,10},{7,3},{... | collective-permute-start | bytes 2359304 | tf_op jit(solution)/shard_map/ppermute | solution.py:32
  12.1 4.7 %collective-permute-start.1 = (s32[5,12]{1,0:T(8,128)S(1)}, s32[5,12]{1,0:T(8,128)S(1)}, u32[]{:S(2)}, u32[]{:S(2)}) collective-permute-start(s32[5,12]{1,0:T(8,128)S(1)} %get-tuple-element.28), channel_id=1, source_target_pairs={{0,2},{1,3},{4,6},{5,7},{8,10},{9,11},{12,14},{13,15},{16,18},{17,... | collective-permute-start | bytes 728 | tf_op jit(solution)/shard_map/ppermute | solution.py:32
  18.3 15.3 %copy-start.1 = (bf16[256,256]{1,0:T(8,128)(2,1)S(1)}, bf16[256,256]{1,0:T(8,128)(2,1)}, u32[]{:S(2)}) copy-start(bf16[256,256]{1,0:T(8,128)(2,1)} %constant.11.clone.sl.refs_6_) | copy-start | bytes 393220
  18.3 15.3 %copy-start.2 = (bf16[256,256]{1,0:T(8,128)(2,1)S(1)}, bf16[256,256]{1,0:T(8,128)(2,1)}, u32[]{:S(2)}) copy-start(bf16[256,256]{1,0:T(8,128)(2,1)} %constant.10.clone.sh.refs_5_) | copy-start | bytes 393220
  18.4 15.3 %copy-start.3 = (bf16[256,256]{1,0:T(8,128)(2,1)S(1)}, bf16[256,256]{1,0:T(8,128)(2,1)}, u32[]{:S(2)}) copy-start(bf16[256,256]{1,0:T(8,128)(2,1)} %constant.9.clone.tl.refs_4_) | copy-start | bytes 393220
  18.4 15.3 %copy-start.4 = (bf16[256,256]{1,0:T(8,128)(2,1)S(1)}, bf16[256,256]{1,0:T(8,128)(2,1)}, u32[]{:S(2)}) copy-start(bf16[256,256]{1,0:T(8,128)(2,1)} %constant.8.clone.th.refs_3_) | copy-start | bytes 393220
  18.4 11.2 %collective-permute-start.2 = (bf16[3,256,256]{2,1,0:T(8,128)(2,1)S(1)}, bf16[3,256,256]{2,1,0:T(8,128)(2,1)S(1)}, u32[]{:S(2)}, u32[]{:S(2)}) collective-permute-start(bf16[3,256,256]{2,1,0:T(8,128)(2,1)S(1)} %get-tuple-element.30), channel_id=1, source_target_pairs={{2,0},{3,1},{6,4},{7,5},{10,8},{11,9},{14,12},{15,13},{18,16},{19,... | collective-permute-start | bytes 1179656 | tf_op jit(solution)/shard_map/ppermute | solution.py:32
  19.8 19.2 %collective-permute-start.4 = (bf16[3,256,256]{2,1,0:T(8,128)(2,1)S(1)}, bf16[3,256,256]{2,1,0:T(8,128)(2,1)S(1)}, u32[]{:S(2)}, u32[]{:S(2)}) collective-permute-start(bf16[3,256,256]{2,1,0:T(8,128)(2,1)S(1)} %get-tuple-element.34), channel_id=1, source_target_pairs={{0,4},{4,8},{8,12},{1,5},{5,9},{9,13},{2,6},{6,10},{10,14},{3,7},{... | collective-permute-start | bytes 1179656 | tf_op jit(solution)/shard_map/ppermute | solution.py:32
  24.7 15.6 %collective-permute-start.5 = (bf16[3,256,256]{2,1,0:T(8,128)(2,1)S(1)}, bf16[3,256,256]{2,1,0:T(8,128)(2,1)S(1)}, u32[]{:S(2)}, u32[]{:S(2)}) collective-permute-start(bf16[3,256,256]{2,1,0:T(8,128)(2,1)S(1)} %get-tuple-element.35), channel_id=1, source_target_pairs={{4,0},{8,4},{12,8},{5,1},{9,5},{13,9},{6,2},{10,6},{14,10},{7,3},{... | collective-permute-start | bytes 1179656 | tf_op jit(solution)/shard_map/ppermute | solution.py:32
  31.0 13.9 %collective-permute-start.6 = (bf16[3,256,256]{2,1,0:T(8,128)(2,1)S(1)}, bf16[3,256,256]{2,1,0:T(8,128)(2,1)S(1)}, u32[]{:S(2)}, u32[]{:S(2)}) collective-permute-start(bf16[3,256,256]{2,1,0:T(8,128)(2,1)S(1)} %get-tuple-element.39), channel_id=1, source_target_pairs={{2,0},{3,1},{6,4},{7,5},{10,8},{11,9},{14,12},{15,13},{18,16},{19,... | collective-permute-start | bytes 1179656 | tf_op jit(solution)/shard_map/ppermute | solution.py:32
  32.3 22.0 %collective-permute-start.7 = (bf16[3,256,256]{2,1,0:T(8,128)(2,1)S(1)}, bf16[3,256,256]{2,1,0:T(8,128)(2,1)S(1)}, u32[]{:S(2)}, u32[]{:S(2)}) collective-permute-start(bf16[3,256,256]{2,1,0:T(8,128)(2,1)S(1)} %get-tuple-element.41), channel_id=1, source_target_pairs={{2,0},{3,1},{6,4},{7,5},{10,8},{11,9},{14,12},{15,13},{18,16},{19,... | collective-permute-start | bytes 1179656 | tf_op jit(solution)/shard_map/ppermute | solution.py:32
  37.7 24.2 %collective-permute-start.8 = (bf16[3,256,256]{2,1,0:T(8,128)(2,1)S(1)}, bf16[3,256,256]{2,1,0:T(8,128)(2,1)S(1)}, u32[]{:S(2)}, u32[]{:S(2)}) collective-permute-start(bf16[3,256,256]{2,1,0:T(8,128)(2,1)S(1)} %get-tuple-element.43), channel_id=1, source_target_pairs={{2,0},{3,1},{6,4},{7,5},{10,8},{11,9},{14,12},{15,13},{18,16},{19,... | collective-permute-start | bytes 1179656 | tf_op jit(solution)/shard_map/ppermute | solution.py:32
  39.0 29.1 %collective-permute-start.9 = (s16[784,256]{1,0:T(8,128)(2,1)S(1)}, s16[784,256]{1,0:T(8,128)(2,1)S(1)}, u32[]{:S(2)}, u32[]{:S(2)}) collective-permute-start(s16[784,256]{1,0:T(8,128)(2,1)S(1)} %get-tuple-element.46), channel_id=1, source_target_pairs={{0,8},{4,12},{8,0},{12,4},{1,9},{5,13},{9,1},{13,5},{2,10},{6,14},... | collective-permute-start | bytes 1204232 | tf_op jit(solution)/shard_map/ppermute | solution.py:37
  40.2 4.7 %copy-start.6 = (s32[5,12]{1,0:T(8,128)S(1)}, s32[5,12]{1,0:T(8,128)}, u32[]{:S(2)}) copy-start(s32[5,12]{1,0:T(8,128)} %lanes.1.refs_0_.refs_1_.table.refs_2_) | copy-start | bytes 724
  50.1 25.5 %collective-permute-start.10 = (s16[800,256]{1,0:T(8,128)(2,1)S(1)}, s16[800,256]{1,0:T(8,128)(2,1)S(1)}, u32[]{:S(2)}, u32[]{:S(2)}) collective-permute-start(s16[800,256]{1,0:T(8,128)(2,1)S(1)} %get-tuple-element.49), channel_id=1, source_target_pairs={{0,4},{4,8},{8,12},{12,0},{1,5},{5,9},{9,13},{13,1},{2,6},{6,10},{... | collective-permute-start | bytes 1228808 | tf_op jit(solution)/shard_map/ppermute | solution.py:37
  58.2 17.4 %collective-permute-start.11 = (s16[784,256]{1,0:T(8,128)(2,1)S(1)}, s16[784,256]{1,0:T(8,128)(2,1)S(1)}, u32[]{:S(2)}, u32[]{:S(2)}) collective-permute-start(s16[784,256]{1,0:T(8,128)(2,1)S(1)} %get-tuple-element.50), channel_id=1, source_target_pairs={{0,12},{4,0},{8,4},{12,8},{1,13},{5,1},{9,5},{13,9},{2,14},{6,2},{... | collective-permute-start | bytes 1204232 | tf_op jit(solution)/shard_map/ppermute | solution.py:37

commit v6 on v5

--- a/solution.py
+++ b/solution.py
@@ -478,9 +478,9 @@
         *tables,
         last=[below[1]],
     )
-    surfaces, before = settled("settle_visit", [visit_codes], guests)
-    before, _ = paired(1, before, before)
+    before, _ = paired(1, guests, guests)
     before, _ = paired(up_one, before, guests)
+    surfaces, before = settled("settle_visit", [visit_codes], before)
     before, _ = paired(0, before, before)
     early = [moving[d] for d in [0] + far]
     surfaces, before = settled("settle_early", early, before, surfaces)

time: 79.3 us -> 79.2 us (level)
    ppermute x3, waiting for transfers between devices: 7.11 us -> 3.11 us  [rotated(): lax.ppermute(value, axis, [(i, (i + steps) % count) for i in range(count)])]
    ppermute x9, waiting for transfers between devices: 7.42 us -> 10.7 us  [shifted(): return lax.ppermute(value, axis, pairs)]
  transfers between devices with their start and end apart: 12 -> 12, of which waited for: 6 -> 6; matrix products, arithmetic and copies ran while one was open for 0% -> 0% of each run, Pallas kernels for 33% -> 34%
where the time goes in v6:
time: 79.2 us; the launch traced here: 78.8 us
  Pallas kernels  32.6 us (41%)
  starting transfers between devices  30.6 us (39%)
  waiting for transfers between devices  13.9 us (18%)
  between operations  1.06 us (1%)
    pallas_call x8, Pallas kernels, call(): pl.pallas_call(kernel, out_shape=outs, in_specs=[VMEM if o.dtype in (own....  22.9 us
    ppermute x9, starting transfers between devices, shifted(): return lax.ppermute(value, axis, pairs)  21 us
    ppermute x9, waiting for transfers between devices, shifted(): return lax.ppermute(value, axis, pairs)  10.7 us
    ppermute x3, starting transfers between devices, rotated(): lax.ppermute(value, axis, [(i, (i + steps) % count) for i in range(count)])  9.51 us
    pallas_call x3, Pallas kernels, settled(): pl.pallas_call(kernel, out_shape=(surfaces_kind,) + ((peaks_kind,) if ext...  8.05 us
    ppermute x3, waiting for transfers between devices, rotated(): lax.ppermute(value, axis, [(i, (i + steps) % count) for i in range(count)])  3.11 us
    pallas_call x1, Pallas kernels, body(): pl.pallas_call(functools.partial(lanes_kernel, tiles, per), out_shape=SDS...  1.64 us
  transfers between devices with their start and end apart: 12, of which 6 were waited for; matrix products, arithmetic and copies ran while one was open for 0% of the time, Pallas kernels for 34%

profile of v6, /device:TPU:0, one launch (start us, length us, event | category | flops | bytes accessed | tf_op | source)
XLA Modules:
  0.0 78.8 jit_solution(18110684352081709222)
XLA Ops:
  0.6 1.6 %lanes.1.refs_0_.refs_1_.table.refs_2_ = s32[5,12]{1,0:T(8,128)} custom-call(s32[3,1,1,12]{3,2,1,0:T(1,128)} %pairs.1, s32[2,1,1,12]{3,2,1,0:T(1,128)} %plan.1), custom_call_target="tpu_custom_call" | custom-call | flops 4000000000 | bytes 1 | tf_op jit(solution)/shard_map/lanes/pallas_call | solution.py:375
  2.3 4.9 %collective-permute-start = (s32[5,12]{1,0:T(8,128)}, s32[5,12]{1,0:T(8,128)S(1)}, u32[]{:S(2)}, u32[]{:S(2)}) collective-permute-start(s32[5,12]{1,0:T(8,128)} %lanes.1.refs_0_.refs_1_.table.refs_2_), channel_id=1, source_target_pairs={{0,4},{4,8},{8,12},{1,5},{5,9},{9,13},{2,6},{6,10},{10,14},{3,7},{... | collective-permute-start | bytes 728 | tf_op jit(solution)/shard_map/ppermute | solution.py:32
  7.2 1.5 %collective-permute-done.refs_1_.refs_2_.table_above = s32[5,12]{1,0:T(8,128)S(1)} collective-permute-done((s32[5,12]{1,0:T(8,128)}, s32[5,12]{1,0:T(8,128)S(1)}, u32[]{:S(2)}, u32[]{:S(2)}) %collective-permute-start) | collective-permute-done | bytes 272 | tf_op jit(solution)/shard_map/ppermute | solution.py:32
  8.8 0.7 copy-done.5
  9.4 1.4 %gather_below.1 = (bf16[6,256,256]{2,1,0:T(8,128)(2,1)S(1)}, s32[5,12]{1,0:T(8,128)S(1)}) custom-call(s32[5,12]{1,0:T(8,128)S(1)} %copy-done.5, s32[5,12]{1,0:T(8,128)S(1)} %collective-permute-done.refs_1_.refs_2_.table_above, bf16[16,256,256]{2,1,0:T(8,128)(2,1)S(1)} %bitcast.3), custom_call_target="tpu_custom_call" | custom-call | flops 200000000 | bytes 1 | tf_op jit(solution)/shard_map/gather_below/pallas_call | solution.py:349
  10.8 1.3 %collective-permute-start.3 = (bf16[6,256,256]{2,1,0:T(8,128)(2,1)S(1)}, bf16[6,256,256]{2,1,0:T(8,128)(2,1)S(1)}, u32[]{:S(2)}, u32[]{:S(2)}) collective-permute-start(bf16[6,256,256]{2,1,0:T(8,128)(2,1)S(1)} %get-tuple-element.32), channel_id=1, source_target_pairs={{4,0},{8,4},{12,8},{5,1},{9,5},{13,9},{6,2},{10,6},{14,10},{7,3},{... | collective-permute-start | bytes 2359304 | tf_op jit(solution)/shard_map/ppermute | solution.py:32
  12.1 3.4 %collective-permute-start.1 = (s32[5,12]{1,0:T(8,128)S(1)}, s32[5,12]{1,0:T(8,128)S(1)}, u32[]{:S(2)}, u32[]{:S(2)}) collective-permute-start(s32[5,12]{1,0:T(8,128)S(1)} %get-tuple-element.28), channel_id=1, source_target_pairs={{0,2},{1,3},{4,6},{5,7},{8,10},{9,11},{12,14},{13,15},{16,18},{17,... | collective-permute-start | bytes 728 | tf_op jit(solution)/shard_map/ppermute | solution.py:32
  15.5 1.3 %collective-permute-done.1.refs_3_.refs_1_.refs_2_.other = s32[5,12]{1,0:T(8,128)S(1)} collective-permute-done((s32[5,12]{1,0:T(8,128)S(1)}, s32[5,12]{1,0:T(8,128)S(1)}, u32[]{:S(2)}, u32[]{:S(2)}) %collective-permute-start.1) | collective-permute-done | bytes 272 | tf_op jit(solution)/shard_map/ppermute | solution.py:32
  16.8 1.5 %gather_later.1 = (bf16[3,256,256]{2,1,0:T(8,128)(2,1)S(1)}, bf16[3,256,256]{2,1,0:T(8,128)(2,1)S(1)}, bf16[3,256,256]{2,1,0:T(8,128)(2,1)S(1)}, s32[5,12]{1,0:T(8,128)S(1)}) custom-call(s32[5,12]{1,0:T(8,128)S(1)} %copy-done.5, s32[5,12]{1,0:T(8,128)S(1)} %copy-done.5, s32[5,12]{1,0:T(8,128)S(1)} %collective-permute-done.refs_1_.refs_2_.table_above, ...), custom_call_target="tpu_custom_call" | custom-call | flops 200000000 | bytes 1 | tf_op jit(solution)/shard_map/gather_later/pallas_call | solution.py:349
  18.3 0.0 copy-start.2
  18.4 1.4 %collective-permute-start.2 = (bf16[3,256,256]{2,1,0:T(8,128)(2,1)S(1)}, bf16[3,256,256]{2,1,0:T(8,128)(2,1)S(1)}, u32[]{:S(2)}, u32[]{:S(2)}) collective-permute-start(bf16[3,256,256]{2,1,0:T(8,128)(2,1)S(1)} %get-tuple-element.30), channel_id=1, source_target_pairs={{2,0},{3,1},{6,4},{7,5},{10,8},{11,9},{14,12},{15,13},{18,16},{19,... | collective-permute-start | bytes 1179656 | tf_op jit(solution)/shard_map/ppermute | solution.py:32
  19.8 4.8 %collective-permute-start.4 = (bf16[3,256,256]{2,1,0:T(8,128)(2,1)S(1)}, bf16[3,256,256]{2,1,0:T(8,128)(2,1)S(1)}, u32[]{:S(2)}, u32[]{:S(2)}) collective-permute-start(bf16[3,256,256]{2,1,0:T(8,128)(2,1)S(1)} %get-tuple-element.34), channel_id=1, source_target_pairs={{0,4},{4,8},{8,12},{1,5},{5,9},{9,13},{2,6},{6,10},{10,14},{3,7},{... | collective-permute-start | bytes 1179656 | tf_op jit(solution)/shard_map/ppermute | solution.py:32
  24.7 1.3 %collective-permute-start.5 = (bf16[3,256,256]{2,1,0:T(8,128)(2,1)S(1)}, bf16[3,256,256]{2,1,0:T(8,128)(2,1)S(1)}, u32[]{:S(2)}, u32[]{:S(2)}) collective-permute-start(bf16[3,256,256]{2,1,0:T(8,128)(2,1)S(1)} %get-tuple-element.35), channel_id=1, source_target_pairs={{4,0},{8,4},{12,8},{5,1},{9,5},{13,9},{6,2},{10,6},{14,10},{7,3},{... | collective-permute-start | bytes 1179656 | tf_op jit(solution)/shard_map/ppermute | solution.py:32
  26.0 3.6 %collective-permute-done.2.refs_4_.later = bf16[3,256,256]{2,1,0:T(8,128)(2,1)S(1)} collective-permute-done((bf16[3,256,256]{2,1,0:T(8,128)(2,1)S(1)}, bf16[3,256,256]{2,1,0:T(8,128)(2,1)S(1)}, u32[]{:S(2)}, u32[]{:S(2)}) %collective-permute-start.2) | collective-permute-done | bytes 393248 | tf_op jit(solution)/shard_map/ppermute | solution.py:32
  29.6 1.4 %gather_next.1 = (bf16[3,256,256]{2,1,0:T(8,128)(2,1)S(1)}, bf16[3,256,256]{2,1,0:T(8,128)(2,1)S(1)}, s32[5,12]{1,0:T(8,128)S(1)}) custom-call(s32[5,12]{1,0:T(8,128)S(1)} %get-tuple-element.29.refs_0_, s32[5,12]{1,0:T(8,128)S(1)} %collective-permute-done.1.refs_3_.refs_1_.refs_2_.other, s32[5,12]{1,0:T(8,128)S(1)} %collective-permute-done.1.refs_3_.refs_1_.refs_2_.other, ...), custom_call_target="tpu_custom_call" | custom-call | flops 200000000 | bytes 1 | tf_op jit(solution)/shard_map/gather_next/pallas_call | solution.py:349
  31.0 1.3 %collective-permute-start.6 = (bf16[3,256,256]{2,1,0:T(8,128)(2,1)S(1)}, bf16[3,256,256]{2,1,0:T(8,128)(2,1)S(1)}, u32[]{:S(2)}, u32[]{:S(2)}) collective-permute-start(bf16[3,256,256]{2,1,0:T(8,128)(2,1)S(1)} %get-tuple-element.37), channel_id=1, source_target_pairs={{2,0},{3,1},{6,4},{7,5},{10,8},{11,9},{14,12},{15,13},{18,16},{19,... | collective-permute-start | bytes 1179656 | tf_op jit(solution)/shard_map/ppermute | solution.py:32
  32.3 1.3 %collective-permute-start.7 = (bf16[3,256,256]{2,1,0:T(8,128)(2,1)S(1)}, bf16[3,256,256]{2,1,0:T(8,128)(2,1)S(1)}, u32[]{:S(2)}, u32[]{:S(2)}) collective-permute-start(bf16[3,256,256]{2,1,0:T(8,128)(2,1)S(1)} %get-tuple-element.39), channel_id=1, source_target_pairs={{2,0},{3,1},{6,4},{7,5},{10,8},{11,9},{14,12},{15,13},{18,16},{19,... | collective-permute-start | bytes 1179656 | tf_op jit(solution)/shard_map/ppermute | solution.py:32
  33.6 4.1 %pairs_2.1 = (s16[784,256]{1,0:T(8,128)(2,1)S(1)}, f32[3]{0:T(128)S(1)}, bf16[3,256,256]{2,1,0:T(8,128)(2,1)S(1)}) custom-call(s32[5,12]{1,0:T(8,128)S(1)} %copy-done.5, s32[5,12]{1,0:T(8,128)S(1)} %get-tuple-element.31.before.guests, bf16[16,256,256]{2,1,0:T(8,128)(2,1)S(1)} %bitcast.6, s32[5,12]{1,0:T(8,128)S(1)} %get-tuple-element.31.before.guests, ...), custom_call_target="tpu_custom_call" | custom-call | flops 35000000512 | bytes 1 | tf_op jit(solution)/shard_map/pairs_2/pallas_call | solution.py:349
  37.8 1.3 %collective-permute-start.8 = (bf16[3,256,256]{2,1,0:T(8,128)(2,1)S(1)}, bf16[3,256,256]{2,1,0:T(8,128)(2,1)S(1)}, u32[]{:S(2)}, u32[]{:S(2)}) collective-permute-start(bf16[3,256,256]{2,1,0:T(8,128)(2,1)S(1)} %get-tuple-element.43), channel_id=1, source_target_pairs={{2,0},{3,1},{6,4},{7,5},{10,8},{11,9},{14,12},{15,13},{18,16},{19,... | collective-permute-start | bytes 1179656 | tf_op jit(solution)/shard_map/ppermute | solution.py:32
  39.1 3.8 %collective-permute-start.9 = (s16[784,256]{1,0:T(8,128)(2,1)S(1)}, s16[784,256]{1,0:T(8,128)(2,1)S(1)}, u32[]{:S(2)}, u32[]{:S(2)}) collective-permute-start(s16[784,256]{1,0:T(8,128)(2,1)S(1)} %get-tuple-element.46), channel_id=1, source_target_pairs={{0,8},{4,12},{8,0},{12,4},{1,9},{5,13},{9,1},{13,5},{2,10},{6,14},... | collective-permute-start | bytes 1204232 | tf_op jit(solution)/shard_map/ppermute | solution.py:37
  42.9 1.2 %visit.1 = (s16[784,256]{1,0:T(8,128)(2,1)S(1)}, f32[3]{0:T(128)S(1)}) custom-call(s32[5,12]{1,0:T(8,128)S(1)} %collective-permute-done.refs_1_.refs_2_.table_above, f32[3]{0:T(128)S(1)} %get-tuple-element.33.token.refs_5_, bf16[16,256,256]{2,1,0:T(8,128)(2,1)S(1)} %bitcast.7, bf16[3,256,256]{2,1,0:T(8,128)(2,1)S(1)} %collective-permute-done.4.up, ...), custom_call_target="tpu_custom_call" | custom-call | flops 200000000 | bytes 1 | tf_op jit(solution)/shard_map/visit/pallas_call | solution.py:349
  44.2 0.8 collective-permute-done.6.refs_2_
  44.9 3.9 %pairs_1.1 = (s16[800,256]{1,0:T(8,128)(2,1)S(1)}, f32[3]{0:T(128)S(1)}) custom-call(s32[5,12]{1,0:T(8,128)S(1)} %copy-done.6, f32[3]{0:T(128)S(1)} %get-tuple-element.36.before.refs_0_, bf16[16,256,256]{2,1,0:T(8,128)(2,1)S(1)} %bitcast.8, f32[3]{0:T(128)S(1)} %get-tuple-element.36.before.refs_0_, ...), custom_call_target="tpu_custom_call" | custom-call | flops 200000000 | bytes 1 | tf_op jit(solution)/shard_map/pairs_1/pallas_call | solution.py:349
  48.9 1.0 %collective-permute-start.10 = (s16[800,256]{1,0:T(8,128)(2,1)S(1)}, s16[800,256]{1,0:T(8,128)(2,1)S(1)}, u32[]{:S(2)}, u32[]{:S(2)}) collective-permute-start(s16[800,256]{1,0:T(8,128)(2,1)S(1)} %get-tuple-element.49), channel_id=1, source_target_pairs={{0,4},{4,8},{8,12},{12,0},{1,5},{5,9},{9,13},{13,1},{2,6},{6,10},{... | collective-permute-start | bytes 1228808 | tf_op jit(solution)/shard_map/ppermute | solution.py:37
  49.8 3.5 %collective-permute-done.7.refs_2_ = bf16[3,256,256]{2,1,0:T(8,128)(2,1)S(1)} collective-permute-done((bf16[3,256,256]{2,1,0:T(8,128)(2,1)S(1)}, bf16[3,256,256]{2,1,0:T(8,128)(2,1)S(1)}, u32[]{:S(2)}, u32[]{:S(2)}) %collective-permute-start.7) | collective-permute-done | bytes 393248 | tf_op jit(solution)/shard_map/ppermute | solution.py:32
  53.4 3.9 %pairs_3.1 = (s16[784,256]{1,0:T(8,128)(2,1)S(1)}, f32[3]{0:T(128)S(1)}) custom-call(s32[5,12]{1,0:T(8,128)S(1)} %copy-done.6, f32[3]{0:T(128)S(1)} %get-tuple-element.38.before.refs_4_, bf16[16,256,256]{2,1,0:T(8,128)(2,1)S(1)} %bitcast.9, f32[3]{0:T(128)S(1)} %get-tuple-element.36.before.refs_0_, ...), custom_call_target="tpu_custom_call" | custom-call | flops 200000000 | bytes 1 | tf_op jit(solution)/shard_map/pairs_3/pallas_call | solution.py:349
  57.3 4.7 %collective-permute-start.11 = (s16[784,256]{1,0:T(8,128)(2,1)S(1)}, s16[784,256]{1,0:T(8,128)(2,1)S(1)}, u32[]{:S(2)}, u32[]{:S(2)}) collective-permute-start(s16[784,256]{1,0:T(8,128)(2,1)S(1)} %get-tuple-element.50), channel_id=1, source_target_pairs={{0,12},{4,0},{8,4},{12,8},{1,13},{5,1},{9,5},{13,9},{2,14},{6,2},{... | collective-permute-start | bytes 1204232 | tf_op jit(solution)/shard_map/ppermute | solution.py:37
  62.0 2.5 %settle_visit.1 = (f32[6,256,256]{2,1,0:T(8,128)}, f32[1]{0:T(128)}) custom-call(f32[3]{0:T(128)S(1)} %get-tuple-element.40.before.refs_6_, s16[784,256]{1,0:T(8,128)(2,1)S(1)} %get-tuple-element.41.refs_0_), custom_call_target="tpu_custom_call" | custom-call | flops 200000000 | bytes 1 | tf_op jit(solution)/shard_map/settle_visit/pallas_call | solution.py:415
  64.5 5.4 %pairs_0.1 = (s16[784,256]{1,0:T(8,128)(2,1)S(1)}, f32[3]{0:T(128)S(1)}) custom-call(s32[5,12]{1,0:T(8,128)S(1)} %copy-done.6, f32[1]{0:T(128)} %get-tuple-element.42.before.refs_0_, bf16[16,256,256]{2,1,0:T(8,128)(2,1)S(1)} %bitcast.10, f32[1]{0:T(128)} %get-tuple-element.42.before.refs_0_, bf16[3,256,256]{2,1,0:T(8,128)(2,1)S(1)} %collective-permute-done.5._.refs_1_, ...), custom_call_target="tpu_custom_call" | custom-call | flops 200000000 | bytes 1 | tf_op jit(solution)/shard_map/pairs_0/pallas_call | solution.py:349
  69.9 2.5 %settle_early.1 = (f32[6,256,256]{2,1,0:T(8,128)}, f32[1]{0:T(128)}) custom-call(f32[3]{0:T(128)S(1)} %get-tuple-element.44.before.refs_3_, s16[784,256]{1,0:T(8,128)(2,1)S(1)} %get-tuple-element.45.refs_0_, s16[784,256]{1,0:T(8,128)(2,1)S(1)} %collective-permute-done.9.refs_1_, ...), custom_call_target="tpu_custom_call", output_to_operand_aliasing={{0}: (3, {})} | custom-call | flops 200000000 | bytes 1 | tf_op jit(solution)/shard_map/settle_early/pallas_call | solution.py:415
  72.4 3.1 %collective-permute-done.11.refs_1_ = s16[784,256]{1,0:T(8,128)(2,1)S(1)} collective-permute-done((s16[784,256]{1,0:T(8,128)(2,1)S(1)}, s16[784,256]{1,0:T(8,128)(2,1)S(1)}, u32[]{:S(2)}, u32[]{:S(2)}) %collective-permute-start.11) | collective-permute-done | bytes 401440 | tf_op jit(solution)/shard_map/ppermute | solution.py:37
  75.6 3.0 %settle_last.1 = (f32[6,256,256]{2,1,0:T(8,128)}, f32[12]{0:T(128)}, f32[1]{0:T(128)}) custom-call(f32[1]{0:T(128)} %get-tuple-element.48.before, s16[800,256]{1,0:T(8,128)(2,1)S(1)} %collective-permute-done.10.refs_0_, s16[784,256]{1,0:T(8,128)(2,1)S(1)} %collective-permute-done.11.refs_1_, s32[5,12]{1,0:T(8,128)S(1)} %copy-done.6, ...), custom_call_target="tpu_custom_call", output_to_operand_aliasing={{0}: (8, {})} | custom-call | flops 200000000 | bytes 1 | tf_op jit(solution)/shard_map/settle_last/pallas_call | solution.py:415
  (18 shorter events, 0.0 us)
Async XLA Ops:
  0.6 8.1 %copy-start = (bf16[1,1,16,256,256]{4,3,2,1,0:T(8,128)(2,1)S(1)}, bf16[1,1,16,256,256]{4,3,2,1,0:T(8,128)(2,1)}, u32[]{:S(2)}) copy-start(bf16[1,1,16,256,256]{4,3,2,1,0:T(8,128)(2,1)} %param.7) | copy-start | bytes 6291460
  2.3 6.5 %collective-permute-start = (s32[5,12]{1,0:T(8,128)}, s32[5,12]{1,0:T(8,128)S(1)}, u32[]{:S(2)}, u32[]{:S(2)}) collective-permute-start(s32[5,12]{1,0:T(8,128)} %lanes.1.refs_0_.refs_1_.table.refs_2_), channel_id=1, source_target_pairs={{0,4},{4,8},{8,12},{1,5},{5,9},{9,13},{2,6},{6,10},{10,14},{3,7},{... | collective-permute-start | bytes 728 | tf_op jit(solution)/shard_map/ppermute | solution.py:32
  8.8 0.7 copy-start.5
  10.8 22.8 %collective-permute-start.3 = (bf16[6,256,256]{2,1,0:T(8,128)(2,1)S(1)}, bf16[6,256,256]{2,1,0:T(8,128)(2,1)S(1)}, u32[]{:S(2)}, u32[]{:S(2)}) collective-permute-start(bf16[6,256,256]{2,1,0:T(8,128)(2,1)S(1)} %get-tuple-element.32), channel_id=1, source_target_pairs={{4,0},{8,4},{12,8},{5,1},{9,5},{13,9},{6,2},{10,6},{14,10},{7,3},{... | collective-permute-start | bytes 2359304 | tf_op jit(solution)/shard_map/ppermute | solution.py:32
  12.1 4.7 %collective-permute-start.1 = (s32[5,12]{1,0:T(8,128)S(1)}, s32[5,12]{1,0:T(8,128)S(1)}, u32[]{:S(2)}, u32[]{:S(2)}) collective-permute-start(s32[5,12]{1,0:T(8,128)S(1)} %get-tuple-element.28), channel_id=1, source_target_pairs={{0,2},{1,3},{4,6},{5,7},{8,10},{9,11},{12,14},{13,15},{16,18},{17,... | collective-permute-start | bytes 728 | tf_op jit(solution)/shard_map/ppermute | solution.py:32
  18.3 15.3 %copy-start.1 = (bf16[256,256]{1,0:T(8,128)(2,1)S(1)}, bf16[256,256]{1,0:T(8,128)(2,1)}, u32[]{:S(2)}) copy-start(bf16[256,256]{1,0:T(8,128)(2,1)} %constant.11.clone.sl.refs_6_) | copy-start | bytes 393220
  18.3 15.3 %copy-start.2 = (bf16[256,256]{1,0:T(8,128)(2,1)S(1)}, bf16[256,256]{1,0:T(8,128)(2,1)}, u32[]{:S(2)}) copy-start(bf16[256,256]{1,0:T(8,128)(2,1)} %constant.10.clone.sh.refs_5_) | copy-start | bytes 393220
  18.4 15.3 %copy-start.3 = (bf16[256,256]{1,0:T(8,128)(2,1)S(1)}, bf16[256,256]{1,0:T(8,128)(2,1)}, u32[]{:S(2)}) copy-start(bf16[256,256]{1,0:T(8,128)(2,1)} %constant.9.clone.tl.refs_4_) | copy-start | bytes 393220
  18.4 15.3 %copy-start.4 = (bf16[256,256]{1,0:T(8,128)(2,1)S(1)}, bf16[256,256]{1,0:T(8,128)(2,1)}, u32[]{:S(2)}) copy-start(bf16[256,256]{1,0:T(8,128)(2,1)} %constant.8.clone.th.refs_3_) | copy-start | bytes 393220
  18.4 11.2 %collective-permute-start.2 = (bf16[3,256,256]{2,1,0:T(8,128)(2,1)S(1)}, bf16[3,256,256]{2,1,0:T(8,128)(2,1)S(1)}, u32[]{:S(2)}, u32[]{:S(2)}) collective-permute-start(bf16[3,256,256]{2,1,0:T(8,128)(2,1)S(1)} %get-tuple-element.30), channel_id=1, source_target_pairs={{2,0},{3,1},{6,4},{7,5},{10,8},{11,9},{14,12},{15,13},{18,16},{19,... | collective-permute-start | bytes 1179656 | tf_op jit(solution)/shard_map/ppermute | solution.py:32
  19.8 19.3 %collective-permute-start.4 = (bf16[3,256,256]{2,1,0:T(8,128)(2,1)S(1)}, bf16[3,256,256]{2,1,0:T(8,128)(2,1)S(1)}, u32[]{:S(2)}, u32[]{:S(2)}) collective-permute-start(bf16[3,256,256]{2,1,0:T(8,128)(2,1)S(1)} %get-tuple-element.34), channel_id=1, source_target_pairs={{0,4},{4,8},{8,12},{1,5},{5,9},{9,13},{2,6},{6,10},{10,14},{3,7},{... | collective-permute-start | bytes 1179656 | tf_op jit(solution)/shard_map/ppermute | solution.py:32
  24.7 18.3 %collective-permute-start.5 = (bf16[3,256,256]{2,1,0:T(8,128)(2,1)S(1)}, bf16[3,256,256]{2,1,0:T(8,128)(2,1)S(1)}, u32[]{:S(2)}, u32[]{:S(2)}) collective-permute-start(bf16[3,256,256]{2,1,0:T(8,128)(2,1)S(1)} %get-tuple-element.35), channel_id=1, source_target_pairs={{4,0},{8,4},{12,8},{5,1},{9,5},{13,9},{6,2},{10,6},{14,10},{7,3},{... | collective-permute-start | bytes 1179656 | tf_op jit(solution)/shard_map/ppermute | solution.py:32
  31.0 13.9 %collective-permute-start.6 = (bf16[3,256,256]{2,1,0:T(8,128)(2,1)S(1)}, bf16[3,256,256]{2,1,0:T(8,128)(2,1)S(1)}, u32[]{:S(2)}, u32[]{:S(2)}) collective-permute-start(bf16[3,256,256]{2,1,0:T(8,128)(2,1)S(1)} %get-tuple-element.37), channel_id=1, source_target_pairs={{2,0},{3,1},{6,4},{7,5},{10,8},{11,9},{14,12},{15,13},{18,16},{19,... | collective-permute-start | bytes 1179656 | tf_op jit(solution)/shard_map/ppermute | solution.py:32
  32.3 21.1 %collective-permute-start.7 = (bf16[3,256,256]{2,1,0:T(8,128)(2,1)S(1)}, bf16[3,256,256]{2,1,0:T(8,128)(2,1)S(1)}, u32[]{:S(2)}, u32[]{:S(2)}) collective-permute-start(bf16[3,256,256]{2,1,0:T(8,128)(2,1)S(1)} %get-tuple-element.39), channel_id=1, source_target_pairs={{2,0},{3,1},{6,4},{7,5},{10,8},{11,9},{14,12},{15,13},{18,16},{19,... | collective-permute-start | bytes 1179656 | tf_op jit(solution)/shard_map/ppermute | solution.py:32
  37.8 26.7 %collective-permute-start.8 = (bf16[3,256,256]{2,1,0:T(8,128)(2,1)S(1)}, bf16[3,256,256]{2,1,0:T(8,128)(2,1)S(1)}, u32[]{:S(2)}, u32[]{:S(2)}) collective-permute-start(bf16[3,256,256]{2,1,0:T(8,128)(2,1)S(1)} %get-tuple-element.43), channel_id=1, source_target_pairs={{2,0},{3,1},{6,4},{7,5},{10,8},{11,9},{14,12},{15,13},{18,16},{19,... | collective-permute-start | bytes 1179656 | tf_op jit(solution)/shard_map/ppermute | solution.py:32
  39.1 30.8 %collective-permute-start.9 = (s16[784,256]{1,0:T(8,128)(2,1)S(1)}, s16[784,256]{1,0:T(8,128)(2,1)S(1)}, u32[]{:S(2)}, u32[]{:S(2)}) collective-permute-start(s16[784,256]{1,0:T(8,128)(2,1)S(1)} %get-tuple-element.46), channel_id=1, source_target_pairs={{0,8},{4,12},{8,0},{12,4},{1,9},{5,13},{9,1},{13,5},{2,10},{6,14},... | collective-permute-start | bytes 1204232 | tf_op jit(solution)/shard_map/ppermute | solution.py:37
  42.9 2.0 %copy-start.6 = (s32[5,12]{1,0:T(8,128)S(1)}, s32[5,12]{1,0:T(8,128)}, u32[]{:S(2)}) copy-start(s32[5,12]{1,0:T(8,128)} %lanes.1.refs_0_.refs_1_.table.refs_2_) | copy-start | bytes 724
  48.9 26.7 %collective-permute-start.10 = (s16[800,256]{1,0:T(8,128)(2,1)S(1)}, s16[800,256]{1,0:T(8,128)(2,1)S(1)}, u32[]{:S(2)}, u32[]{:S(2)}) collective-permute-start(s16[800,256]{1,0:T(8,128)(2,1)S(1)} %get-tuple-element.49), channel_id=1, source_target_pairs={{0,4},{4,8},{8,12},{12,0},{1,5},{5,9},{9,13},{13,1},{2,6},{6,10},{... | collective-permute-start | bytes 1228808 | tf_op jit(solution)/shard_map/ppermute | solution.py:37
  57.3 18.2 %collective-permute-start.11 = (s16[784,256]{1,0:T(8,128)(2,1)S(1)}, s16[784,256]{1,0:T(8,128)(2,1)S(1)}, u32[]{:S(2)}, u32[]{:S(2)}) collective-permute-start(s16[784,256]{1,0:T(8,128)(2,1)S(1)} %get-tuple-element.50), channel_id=1, source_target_pairs={{0,12},{4,0},{8,4},{12,8},{1,13},{5,1},{9,5},{13,9},{2,14},{6,2},{... | collective-permute-start | bytes 1204232 | tf_op jit(solution)/shard_map/ppermute | solution.py:37
